TPU v7x, 256 devices: a whole 4x4x8 slice. The times are simulated.
256 devices in a mesh: rcv: 16 (over z_hi, y, core), shot: 16 (over z_lo, x).
Axes of the slice: x: 4, y: 4, z: 8 (z_hi: 2, z_lo: 4; z = z_hi * 4 + z_lo), core: 2. Of those that a mesh axis runs over, the one named last changes fastest.
Arguments:
- wavefield: bfloat16 [2, 2, 8192, 4096], P(None, None, 'shot', 'rcv'), may hold values from -6 to 6
Outputs:
- psf: float32 [2, 2, 4096, 4096], P(None, None, 'rcv', 'shot')
All inputs are finite; a program needn't handle non-finite values.
Results may differ from a plain program's by a relative error of at most 0.0003.
Values may be sent and summed in bfloat16 or wider, within the bound.
No kernel may reach another device: no remote copies, remote signals or barrier semaphores. Data moves between devices by JAX's collectives and lax.ppermute only.
A program may use at most 192 MiB of HBM per device.

v0:
```python
import jax
import jax.numpy as jnp
from jax import lax
from jax.sharding import PartitionSpec as P


def hermitian_product(left, right):
    left_re = left[:, 0]
    left_im = left[:, 1]
    right_re = right[:, 0]
    right_im = right[:, 1]
    real_part = jnp.einsum("fsm,fsn->fmn", left_re, right_re, preferred_element_type=jnp.float32)
    real_part = real_part + jnp.einsum(
        "fsm,fsn->fmn", left_im, right_im, preferred_element_type=jnp.float32
    )
    imag_part = jnp.einsum("fsm,fsn->fmn", left_re, right_im, preferred_element_type=jnp.float32)
    imag_part = imag_part - jnp.einsum(
        "fsm,fsn->fmn", left_im, right_re, preferred_element_type=jnp.float32
    )
    return jnp.stack([real_part, imag_part], axis=1)


def body(wavefield):
    total_shots = wavefield.shape[2] * lax.axis_size("shot")
    scale = 1.0 / jnp.sqrt(jnp.float32(total_shots))
    partial_gram = hermitian_product(
        wavefield, lax.all_gather(wavefield, "rcv", axis=3, tiled=True)
    )
    summed = lax.psum_scatter(partial_gram, "shot", scatter_dimension=3, tiled=True)
    return summed * scale


def solution(mesh):
    return jax.shard_map(
        body,
        mesh=mesh,
        in_specs=(P(None, None, "shot", "rcv"),),
        out_specs=P(None, None, "rcv", "shot"),
        check_vma=False,
    )
```

profile of v0, /device:TPU:16, one launch (start us, length us, event | category | flops | bytes accessed | tf_op | source)
XLA Modules:
  0.0 437.1 jit_solution(8958376037879085605)
XLA Ops:
  6.5 0.0 all-gather.2.cloned.1.call-start
  6.5 2.3 copy.3
  8.8 0.0 copy-start.1
  8.8 0.0 all-gather.2.cloned.1.call-update
  8.8 0.0 reduce-scatter.2.cloned.1.call-start
  8.9 187.2 %all-gather.2.cloned.1.call-done = bf16[2,2,512,4096]{3,2,0,1:T(8,128)(2,1)} async-done(((bf16[2,2,512,256]{3,2,0,1:T(8,128)(2,1)}), bf16[2,2,512,4096]{3,2,0,1:T(8,128)(2,1)}) %all-gather.2.cloned.1.call-update) | async-done | bytes 16777232 | tf_op jit(solution)/shard_map/all_gather | solution.py:27
  196.0 0.0 copy-start
  196.0 10.3 %fusion = f32[2,256,4096]{2,1,0:T(8,128)} fusion(bf16[2,2,512,4096]{3,2,0,1:T(8,128)(2,1)} %all-gather.2.cloned.1.call-done, bf16[2,2,512,256]{3,2,1,0:T(8,128)(2,1)} %param.1), kind=kOutput, calls=%fused_computation.5 | convolution fusion | flops 2147483648 | bytes 17301504 | tf_op jit(solution)/shard_map/fsm,fsn->fmn/dot_general | solution.py:17
  206.4 0.0 copy-done.1
  206.4 1.0 copy-done
  207.4 5.8 %fusion.1 = f32[2,256,4096]{2,1,0:T(8,128)} fusion(bf16[2,2,512,4096]{3,2,0,1:T(8,128)(2,1)S(1)} %copy-done, bf16[2,2,512,256]{3,2,1,0:T(8,128)(2,1)S(1)} %copy-done.1), kind=kOutput, calls=%fused_computation.6 | convolution fusion | flops 2147483648 | bytes 17301504 | tf_op jit(solution)/shard_map/fsm,fsn->fmn/dot_general | solution.py:12
  213.2 9.4 %subtract_bitcast_fusion = f32[2,1,256,4096]{3,2,0,1:T(8,128)} fusion(f32[2,256,4096]{2,1,0:T(8,128)} %fusion, bf16[2,2,512,4096]{3,2,0,1:T(8,128)(2,1)S(1)} %copy-done, bf16[2,2,512,256]{3,2,1,0:T(8,128)(2,1)S(1)} %copy-done.1), kind=kOutput, calls=%fused_computation.3 | convolution fusion | flops 2149580800 | bytes 25690112 | tf_op jit(solution)/shard_map/fsm,fsn->fmn/dot_general | solution.py:16
  222.5 9.4 %add_bitcast_fusion = f32[2,1,256,4096]{3,2,0,1:T(8,128)} fusion(f32[2,256,4096]{2,1,0:T(8,128)} %fusion.1, bf16[2,2,512,4096]{3,2,0,1:T(8,128)(2,1)S(1)} %copy-done, bf16[2,2,512,256]{3,2,1,0:T(8,128)(2,1)S(1)} %copy-done.1), kind=kOutput, calls=%fused_computation.4 | convolution fusion | flops 2149580800 | bytes 25690112 | tf_op jit(solution)/shard_map/fsm,fsn->fmn/dot_general | solution.py:13
  231.9 11.6 %pad_maximum_fusion = f32[2,2,256,4096]{3,2,0,1:T(8,128)} fusion(f32[2,1,256,4096]{3,2,0,1:T(8,128)} %subtract_bitcast_fusion, f32[2,1,256,4096]{3,2,0,1:T(8,128)} %add_bitcast_fusion), kind=kLoop, calls=%fused_computation | loop fusion | flops 4194304 | bytes 33554432 | tf_op jit(solution)/shard_map/stack | solution.py:20
  243.5 0.0 reduce-scatter.2.cloned.1.call-update
  243.5 184.3 %reduce-scatter.2.cloned.1.call-done = f32[2,2,256,256]{3,2,0,1:T(8,128)} async-done(((f32[2,2,256,4096]{3,2,0,1:T(8,128)}), f32[2,2,256,256]{3,2,0,1:T(8,128)}) %reduce-scatter.2.cloned.1.call-update) | async-done | bytes 1048592 | tf_op jit(solution)/shard_map/reduce_scatter | solution.py:29
  427.9 1.3 broadcast_multiply_fusion
  429.2 1.0 copy.5
Async XLA Ops:
  6.5 189.5 %all-gather.2.cloned.1.call-start = ((), (), s32[]{:S(2)}) async-start(), calls=%async_computation.1 | async-start | bytes 17825792 | tf_op jit(solution)/shard_map/all_gather | solution.py:27
  8.8 197.6 %copy-start.1 = (bf16[2,2,512,256]{3,2,1,0:T(8,128)(2,1)S(1)}, bf16[2,2,512,256]{3,2,1,0:T(8,128)(2,1)}, u32[]{:S(2)}) copy-start(bf16[2,2,512,256]{3,2,1,0:T(8,128)(2,1)} %param.1) | copy-start | bytes 3145732
  8.8 419.0 %reduce-scatter.2.cloned.1.call-start = ((), (), s32[]{:S(2)}) async-start(), calls=%async_computation.2 | async-start | bytes 17825792 | tf_op jit(solution)/shard_map/reduce_scatter | solution.py:29
  196.0 11.3 %copy-start = (bf16[2,2,512,4096]{3,2,0,1:T(8,128)(2,1)S(1)}, bf16[2,2,512,4096]{3,2,0,1:T(8,128)(2,1)}, u32[]{:S(2)}) copy-start(bf16[2,2,512,4096]{3,2,0,1:T(8,128)(2,1)} %all-gather.2.cloned.1.call-done) | copy-start | bytes 50331652
Sparse Core Ops, SparseCore 0:
  9.9 186.0 all-gather.1
  243.6 184.1 reduce-scatter.1
where the time goes:
time: 438 us; the launch traced here: 437 us
  waiting for transfers between devices  372 us (85%)
  matrix products  34.9 us (8%)
  between operations  13.4 us (3%)
  other arithmetic  12.9 us (3%)
    all_gather x1, waiting for transfers between devices, body(): lax.all_gather(wavefield, 'rcv', axis=3, tiled=True)  187 us
    reduce_scatter x1, waiting for transfers between devices, body(): lax.psum_scatter(partial_gram, 'shot', scatter_dimension=3, tiled=True)  184 us
    another operation x1, other arithmetic, hermitian_product(): return jnp.stack([real_part, imag_part], axis=1)  11.6 us
    dot_general x1, matrix products, hermitian_product(): jnp.einsum('fsm,fsn->fmn', left_im, right_re, preferred_element_type=jnp....  10.3 us
    dot_general x1, matrix products, hermitian_product(): jnp.einsum('fsm,fsn->fmn', left_re, right_im, preferred_element_type=jnp....  9.39 us
    dot_general x1, matrix products, hermitian_product(): jnp.einsum('fsm,fsn->fmn', left_im, right_im, preferred_element_type=jnp....  9.36 us
  transfers between devices with their start and end apart: 2, of which 2 were waited for; matrix products, arithmetic and copies ran while one was open for 0% of the time, Pallas kernels for 0%

commit v1 on v0

v1 whole, which is shorter than its diff:
```python
import itertools

import jax
import jax.numpy as jnp
import numpy as np
from jax import lax
from jax.sharding import Mesh
from jax.sharding import PartitionSpec as P

AXES = ("zh", "y", "core", "zl", "x")
SIZES = (2, 4, 2, 4, 4)
BLOCKS = 4


def rcv_of(zh, y, core):
    return (zh * 4 + y) * 2 + core


def device_of(row, col):
    return row * 16 + col


def z_of(row, col):
    return (row // 8) * 4 + col // 4


def held_pair(f, y, core, x, block):
    e_col, core_col = x // 2, x % 2
    if block < 2:
        e_row, dy = block, 1
    elif block == 2:
        e_row, dy = (e_col if y < 2 else 1 - e_col), 2
    else:
        if core_col == core:
            return None
        e_row, dy = (e_col if core == 0 else 1 - e_col), 0
    return rcv_of(f ^ e_row, y, core), rcv_of(f ^ e_col, (y + dy) % 4, core_col)


def deliveries(f, y, core, x, block):
    pair = held_pair(f, y, core, x, block)
    if pair is not None:
        row, col = pair
        plain, flipped = device_of(row, col), device_of(col, row)
        first, second = (plain, flipped) if f == 0 else (flipped, plain)
        return [(0, first), (1, first), (2, second), (3, second)]
    e_col = x // 2
    r0, r1 = rcv_of(0, y, core), rcv_of(1, y, core)
    own = rcv_of(f ^ e_col, y, core)
    d01, d10 = device_of(r0, r1), device_of(r1, r0)
    diag = device_of(own, own)
    if f == 0:
        return [(0, diag), (1, d01 if e_col == 0 else d10), (2, d10 if e_col == 0 else d01)]
    return [(1, diag), (0, d01 if e_col == 0 else d10), (3, d10 if e_col == 0 else d01)]


def ring_distance(a, b):
    d = (a - b) % 8
    return min(d, 8 - d)


def tables():
    slot_block = np.zeros((2, 4, 2, 4, 4), np.int32)
    perms = [[], [], [], []]
    for f, y, core, x in itertools.product(range(2), range(4), range(2), range(4)):
        costs = np.zeros((4, 4))
        for block in range(BLOCKS):
            for _, target in deliveries(f, y, core, x, block):
                z = z_of(target // 16, target % 16)
                for zl in range(4):
                    costs[zl, block] += ring_distance(4 * f + zl, z)
        best = min(itertools.permutations(range(4)), key=lambda p: sum(costs[zl, p[zl]] ** 2 for zl in range(4)))
        slot_block[f, y, core, x] = best
        for zl in range(4):
            source = device_of(rcv_of(f, y, core), zl * 4 + x)
            for slot, target in deliveries(f, y, core, x, best[zl]):
                perms[slot].append((source, target))
    for perm in perms:
        assert len({s for s, _ in perm}) == len(perm) == len({t for _, t in perm})
    case = np.zeros((16, 16), np.int32)
    for f, y, core, x, block in itertools.product(range(2), range(4), range(2), range(4), range(BLOCKS)):
        pair = held_pair(f, y, core, x, block)
        if pair is not None and f == 0:
            case[pair] = 1
    for y, core in itertools.product(range(4), range(2)):
        r0, r1 = rcv_of(0, y, core), rcv_of(1, y, core)
        case[r0, r0] = case[r1, r1] = 2
        case[r0, r1], case[r1, r0] = 3, 4
    return slot_block, perms, case


def ring(n, step):
    return [(i, (i + step) % n) for i in range(n)]


def gather_x(block):
    half = block.shape[1] // 2
    above = lax.ppermute(block, "x", ring(4, -1))
    below = lax.ppermute(block, "x", ring(4, 1))
    far_a = lax.ppermute(above[:, :half], "x", ring(4, -1))
    far_b = lax.ppermute(below[:, half:], "x", ring(4, 1))
    return jnp.concatenate([block, above, below, far_a, far_b], axis=1)


def from_core(mine, core_perm):
    return lax.ppermute(mine, ("core", "x"), core_perm)


def both_products(rows, cols):
    real = jnp.einsum("psm,psn->mn", rows, cols, preferred_element_type=jnp.float32)
    turned = jnp.stack([cols[1], -cols[0]])
    imag = jnp.einsum("psm,psn->mn", rows, turned, preferred_element_type=jnp.float32)
    return real, imag


def body(wavefield):
    slot_block, perms, case_of = tables()
    f, y, core, zl, x = (lax.axis_index(name) for name in AXES)
    n = wavefield.shape[3]
    shots = wavefield.shape[2] * 16
    scale = 1.0 / jnp.sqrt(jnp.float32(shots))

    own = lax.dynamic_index_in_dim(wavefield, f, 0, keepdims=False)
    other = lax.dynamic_index_in_dim(wavefield, 1 - f, 0, keepdims=False)
    other = lax.ppermute(other, "zh", ring(2, 1))
    block0, block1 = gather_x(own), gather_x(other)

    e_col, core_col = x // 2, x % 2
    mine = jnp.where(e_col == 0, block0, block1)
    one_way = [(a * 4 + b, (1 - a) * 4 + b) for a in range(2) for b in range(4) if b % 2 == a]
    cols0 = jnp.where(core_col == core, mine, from_core(mine, one_way))
    part = lax.dynamic_index_in_dim(cols0, core, 0, keepdims=False)
    swap = ring(2, 1)

    def from_y(step):
        near = lax.ppermute(part, "y", ring(4, -step))
        far = lax.ppermute(near, "core", swap)
        return jnp.where(core == 0, jnp.stack([near, far]), jnp.stack([far, near]))

    cols1, cols2 = from_y(1), from_y(2)

    rows = jnp.concatenate([block0, block1], axis=2)
    real1, imag1 = both_products(rows, cols1)
    e_row2 = jnp.where(y < 2, e_col, 1 - e_col)
    real2, imag2 = both_products(jnp.where(e_row2 == 0, block0, block1), cols2)
    real0, imag0 = both_products(rows, cols0)

    def rows_of(a, e):
        return lax.dynamic_slice_in_dim(a, e * n, n, 0)

    same = core_col == core
    e_row0 = jnp.where(same, 1 - e_col, jnp.where(core == 0, e_col, 1 - e_col))
    upper = lax.broadcasted_iota(jnp.int32, (n, n), 0) <= lax.broadcasted_iota(jnp.int32, (n, n), 1)
    packed = jnp.where(upper, rows_of(real0, e_col), rows_of(imag0, e_col))
    off_real, off_imag = rows_of(real0, e_row0), rows_of(imag0, e_row0)
    first0 = jnp.where(same, packed, off_real)
    second0 = jnp.where(same & (e_col == 0), off_real, off_imag)
    blocks = jnp.stack(
        [
            jnp.stack([real1[:n], imag1[:n]]),
            jnp.stack([real1[n:], imag1[n:]]),
            jnp.stack([real2, imag2]),
            jnp.stack([first0, second0]),
        ]
    )

    order = jnp.asarray(slot_block)[f, y, core, x]

    def partial_of(slot):
        return lax.dynamic_index_in_dim(blocks, order[jnp.clip(slot, 0, 3)], 0, keepdims=False)

    up = down = None
    for step in (1, 2, 3):
        send_up, send_down = partial_of(zl + 4 - step), partial_of(zl - 4 + step)
        if up is not None:
            send_up, send_down = send_up + up, send_down + down
        up = lax.ppermute(send_up, "zl", [(i, i + 1) for i in range(step)])
        down = lax.ppermute(send_down, "zl", [(3 - i, 2 - i) for i in range(step)])
    held = (partial_of(zl) + up + down) * scale

    plain_a, plain_b = held[0], held[1]
    turned_a, turned_b = held[0].T, -held[1].T
    special = same & (order[zl] == 3)
    other_turned = jnp.where(e_col == 0, held[1].T, turned_b)
    is0 = f == 0
    send = [
        jnp.where(is0, plain_a, jnp.where(special, plain_b, turned_a)),
        jnp.where(is0, jnp.where(special, other_turned, plain_b), jnp.where(special, plain_a, turned_b)),
        jnp.where(is0, jnp.where(special, plain_b, turned_a), plain_a),
        jnp.where(is0, turned_b, jnp.where(special, other_turned, plain_b)),
    ]
    got = [lax.ppermute(s, AXES, perm) for s, perm in zip(send, perms)]

    case = jnp.asarray(case_of)[rcv_of(f, y, core), zl * 4 + x]

    def unpack(packed):
        strict = lax.broadcasted_iota(jnp.int32, (n, n), 0) < lax.broadcasted_iota(jnp.int32, (n, n), 1)
        top, low = jnp.where(upper, packed, 0.0), jnp.where(upper, 0.0, packed)
        return top + jnp.where(strict, packed, 0.0).T, low - low.T

    real_d0, imag_d0 = unpack(got[0])
    real_d1, imag_d1 = unpack(got[1])

    def pick(plain, flipped, diag, d01, d10):
        return jnp.where(
            case == 0, flipped, jnp.where(case == 1, plain, jnp.where(case == 2, diag, jnp.where(case == 3, d01, d10)))
        )

    a1, b1, a2, b2 = got
    return jnp.stack(
        [
            jnp.stack([pick(a1, a2, real_d0, b1, a2), pick(b1, b2, imag_d0, a2, b1)]),
            jnp.stack([pick(a2, a1, real_d1, a1, b2), pick(b2, b1, imag_d1, b2, a1)]),
        ]
    )


def solution(mesh):
    fine = Mesh(mesh.devices.reshape(SIZES), AXES)
    return jax.shard_map(
        body,
        mesh=fine,
        in_specs=(P(None, None, ("zl", "x"), ("zh", "y", "core")),),
        out_specs=P(None, None, ("zh", "y", "core"), ("zl", "x")),
        check_vma=False,
    )
```

time: 438 us -> 268 us (0.61)
  the two profiles are of different devices: /device:TPU:16 before, /device:TPU:34 now
where the time goes in v1:
time: 268 us; the launch traced here: 267 us
  waiting for transfers between devices  161 us (60%)
  starting transfers between devices  50.1 us (19%)
  between operations  16.5 us (6%)
  local copies, waits for them, and re-layouts  14.6 us (5%)
  other arithmetic  14.6 us (5%)
  matrix products  9.49 us (4%)
    ppermute x4, waiting for transfers between devices, body(): got = [lax.ppermute(s, AXES, perm) for s, perm in zip(send, perms)]  41.3 us
    ppermute x2, waiting for transfers between devices, from_y(): near = lax.ppermute(part, 'y', ring(4, -step))  39.9 us
    ppermute x1, waiting for transfers between devices, body(): other = lax.ppermute(other, 'zh', ring(2, 1))  21.1 us
    ppermute x3, waiting for transfers between devices, body(): up = lax.ppermute(send_up, 'zl', [(i, i + 1) for i in range(step)])  20.3 us
    ppermute x4, starting transfers between devices, body(): got = [lax.ppermute(s, AXES, perm) for s, perm in zip(send, perms)]  18.3 us
    ppermute x3, waiting for transfers between devices, body(): down = lax.ppermute(send_down, 'zl', [(3 - i, 2 - i) for i in range(step)])  15.2 us
    ppermute x2, waiting for transfers between devices, gather_x(): far_a = lax.ppermute(above[:, :half], 'x', ring(4, -1))  10.5 us
    ppermute x3, starting transfers between devices, body(): up = lax.ppermute(send_up, 'zl', [(i, i + 1) for i in range(step)])  7.75 us
  transfers between devices with their start and end apart: 24, of which 13 were waited for; matrix products, arithmetic and copies ran while one was open for 6% of the time, Pallas kernels for 0%

profile of v1, /device:TPU:34, one launch (start us, length us, event | category | flops | bytes accessed | tf_op | source)
XLA Modules:
  0.0 266.8 jit_solution(15491783715290603136)
XLA Ops:
  1.5 6.4 %collective-permute-start.4 = (bf16[2,512,256]{1,2,0:T(8,128)(2,1)S(1)}, bf16[2,512,256]{1,2,0:T(8,128)(2,1)}, u32[]{:S(2)}, u32[]{:S(2)}) collective-permute-start(bf16[2,512,256]{1,2,0:T(8,128)(2,1)S(1)} %bitcast.157), channel_id=1, source_target_pairs={{0,128},{128,0},{1,129},{129,1},{2,130},{130,2},{3,131},{131,3},{4... | collective-permute-start | bytes 1572872 | tf_op jit(solution)/shard_map/ppermute | solution.py:125
  8.7 1.5 collective-permute-start.1
  10.2 21.1 %collective-permute-done.4 = bf16[2,512,256]{1,2,0:T(8,128)(2,1)} collective-permute-done((bf16[2,512,256]{1,2,0:T(8,128)(2,1)S(1)}, bf16[2,512,256]{1,2,0:T(8,128)(2,1)}, u32[]{:S(2)}, u32[]{:S(2)}) %collective-permute-start.4) | collective-permute-done | bytes 524320 | tf_op jit(solution)/shard_map/ppermute | solution.py:125
  32.9 2.8 %collective-permute-start.2 = (bf16[2,256,256]{1,2,0:T(8,128)(2,1)S(1)}, bf16[2,256,256]{1,2,0:T(8,128)(2,1)S(1)}, u32[]{:S(2)}, u32[]{:S(2)}) collective-permute-start(bf16[2,256,256]{1,2,0:T(8,128)(2,1)S(1)} %slice.67), channel_id=1, source_target_pairs={{0,3},{1,0},{2,1},{3,2},{4,7},{5,4},{6,5},{7,6},{8,11},{9,8},{10,9... | collective-permute-start | bytes 786440 | tf_op jit(solution)/shard_map/ppermute | solution.py:100
  40.9 9.2 %collective-permute-done.2 = bf16[2,256,256]{1,2,0:T(8,128)(2,1)S(1)} collective-permute-done((bf16[2,256,256]{1,2,0:T(8,128)(2,1)S(1)}, bf16[2,256,256]{1,2,0:T(8,128)(2,1)S(1)}, u32[]{:S(2)}, u32[]{:S(2)}) %collective-permute-start.2) | collective-permute-done | bytes 262176 | tf_op jit(solution)/shard_map/ppermute | solution.py:100
  51.1 3.7 %collective-permute-done.6 = bf16[2,512,256]{1,2,0:T(8,128)(2,1)S(1)} collective-permute-done((bf16[2,512,256]{1,2,0:T(8,128)(2,1)}, bf16[2,512,256]{1,2,0:T(8,128)(2,1)S(1)}, u32[]{:S(2)}, u32[]{:S(2)}) %collective-permute-start.6) | collective-permute-done | bytes 524320 | tf_op jit(solution)/shard_map/ppermute | solution.py:99
  55.3 1.3 collective-permute-done.7
  56.7 4.6 %collective-permute-done.8 = bf16[2,256,256]{1,2,0:T(8,128)(2,1)S(1)} collective-permute-done((bf16[2,256,256]{1,2,0:T(8,128)(2,1)S(1)}, bf16[2,256,256]{1,2,0:T(8,128)(2,1)S(1)}, u32[]{:S(2)}, u32[]{:S(2)}) %collective-permute-start.8) | collective-permute-done | bytes 262176 | tf_op jit(solution)/shard_map/ppermute | solution.py:101
  61.3 2.6 broadcast_select_fusion.1
  65.3 4.8 %collective-permute-done.9 = bf16[2,2048,256]{1,2,0:T(8,128)(2,1)} collective-permute-done((bf16[2,2048,256]{1,2,0:T(8,128)(2,1)S(1)}, bf16[2,2048,256]{1,2,0:T(8,128)(2,1)}, u32[]{:S(2)}, u32[]{:S(2)}) %collective-permute-start.9) | collective-permute-done | bytes 2097184 | tf_op jit(solution)/shard_map/ppermute | solution.py:106
  70.1 1.8 broadcast_select_fusion.2
  71.9 1.5 constant_dynamic-slice_fusion
  74.8 3.0 %collective-permute-start.10 = (bf16[2048,256]{1,0:T(8,128)(2,1)}, bf16[2048,256]{1,0:T(8,128)(2,1)S(1)}, u32[]{:S(2)}, u32[]{:S(2)}) collective-permute-start(bf16[2048,256]{1,0:T(8,128)(2,1)} %bitcast.155), channel_id=1, source_target_pairs={{0,96},{32,0},{64,32},{96,64},{1,97},{33,1},{65,33},{97,65},{2,98}... | collective-permute-start | bytes 3145736 | tf_op jit(solution)/shard_map/ppermute | solution.py:136
  78.4 1.6 fusion.51
  83.4 39.9 %collective-permute-done.10 = bf16[2048,256]{1,0:T(8,128)(2,1)S(1)} collective-permute-done((bf16[2048,256]{1,0:T(8,128)(2,1)}, bf16[2048,256]{1,0:T(8,128)(2,1)S(1)}, u32[]{:S(2)}, u32[]{:S(2)}) %collective-permute-start.10) | collective-permute-done | bytes 1048608 | tf_op jit(solution)/shard_map/ppermute | solution.py:136
  123.8 4.2 %fusion.12 = f32[512,256]{1,0:T(8,128)S(1)} fusion(bf16[1,2048,256]{1,2,0:T(8,128)(2,1)} %get-tuple-element.16, bf16[1,2048,256]{1,2,0:T(8,128)(2,1)} %get-tuple-element.17, bf16[2,2048,256]{1,2,0:T(8,128)(2,1)} %copy-done.3, bf16[2,2048,256]{1,2,0:T(8,128)(2,1)} %copy-done.1), kind=kOutput, calls=%fused_computation.19 | convolution fusion | flops 1083179008 | bytes 6815744 | tf_op jit(solution)/shard_map/psm,psn->mn/dot_general | solution.py:112
  129.5 2.2 maximum_select_fusion
  140.4 1.5 collective-permute-start.17
  141.9 11.1 %collective-permute-done.14 = f32[2,256,256]{2,1,0:T(8,128)S(1)} collective-permute-done((f32[2,256,256]{2,1,0:T(8,128)S(1)}, f32[2,256,256]{2,1,0:T(8,128)S(1)}, u32[]{:S(2)}, u32[]{:S(2)}) %collective-permute-start.14) | collective-permute-done | bytes 524320 | tf_op jit(solution)/shard_map/ppermute | solution.py:177
  153.1 1.9 collective-permute-start.15
  158.7 9.2 %collective-permute-done.15 = f32[2,256,256]{2,1,0:T(8,128)S(1)} collective-permute-done((f32[2,256,256]{2,1,0:T(8,128)S(1)}, f32[2,256,256]{2,1,0:T(8,128)S(1)}, u32[]{:S(2)}, u32[]{:S(2)}) %collective-permute-start.15) | collective-permute-done | bytes 524320 | tf_op jit(solution)/shard_map/ppermute | solution.py:177
  167.9 2.0 bitcast_add_fusion.3
  172.9 4.6 %collective-permute-start.16 = (f32[2,256,256]{2,1,0:T(8,128)}, f32[2,256,256]{2,1,0:T(8,128)S(1)}, u32[]{:S(2)}, u32[]{:S(2)}) collective-permute-start(f32[2,256,256]{2,1,0:T(8,128)} %get-tuple-element.7), channel_id=1, source_target_pairs={{0,4},{4,8},{8,12},{1,5},{5,9},{9,13},{2,6},{6,10},{10,14},{3,7},{... | collective-permute-start | bytes 1572872 | tf_op jit(solution)/shard_map/ppermute | solution.py:177
  177.4 6.5 %collective-permute-done.18 = f32[2,256,256]{2,1,0:T(8,128)} collective-permute-done((f32[2,256,256]{2,1,0:T(8,128)S(1)}, f32[2,256,256]{2,1,0:T(8,128)}, u32[]{:S(2)}, u32[]{:S(2)}) %collective-permute-start.18) | collective-permute-done | bytes 524320 | tf_op jit(solution)/shard_map/ppermute | solution.py:178
  185.1 1.9 collective-permute-start.19
  189.6 8.6 %collective-permute-done.19 = f32[2,256,256]{2,1,0:T(8,128)} collective-permute-done((f32[2,256,256]{2,1,0:T(8,128)S(1)}, f32[2,256,256]{2,1,0:T(8,128)}, u32[]{:S(2)}, u32[]{:S(2)}) %collective-permute-start.19) | collective-permute-done | bytes 524320 | tf_op jit(solution)/shard_map/ppermute | solution.py:178
  200.0 2.2 collective-permute-start.21
  202.5 2.2 collective-permute-start.22
  208.6 2.1 collective-permute-start.23
  210.7 11.8 %collective-permute-start.20 = (f32[256,256]{0,1:T(8,128)S(1)}, f32[256,256]{0,1:T(8,128)S(1)}, u32[]{:S(2)}, u32[]{:S(2)}) collective-permute-start(f32[256,256]{0,1:T(8,128)S(1)} %get-tuple-element.35), channel_id=1, source_target_pairs={{0,32},{4,64},{8,128},{12,40},{1,48},{5,16},{9,80},{13,56},{2,168}... | collective-permute-start | bytes 786440 | tf_op jit(solution)/shard_map/ppermute | solution.py:192
  223.3 38.5 %collective-permute-done.23 = f32[256,256]{0,1:T(8,128)S(1)} collective-permute-done((f32[256,256]{0,1:T(8,128)S(1)}, f32[256,256]{0,1:T(8,128)S(1)}, u32[]{:S(2)}, u32[]{:S(2)}) %collective-permute-start.23) | collective-permute-done | bytes 262176 | tf_op jit(solution)/shard_map/ppermute | solution.py:192
  261.8 2.8 %collective-permute-done.20 = f32[256,256]{0,1:T(8,128)S(1)} collective-permute-done((f32[256,256]{0,1:T(8,128)S(1)}, f32[256,256]{0,1:T(8,128)S(1)}, u32[]{:S(2)}, u32[]{:S(2)}) %collective-permute-start.20) | collective-permute-done | bytes 262176 | tf_op jit(solution)/shard_map/ppermute | solution.py:192
  (97 shorter events, 31.0 us)
Async XLA Ops:
  1.5 29.8 %collective-permute-start.4 = (bf16[2,512,256]{1,2,0:T(8,128)(2,1)S(1)}, bf16[2,512,256]{1,2,0:T(8,128)(2,1)}, u32[]{:S(2)}, u32[]{:S(2)}) collective-permute-start(bf16[2,512,256]{1,2,0:T(8,128)(2,1)S(1)} %bitcast.157), channel_id=1, source_target_pairs={{0,128},{128,0},{1,129},{129,1},{2,130},{130,2},{3,131},{131,3},{4... | collective-permute-start | bytes 1572872 | tf_op jit(solution)/shard_map/ppermute | solution.py:125
  8.1 23.8 %collective-permute-start = (bf16[2,512,256]{1,2,0:T(8,128)(2,1)S(1)}, bf16[2,512,256]{1,2,0:T(8,128)(2,1)}, u32[]{:S(2)}, u32[]{:S(2)}) collective-permute-start(bf16[2,512,256]{1,2,0:T(8,128)(2,1)S(1)} %bitcast.150), channel_id=1, source_target_pairs={{0,3},{1,0},{2,1},{3,2},{4,7},{5,4},{6,5},{7,6},{8,11},{9,8},{10,9... | collective-permute-start | bytes 1572872 | tf_op jit(solution)/shard_map/ppermute | solution.py:98
  8.7 27.0 %collective-permute-start.1 = (bf16[2,512,256]{1,2,0:T(8,128)(2,1)S(1)}, bf16[2,512,256]{1,2,0:T(8,128)(2,1)}, u32[]{:S(2)}, u32[]{:S(2)}) collective-permute-start(bf16[2,512,256]{1,2,0:T(8,128)(2,1)S(1)} %bitcast.151), channel_id=1, source_target_pairs={{0,1},{1,2},{2,3},{3,0},{4,5},{5,6},{6,7},{7,4},{8,9},{9,10},{10,1... | collective-permute-start | bytes 1572872 | tf_op jit(solution)/shard_map/ppermute | solution.py:99
  31.3 18.8 %collective-permute-start.5 = (bf16[2,512,256]{1,2,0:T(8,128)(2,1)}, bf16[2,512,256]{1,2,0:T(8,128)(2,1)S(1)}, u32[]{:S(2)}, u32[]{:S(2)}) collective-permute-start(bf16[2,512,256]{1,2,0:T(8,128)(2,1)} %collective-permute-done.4), channel_id=1, source_target_pairs={{0,3},{1,0},{2,1},{3,2},{4,7},{5,4},{6,5},{7,6},{8,11},{9,8},{10,9... | collective-permute-start | bytes 1572872 | tf_op jit(solution)/shard_map/ppermute | solution.py:98
  32.9 17.2 %collective-permute-start.2 = (bf16[2,256,256]{1,2,0:T(8,128)(2,1)S(1)}, bf16[2,256,256]{1,2,0:T(8,128)(2,1)S(1)}, u32[]{:S(2)}, u32[]{:S(2)}) collective-permute-start(bf16[2,256,256]{1,2,0:T(8,128)(2,1)S(1)} %slice.67), channel_id=1, source_target_pairs={{0,3},{1,0},{2,1},{3,2},{4,7},{5,4},{6,5},{7,6},{8,11},{9,8},{10,9... | collective-permute-start | bytes 786440 | tf_op jit(solution)/shard_map/ppermute | solution.py:100
  36.7 14.4 %collective-permute-start.3 = (bf16[2,256,256]{1,2,0:T(8,128)(2,1)S(1)}, bf16[2,256,256]{1,2,0:T(8,128)(2,1)S(1)}, u32[]{:S(2)}, u32[]{:S(2)}) collective-permute-start(bf16[2,256,256]{1,2,0:T(8,128)(2,1)S(1)} %slice.68), channel_id=1, source_target_pairs={{0,1},{1,2},{2,3},{3,0},{4,5},{5,6},{6,7},{7,4},{8,9},{9,10},{10,1... | collective-permute-start | bytes 786440 | tf_op jit(solution)/shard_map/ppermute | solution.py:101
  36.8 18.0 %collective-permute-start.6 = (bf16[2,512,256]{1,2,0:T(8,128)(2,1)}, bf16[2,512,256]{1,2,0:T(8,128)(2,1)S(1)}, u32[]{:S(2)}, u32[]{:S(2)}) collective-permute-start(bf16[2,512,256]{1,2,0:T(8,128)(2,1)} %collective-permute-done.4), channel_id=1, source_target_pairs={{0,1},{1,2},{2,3},{3,0},{4,5},{5,6},{6,7},{7,4},{8,9},{9,10},{10,1... | collective-permute-start | bytes 1572872 | tf_op jit(solution)/shard_map/ppermute | solution.py:99
  50.1 6.5 %collective-permute-start.7 = (bf16[2,256,256]{1,2,0:T(8,128)(2,1)S(1)}, bf16[2,256,256]{1,2,0:T(8,128)(2,1)S(1)}, u32[]{:S(2)}, u32[]{:S(2)}) collective-permute-start(bf16[2,256,256]{1,2,0:T(8,128)(2,1)S(1)} %slice.69), channel_id=1, source_target_pairs={{0,3},{1,0},{2,1},{3,2},{4,7},{5,4},{6,5},{7,6},{8,11},{9,8},{10,9... | collective-permute-start | bytes 786440 | tf_op jit(solution)/shard_map/ppermute | solution.py:100
  51.1 10.2 %copy-start.1 = (bf16[2,2048,256]{1,2,0:T(8,128)(2,1)}, bf16[2,2048,256]{1,2,0:T(8,128)(2,1)S(1)}, u32[]{:S(2)}) copy-start(bf16[2,2048,256]{1,2,0:T(8,128)(2,1)S(1)} %constant_dynamic-update-slice_fusion) | copy-start | bytes 6291460
  54.8 6.5 %collective-permute-start.8 = (bf16[2,256,256]{1,2,0:T(8,128)(2,1)S(1)}, bf16[2,256,256]{1,2,0:T(8,128)(2,1)S(1)}, u32[]{:S(2)}, u32[]{:S(2)}) collective-permute-start(bf16[2,256,256]{1,2,0:T(8,128)(2,1)S(1)} %slice.70), channel_id=1, source_target_pairs={{0,1},{1,2},{2,3},{3,0},{4,5},{5,6},{6,7},{7,4},{8,9},{9,10},{10,1... | collective-permute-start | bytes 786440 | tf_op jit(solution)/shard_map/ppermute | solution.py:101
  61.3 2.6 copy-start.3
  63.9 1.4 copy-start
  63.9 6.2 %collective-permute-start.9 = (bf16[2,2048,256]{1,2,0:T(8,128)(2,1)S(1)}, bf16[2,2048,256]{1,2,0:T(8,128)(2,1)}, u32[]{:S(2)}, u32[]{:S(2)}) collective-permute-start(bf16[2,2048,256]{1,2,0:T(8,128)(2,1)S(1)} %broadcast_select_fusion.1), channel_id=1, source_target_pairs={{0,16},{2,18},{17,1},{19,3},{4,20},{6,22},{21,5},{23,7},{8,24},{10... | collective-permute-start | bytes 6291464 | tf_op jit(solution)/shard_map/ppermute | solution.py:106
  74.8 48.5 %collective-permute-start.10 = (bf16[2048,256]{1,0:T(8,128)(2,1)}, bf16[2048,256]{1,0:T(8,128)(2,1)S(1)}, u32[]{:S(2)}, u32[]{:S(2)}) collective-permute-start(bf16[2048,256]{1,0:T(8,128)(2,1)} %bitcast.155), channel_id=1, source_target_pairs={{0,96},{32,0},{64,32},{96,64},{1,97},{33,1},{65,33},{97,65},{2,98}... | collective-permute-start | bytes 3145736 | tf_op jit(solution)/shard_map/ppermute | solution.py:136
  77.8 45.5 %collective-permute-start.12 = (bf16[2048,256]{1,0:T(8,128)(2,1)}, bf16[2048,256]{1,0:T(8,128)(2,1)}, u32[]{:S(2)}, u32[]{:S(2)}) collective-permute-start(bf16[2048,256]{1,0:T(8,128)(2,1)} %bitcast.156), channel_id=1, source_target_pairs={{0,64},{32,96},{64,0},{96,32},{1,65},{33,97},{65,1},{97,33},{2,66}... | collective-permute-start | bytes 3145736 | tf_op jit(solution)/shard_map/ppermute | solution.py:136
  123.3 6.2 %collective-permute-start.11 = (bf16[2048,256]{1,0:T(8,128)(2,1)S(1)}, bf16[2048,256]{1,0:T(8,128)(2,1)S(1)}, u32[]{:S(2)}, u32[]{:S(2)}) collective-permute-start(bf16[2048,256]{1,0:T(8,128)(2,1)S(1)} %collective-permute-done.10), channel_id=1, source_target_pairs={{0,16},{16,0},{1,17},{17,1},{2,18},{18,2},{3,19},{19,3},{4,20},{20... | collective-permute-start | bytes 3145736 | tf_op jit(solution)/shard_map/ppermute | solution.py:137
  123.3 6.2 %collective-permute-start.13 = (bf16[2048,256]{1,0:T(8,128)(2,1)}, bf16[2048,256]{1,0:T(8,128)(2,1)S(1)}, u32[]{:S(2)}, u32[]{:S(2)}) collective-permute-start(bf16[2048,256]{1,0:T(8,128)(2,1)} %collective-permute-done.12), channel_id=1, source_target_pairs={{0,16},{16,0},{1,17},{17,1},{2,18},{18,2},{3,19},{19,3},{4,20},{20... | collective-permute-start | bytes 3145736 | tf_op jit(solution)/shard_map/ppermute | solution.py:137
  123.8 4.2 %copy-start.2 = (bf16[2,2048,256]{1,2,0:T(8,128)(2,1)S(1)}, bf16[2,2048,256]{1,2,0:T(8,128)(2,1)}, u32[]{:S(2)}) copy-start(bf16[2,2048,256]{1,2,0:T(8,128)(2,1)} %copy-done.1) | copy-start | bytes 6291460
  123.8 4.3 %copy-start.4 = (bf16[2,2048,256]{1,2,0:T(8,128)(2,1)S(1)}, bf16[2,2048,256]{1,2,0:T(8,128)(2,1)}, u32[]{:S(2)}) copy-start(bf16[2,2048,256]{1,2,0:T(8,128)(2,1)} %copy-done.3) | copy-start | bytes 6291460
  137.3 15.7 %collective-permute-start.14 = (f32[2,256,256]{2,1,0:T(8,128)S(1)}, f32[2,256,256]{2,1,0:T(8,128)S(1)}, u32[]{:S(2)}, u32[]{:S(2)}) collective-permute-start(f32[2,256,256]{2,1,0:T(8,128)S(1)} %get-tuple-element.9), channel_id=1, source_target_pairs={{0,4},{1,5},{2,6},{3,7},{16,20},{17,21},{18,22},{19,23},{32,36},{3... | collective-permute-start | bytes 1572872 | tf_op jit(solution)/shard_map/ppermute | solution.py:177
  140.4 18.3 %collective-permute-start.17 = (f32[2,256,256]{2,1,0:T(8,128)}, f32[2,256,256]{2,1,0:T(8,128)}, u32[]{:S(2)}, u32[]{:S(2)}) collective-permute-start(f32[2,256,256]{2,1,0:T(8,128)} %get-tuple-element.10), channel_id=1, source_target_pairs={{12,8},{13,9},{14,10},{15,11},{28,24},{29,25},{30,26},{31,27},{44,... | collective-permute-start | bytes 1572872 | tf_op jit(solution)/shard_map/ppermute | solution.py:178
  153.1 14.9 %collective-permute-start.15 = (f32[2,256,256]{2,1,0:T(8,128)S(1)}, f32[2,256,256]{2,1,0:T(8,128)S(1)}, u32[]{:S(2)}, u32[]{:S(2)}) collective-permute-start(f32[2,256,256]{2,1,0:T(8,128)S(1)} %bitcast_add_fusion.2), channel_id=1, source_target_pairs={{0,4},{4,8},{1,5},{5,9},{2,6},{6,10},{3,7},{7,11},{16,20},{20,24},... | collective-permute-start | bytes 1572872 | tf_op jit(solution)/shard_map/ppermute | solution.py:177
  169.9 14.1 %collective-permute-start.18 = (f32[2,256,256]{2,1,0:T(8,128)S(1)}, f32[2,256,256]{2,1,0:T(8,128)}, u32[]{:S(2)}, u32[]{:S(2)}) collective-permute-start(f32[2,256,256]{2,1,0:T(8,128)S(1)} %get-tuple-element.8), channel_id=1, source_target_pairs={{12,8},{8,4},{13,9},{9,5},{14,10},{10,6},{15,11},{11,7},{28,24},{2... | collective-permute-start | bytes 1572872 | tf_op jit(solution)/shard_map/ppermute | solution.py:178
  172.9 16.7 %collective-permute-start.16 = (f32[2,256,256]{2,1,0:T(8,128)}, f32[2,256,256]{2,1,0:T(8,128)S(1)}, u32[]{:S(2)}, u32[]{:S(2)}) collective-permute-start(f32[2,256,256]{2,1,0:T(8,128)} %get-tuple-element.7), channel_id=1, source_target_pairs={{0,4},{4,8},{8,12},{1,5},{5,9},{9,13},{2,6},{6,10},{10,14},{3,7},{... | collective-permute-start | bytes 1572872 | tf_op jit(solution)/shard_map/ppermute | solution.py:177
  185.1 13.2 %collective-permute-start.19 = (f32[2,256,256]{2,1,0:T(8,128)S(1)}, f32[2,256,256]{2,1,0:T(8,128)}, u32[]{:S(2)}, u32[]{:S(2)}) collective-permute-start(f32[2,256,256]{2,1,0:T(8,128)S(1)} %bitcast_add_fusion.1), channel_id=1, source_target_pairs={{12,8},{8,4},{4,0},{13,9},{9,5},{5,1},{14,10},{10,6},{6,2},{15,11}... | collective-permute-start | bytes 1572872 | tf_op jit(solution)/shard_map/ppermute | solution.py:178
  200.0 22.5 %collective-permute-start.21 = (f32[256,256]{0,1:T(8,128)S(1)}, f32[256,256]{0,1:T(8,128)S(1)}, u32[]{:S(2)}, u32[]{:S(2)}) collective-permute-start(f32[256,256]{0,1:T(8,128)S(1)} %copy.49), channel_id=1, source_target_pairs={{0,2},{4,4},{8,0},{12,130},{1,3},{5,1},{9,5},{13,131},{2,138},{6,1... | collective-permute-start | bytes 786440 | tf_op jit(solution)/shard_map/ppermute | solution.py:192
  202.5 20.5 %collective-permute-start.22 = (f32[256,256]{1,0:T(8,128)S(1)}, f32[256,256]{1,0:T(8,128)S(1)}, u32[]{:S(2)}, u32[]{:S(2)}) collective-permute-start(f32[256,256]{1,0:T(8,128)S(1)} %copy.57), channel_id=1, source_target_pairs={{0,2},{4,4},{8,8},{12,130},{1,3},{5,1},{9,5},{13,131},{2,138},{6,1... | collective-permute-start | bytes 786440 | tf_op jit(solution)/shard_map/ppermute | solution.py:192
  208.6 53.2 %collective-permute-start.23 = (f32[256,256]{0,1:T(8,128)S(1)}, f32[256,256]{0,1:T(8,128)S(1)}, u32[]{:S(2)}, u32[]{:S(2)}) collective-permute-start(f32[256,256]{0,1:T(8,128)S(1)} %get-tuple-element.22), channel_id=1, source_target_pairs={{0,32},{4,64},{12,40},{1,48},{5,16},{9,80},{13,56},{2,168},{6,200}... | collective-permute-start | bytes 786440 | tf_op jit(solution)/shard_map/ppermute | solution.py:192
  210.7 53.9 %collective-permute-start.20 = (f32[256,256]{0,1:T(8,128)S(1)}, f32[256,256]{0,1:T(8,128)S(1)}, u32[]{:S(2)}, u32[]{:S(2)}) collective-permute-start(f32[256,256]{0,1:T(8,128)S(1)} %get-tuple-element.35), channel_id=1, source_target_pairs={{0,32},{4,64},{8,128},{12,40},{1,48},{5,16},{9,80},{13,56},{2,168}... | collective-permute-start | bytes 786440 | tf_op jit(solution)/shard_map/ppermute | solution.py:192

commit v2 on v1

--- a/solution.py
+++ b/solution.py
@@ -99,18 +99,15 @@
     below = lax.ppermute(block, "x", ring(4, 1))
     far_a = lax.ppermute(above[:, :half], "x", ring(4, -1))
     far_b = lax.ppermute(below[:, half:], "x", ring(4, 1))
-    return jnp.concatenate([block, above, below, far_a, far_b], axis=1)
-
-
-def from_core(mine, core_perm):
-    return lax.ppermute(mine, ("core", "x"), core_perm)
-
-
-def both_products(rows, cols):
-    real = jnp.einsum("psm,psn->mn", rows, cols, preferred_element_type=jnp.float32)
-    turned = jnp.stack([cols[1], -cols[0]])
-    imag = jnp.einsum("psm,psn->mn", rows, turned, preferred_element_type=jnp.float32)
-    return real, imag
+    return block, jnp.concatenate([above, below], axis=1), jnp.concatenate([far_a, far_b], axis=1)
+
+
+def with_turned(real, imag):
+    return jnp.stack([jnp.concatenate([real, imag], axis=1), jnp.concatenate([imag, -real], axis=1)])
+
+
+def product(rows, cols):
+    return jnp.einsum("psm,psn->mn", rows, cols, preferred_element_type=jnp.float32)
 
 
 def body(wavefield):
@@ -123,32 +120,39 @@
     own = lax.dynamic_index_in_dim(wavefield, f, 0, keepdims=False)
     other = lax.dynamic_index_in_dim(wavefield, 1 - f, 0, keepdims=False)
     other = lax.ppermute(other, "zh", ring(2, 1))
-    block0, block1 = gather_x(own), gather_x(other)
+    group0, group1 = gather_x(own), gather_x(other)
 
     e_col, core_col = x // 2, x % 2
-    mine = jnp.where(e_col == 0, block0, block1)
+    same = core_col == core
+    e_row2 = jnp.where(y < 2, e_col, 1 - e_col)
     one_way = [(a * 4 + b, (1 - a) * 4 + b) for a in range(2) for b in range(4) if b % 2 == a]
-    cols0 = jnp.where(core_col == core, mine, from_core(mine, one_way))
-    part = lax.dynamic_index_in_dim(cols0, core, 0, keepdims=False)
     swap = ring(2, 1)
-
-    def from_y(step):
-        near = lax.ppermute(part, "y", ring(4, -step))
-        far = lax.ppermute(near, "core", swap)
-        return jnp.where(core == 0, jnp.stack([near, far]), jnp.stack([far, near]))
-
-    cols1, cols2 = from_y(1), from_y(2)
-
-    rows = jnp.concatenate([block0, block1], axis=2)
-    real1, imag1 = both_products(rows, cols1)
-    e_row2 = jnp.where(y < 2, e_col, 1 - e_col)
-    real2, imag2 = both_products(jnp.where(e_row2 == 0, block0, block1), cols2)
-    real0, imag0 = both_products(rows, cols0)
+    product0 = product1 = product2 = 0.0
+
+    def on_both(part):
+        far = lax.ppermute(part, "core", swap)
+        return with_turned(jnp.where(core == 0, part, far), jnp.where(core == 0, far, part))
+
+    for group, (block0, block1) in enumerate(zip(group0, group1)):
+        mine = jnp.where(e_col == 0, block0, block1)
+        cols0 = jnp.where(same, mine, lax.ppermute(mine, ("core", "x"), one_way))
+        part0 = lax.dynamic_index_in_dim(cols0, core, 0, keepdims=False)
+        part1 = lax.ppermute(part0, "y", ring(4, -1))
+        if group < 2:
+            part2 = lax.ppermute(lax.ppermute(part0, "y", ring(4, 1)), "y", ring(4, 1))
+        else:
+            part2 = lax.ppermute(part1, "y", ring(4, -1))
+        rows = jnp.concatenate([block0, block1], axis=2)
+        product0 += product(rows, with_turned(cols0[0], cols0[1]))
+        product1 += product(rows, on_both(part1))
+        product2 += product(jnp.where(e_row2 == 0, block0, block1), on_both(part2))
+    real0, imag0 = product0[:, :n], product0[:, n:]
+    real1, imag1 = product1[:, :n], product1[:, n:]
+    real2, imag2 = product2[:, :n], product2[:, n:]
 
     def rows_of(a, e):
         return lax.dynamic_slice_in_dim(a, e * n, n, 0)
 
-    same = core_col == core
     e_row0 = jnp.where(same, 1 - e_col, jnp.where(core == 0, e_col, 1 - e_col))
     upper = lax.broadcasted_iota(jnp.int32, (n, n), 0) <= lax.broadcasted_iota(jnp.int32, (n, n), 1)
     packed = jnp.where(upper, rows_of(real0, e_col), rows_of(imag0, e_col))

time: 268 us -> 257 us (0.959)
  waiting for transfers between devices: 161 us -> 142 us
  starting transfers between devices: 50.1 us -> 56.8 us
    ppermute x5 -> x17, waiting for transfers between devices: 44.7 us -> 28 us  [the longest x4 20.3 us: body(): part2 = lax.ppermute(lax.ppermute(part0, 'y', ring(4, 1)), 'y', ring(4, 1))]
    ppermute x5 -> x17, starting transfers between devices: 5.45 us -> 15.8 us  [the longest x3 6.18 us: body(): part1 = lax.ppermute(part0, 'y', ring(4, -1))]
    ppermute x2, waiting for transfers between devices: 0.01 us -> 8.76 us  [gather_x(): above = lax.ppermute(block, 'x', ring(4, -1))]
    ppermute x2, waiting for transfers between devices: 10.5 us -> 3.88 us  [gather_x(): far_a = lax.ppermute(above[:, :half], 'x', ring(4, -1))]
    ppermute x1, waiting for transfers between devices: 21.1 us -> 15.2 us  [body(): other = lax.ppermute(other, 'zh', ring(2, 1))]
    dynamic_slice x1 -> x5, local copies, waits for them, and re-layouts: 1.31 us -> 6.78 us  [body(): part0 = lax.dynamic_index_in_dim(cols0, core, 0, keepdims=False)]
    ppermute x4, starting transfers between devices: 18.3 us -> 13.7 us  [body(): got = [lax.ppermute(s, AXES, perm) for s, perm in zip(send, perms)]]
    ppermute x4, waiting for transfers between devices: 41.3 us -> 45.9 us  [body(): got = [lax.ppermute(s, AXES, perm) for s, perm in zip(send, perms)]]
  transfers between devices with their start and end apart: 24 -> 36, of which waited for: 13 -> 18; matrix products, arithmetic and copies ran while one was open for 6% -> 11% of each run, Pallas kernels for 0% -> 0%
where the time goes in v2:
time: 257 us; the launch traced here: 256 us
  waiting for transfers between devices  142 us (55%)
  starting transfers between devices  56.8 us (22%)
  local copies, waits for them, and re-layouts  17.1 us (7%)
  between operations  17.1 us (7%)
  other arithmetic  15.7 us (6%)
  matrix products  7.07 us (3%)
    ppermute x4, waiting for transfers between devices, body(): got = [lax.ppermute(s, AXES, perm) for s, perm in zip(send, perms)]  45.9 us
    ppermute x3, waiting for transfers between devices, body(): up = lax.ppermute(send_up, 'zl', [(i, i + 1) for i in range(step)])  20.8 us
    ppermute x4, waiting for transfers between devices, body(): part2 = lax.ppermute(lax.ppermute(part0, 'y', ring(4, 1)), 'y', ring(4, 1))  20.3 us
    ppermute x3, waiting for transfers between devices, body(): down = lax.ppermute(send_down, 'zl', [(3 - i, 2 - i) for i in range(step)])  15.4 us
    ppermute x1, waiting for transfers between devices, body(): other = lax.ppermute(other, 'zh', ring(2, 1))  15.2 us
    ppermute x4, starting transfers between devices, body(): got = [lax.ppermute(s, AXES, perm) for s, perm in zip(send, perms)]  13.7 us
    ppermute x2, waiting for transfers between devices, gather_x(): above = lax.ppermute(block, 'x', ring(4, -1))  8.76 us
    ppermute x3, starting transfers between devices, body(): up = lax.ppermute(send_up, 'zl', [(i, i + 1) for i in range(step)])  7.75 us
  transfers between devices with their start and end apart: 36, of which 18 were waited for; matrix products, arithmetic and copies ran while one was open for 11% of the time, Pallas kernels for 0%

profile of v2, /device:TPU:34, one launch (start us, length us, event | category | flops | bytes accessed | tf_op | source)
XLA Modules:
  0.0 255.7 jit_solution(15250109583805885908)
XLA Ops:
  3.8 6.4 %collective-permute-start = (bf16[2,512,256]{1,2,0:T(8,128)(2,1)S(1)}, bf16[2,512,256]{1,2,0:T(8,128)(2,1)S(1)}, u32[]{:S(2)}, u32[]{:S(2)}) collective-permute-start(bf16[2,512,256]{1,2,0:T(8,128)(2,1)S(1)} %bitcast.223), channel_id=1, source_target_pairs={{0,128},{128,0},{1,129},{129,1},{2,130},{130,2},{3,131},{131,3},{4... | collective-permute-start | bytes 1572872 | tf_op jit(solution)/shard_map/ppermute | solution.py:122
  10.2 1.6 fusion.100
  17.8 15.2 %collective-permute-done = bf16[2,512,256]{1,2,0:T(8,128)(2,1)S(1)} collective-permute-done((bf16[2,512,256]{1,2,0:T(8,128)(2,1)S(1)}, bf16[2,512,256]{1,2,0:T(8,128)(2,1)S(1)}, u32[]{:S(2)}, u32[]{:S(2)}) %collective-permute-start) | collective-permute-done | bytes 524320 | tf_op jit(solution)/shard_map/ppermute | solution.py:122
  36.5 8.8 %collective-permute-done.6 = bf16[2,512,256]{1,2,0:T(8,128)(2,1)S(1)} collective-permute-done((bf16[2,512,256]{1,2,0:T(8,128)(2,1)S(1)}, bf16[2,512,256]{1,2,0:T(8,128)(2,1)S(1)}, u32[]{:S(2)}, u32[]{:S(2)}) %collective-permute-start.6) | collective-permute-done | bytes 524320 | tf_op jit(solution)/shard_map/ppermute | solution.py:98
  45.3 2.1 collective-permute-start.13
  48.0 3.9 %collective-permute-done.13 = bf16[2,256,256]{1,2,0:T(8,128)(2,1)S(1)} collective-permute-done((bf16[2,256,256]{1,2,0:T(8,128)(2,1)S(1)}, bf16[2,256,256]{1,2,0:T(8,128)(2,1)S(1)}, u32[]{:S(2)}, u32[]{:S(2)}) %collective-permute-start.13) | collective-permute-done | bytes 262176 | tf_op jit(solution)/shard_map/ppermute | solution.py:100
  51.9 3.7 %collective-permute-done.14 = bf16[2,256,256]{1,2,0:T(8,128)(2,1)S(1)} collective-permute-done((bf16[2,256,256]{1,2,0:T(8,128)(2,1)S(1)}, bf16[2,256,256]{1,2,0:T(8,128)(2,1)S(1)}, u32[]{:S(2)}, u32[]{:S(2)}) %collective-permute-start.14) | collective-permute-done | bytes 262176 | tf_op jit(solution)/shard_map/ppermute | solution.py:101
  61.5 1.8 copy.45
  64.8 1.7 collective-permute-start.2
  66.5 1.8 copy.47
  68.3 1.8 collective-permute-start.16
  75.9 4.0 %collective-permute-done.16 = bf16[512,256]{1,0:T(8,128)(2,1)} collective-permute-done((bf16[512,256]{1,0:T(8,128)(2,1)}, bf16[512,256]{1,0:T(8,128)(2,1)}, u32[]{:S(2)}, u32[]{:S(2)}) %collective-permute-start.16) | collective-permute-done | bytes 262176 | tf_op jit(solution)/shard_map/ppermute | solution.py:140
  79.9 2.9 %collective-permute-start.24 = (bf16[512,256]{1,0:T(8,128)(2,1)}, bf16[512,256]{1,0:T(8,128)(2,1)S(1)}, u32[]{:S(2)}, u32[]{:S(2)}) collective-permute-start(bf16[512,256]{1,0:T(8,128)(2,1)} %collective-permute-done.16), channel_id=1, source_target_pairs={{0,96},{32,0},{64,32},{96,64},{1,97},{33,1},{65,33},{97,65},{2,98}... | collective-permute-start | bytes 786440 | tf_op jit(solution)/shard_map/ppermute | solution.py:144
  88.3 2.7 %collective-permute-start.9 = (bf16[1024,256]{1,0:T(8,128)(2,1)S(1)}, bf16[1024,256]{1,0:T(8,128)(2,1)S(1)}, u32[]{:S(2)}, u32[]{:S(2)}) collective-permute-start(bf16[1024,256]{1,0:T(8,128)(2,1)S(1)} %bitcast.225), channel_id=1, source_target_pairs={{0,96},{32,0},{64,32},{96,64},{1,97},{33,1},{65,33},{97,65},{2,98}... | collective-permute-start | bytes 1572872 | tf_op jit(solution)/shard_map/ppermute | solution.py:140
  91.0 3.8 %collective-permute-done.19 = bf16[512,256]{1,0:T(8,128)(2,1)} collective-permute-done((bf16[512,256]{1,0:T(8,128)(2,1)}, bf16[512,256]{1,0:T(8,128)(2,1)}, u32[]{:S(2)}, u32[]{:S(2)}) %collective-permute-start.19) | collective-permute-done | bytes 262176 | tf_op jit(solution)/shard_map/ppermute | solution.py:142
  100.3 2.3 collective-permute-done.9
  103.1 2.5 collective-permute-done.21
  106.3 14.0 %collective-permute-done.22 = bf16[1024,256]{1,0:T(8,128)(2,1)S(1)} collective-permute-done((bf16[1024,256]{1,0:T(8,128)(2,1)S(1)}, bf16[1024,256]{1,0:T(8,128)(2,1)S(1)}, u32[]{:S(2)}, u32[]{:S(2)}) %collective-permute-start.22) | collective-permute-done | bytes 524320 | tf_op jit(solution)/shard_map/ppermute | solution.py:142
  128.9 11.4 %collective-permute-done.26 = f32[2,256,256]{2,1,0:T(8,128)S(1)} collective-permute-done((f32[2,256,256]{2,1,0:T(8,128)S(1)}, f32[2,256,256]{2,1,0:T(8,128)S(1)}, u32[]{:S(2)}, u32[]{:S(2)}) %collective-permute-start.26) | collective-permute-done | bytes 524320 | tf_op jit(solution)/shard_map/ppermute | solution.py:181
  140.4 1.9 collective-permute-start.27
  146.1 9.3 %collective-permute-done.27 = f32[2,256,256]{2,1,0:T(8,128)S(1)} collective-permute-done((f32[2,256,256]{2,1,0:T(8,128)S(1)}, f32[2,256,256]{2,1,0:T(8,128)S(1)}, u32[]{:S(2)}, u32[]{:S(2)}) %collective-permute-start.27) | collective-permute-done | bytes 524320 | tf_op jit(solution)/shard_map/ppermute | solution.py:181
  155.4 2.2 bitcast_add_fusion.3
  160.9 4.6 %collective-permute-start.28 = (f32[2,256,256]{2,1,0:T(8,128)}, f32[2,256,256]{2,1,0:T(8,128)S(1)}, u32[]{:S(2)}, u32[]{:S(2)}) collective-permute-start(f32[2,256,256]{2,1,0:T(8,128)} %get-tuple-element.19), channel_id=1, source_target_pairs={{0,4},{4,8},{8,12},{1,5},{5,9},{9,13},{2,6},{6,10},{10,14},{3,7},{... | collective-permute-start | bytes 1572872 | tf_op jit(solution)/shard_map/ppermute | solution.py:181
  165.5 6.5 %collective-permute-done.30 = f32[2,256,256]{2,1,0:T(8,128)} collective-permute-done((f32[2,256,256]{2,1,0:T(8,128)}, f32[2,256,256]{2,1,0:T(8,128)}, u32[]{:S(2)}, u32[]{:S(2)}) %collective-permute-start.30) | collective-permute-done | bytes 524320 | tf_op jit(solution)/shard_map/ppermute | solution.py:182
  173.1 1.9 collective-permute-start.31
  177.5 8.9 %collective-permute-done.31 = f32[2,256,256]{2,1,0:T(8,128)} collective-permute-done((f32[2,256,256]{2,1,0:T(8,128)S(1)}, f32[2,256,256]{2,1,0:T(8,128)}, u32[]{:S(2)}, u32[]{:S(2)}) %collective-permute-start.31) | collective-permute-done | bytes 524320 | tf_op jit(solution)/shard_map/ppermute | solution.py:182
  188.2 2.2 collective-permute-start.33
  191.4 3.8 %collective-permute-start.34 = (f32[256,256]{1,0:T(8,128)S(1)}, f32[256,256]{1,0:T(8,128)S(1)}, u32[]{:S(2)}, u32[]{:S(2)}) collective-permute-start(f32[256,256]{1,0:T(8,128)S(1)} %copy.63), channel_id=1, source_target_pairs={{0,2},{4,4},{8,8},{12,130},{1,3},{5,1},{9,5},{13,131},{2,138},{6,1... | collective-permute-start | bytes 786440 | tf_op jit(solution)/shard_map/ppermute | solution.py:196
  199.1 1.9 collective-permute-start.35
  201.1 5.7 %collective-permute-start.32 = (f32[256,256]{0,1:T(8,128)}, f32[256,256]{0,1:T(8,128)S(1)}, u32[]{:S(2)}, u32[]{:S(2)}) collective-permute-start(f32[256,256]{0,1:T(8,128)} %get-tuple-element.65), channel_id=1, source_target_pairs={{0,32},{4,64},{8,128},{12,40},{1,48},{5,16},{9,80},{13,56},{2,168}... | collective-permute-start | bytes 786440 | tf_op jit(solution)/shard_map/ppermute | solution.py:196
  207.6 41.4 %collective-permute-done.35 = f32[256,256]{0,1:T(8,128)S(1)} collective-permute-done((f32[256,256]{0,1:T(8,128)}, f32[256,256]{0,1:T(8,128)S(1)}, u32[]{:S(2)}, u32[]{:S(2)}) %collective-permute-start.35) | collective-permute-done | bytes 262176 | tf_op jit(solution)/shard_map/ppermute | solution.py:196
  249.0 4.5 %collective-permute-done.32 = f32[256,256]{0,1:T(8,128)S(1)} collective-permute-done((f32[256,256]{0,1:T(8,128)}, f32[256,256]{0,1:T(8,128)S(1)}, u32[]{:S(2)}, u32[]{:S(2)}) %collective-permute-start.32) | collective-permute-done | bytes 262176 | tf_op jit(solution)/shard_map/ppermute | solution.py:196
  (165 shorter events, 51.4 us)
Async XLA Ops:
  1.5 14.0 %collective-permute-start.4 = (bf16[2,512,256]{1,2,0:T(8,128)(2,1)S(1)}, bf16[2,512,256]{1,2,0:T(8,128)(2,1)S(1)}, u32[]{:S(2)}, u32[]{:S(2)}) collective-permute-start(bf16[2,512,256]{1,2,0:T(8,128)(2,1)S(1)} %bitcast.219), channel_id=1, source_target_pairs={{0,3},{1,0},{2,1},{3,2},{4,7},{5,4},{6,5},{7,6},{8,11},{9,8},{10,9... | collective-permute-start | bytes 1572872 | tf_op jit(solution)/shard_map/ppermute | solution.py:98
  2.1 14.8 %collective-permute-start.5 = (bf16[2,512,256]{1,2,0:T(8,128)(2,1)S(1)}, bf16[2,512,256]{1,2,0:T(8,128)(2,1)S(1)}, u32[]{:S(2)}, u32[]{:S(2)}) collective-permute-start(bf16[2,512,256]{1,2,0:T(8,128)(2,1)S(1)} %bitcast.220), channel_id=1, source_target_pairs={{0,1},{1,2},{2,3},{3,0},{4,5},{5,6},{6,7},{7,4},{8,9},{9,10},{10,1... | collective-permute-start | bytes 1572872 | tf_op jit(solution)/shard_map/ppermute | solution.py:99
  3.8 29.1 %collective-permute-start = (bf16[2,512,256]{1,2,0:T(8,128)(2,1)S(1)}, bf16[2,512,256]{1,2,0:T(8,128)(2,1)S(1)}, u32[]{:S(2)}, u32[]{:S(2)}) collective-permute-start(bf16[2,512,256]{1,2,0:T(8,128)(2,1)S(1)} %bitcast.223), channel_id=1, source_target_pairs={{0,128},{128,0},{1,129},{129,1},{2,130},{130,2},{3,131},{131,3},{4... | collective-permute-start | bytes 1572872 | tf_op jit(solution)/shard_map/ppermute | solution.py:122
  15.6 20.9 %collective-permute-start.11 = (bf16[2,256,256]{1,2,0:T(8,128)(2,1)S(1)}, bf16[2,256,256]{1,2,0:T(8,128)(2,1)S(1)}, u32[]{:S(2)}, u32[]{:S(2)}) collective-permute-start(bf16[2,256,256]{1,2,0:T(8,128)(2,1)S(1)} %slice.89), channel_id=1, source_target_pairs={{0,3},{1,0},{2,1},{3,2},{4,7},{5,4},{6,5},{7,6},{8,11},{9,8},{10,9... | collective-permute-start | bytes 786440 | tf_op jit(solution)/shard_map/ppermute | solution.py:100
  16.9 30.5 %collective-permute-start.12 = (bf16[2,256,256]{1,2,0:T(8,128)(2,1)S(1)}, bf16[2,256,256]{1,2,0:T(8,128)(2,1)S(1)}, u32[]{:S(2)}, u32[]{:S(2)}) collective-permute-start(bf16[2,256,256]{1,2,0:T(8,128)(2,1)S(1)} %slice.90), channel_id=1, source_target_pairs={{0,1},{1,2},{2,3},{3,0},{4,5},{5,6},{6,7},{7,4},{8,9},{9,10},{10,1... | collective-permute-start | bytes 786440 | tf_op jit(solution)/shard_map/ppermute | solution.py:101
  32.9 12.3 %collective-permute-start.6 = (bf16[2,512,256]{1,2,0:T(8,128)(2,1)S(1)}, bf16[2,512,256]{1,2,0:T(8,128)(2,1)S(1)}, u32[]{:S(2)}, u32[]{:S(2)}) collective-permute-start(bf16[2,512,256]{1,2,0:T(8,128)(2,1)S(1)} %collective-permute-done), channel_id=1, source_target_pairs={{0,3},{1,0},{2,1},{3,2},{4,7},{5,4},{6,5},{7,6},{8,11},{9,8},{10,9... | collective-permute-start | bytes 1572872 | tf_op jit(solution)/shard_map/ppermute | solution.py:98
  34.5 13.3 %collective-permute-start.7 = (bf16[2,512,256]{1,2,0:T(8,128)(2,1)S(1)}, bf16[2,512,256]{1,2,0:T(8,128)(2,1)S(1)}, u32[]{:S(2)}, u32[]{:S(2)}) collective-permute-start(bf16[2,512,256]{1,2,0:T(8,128)(2,1)S(1)} %collective-permute-done), channel_id=1, source_target_pairs={{0,1},{1,2},{2,3},{3,0},{4,5},{5,6},{6,7},{7,4},{8,9},{9,10},{10,1... | collective-permute-start | bytes 1572872 | tf_op jit(solution)/shard_map/ppermute | solution.py:99
  35.0 24.1 %collective-permute-start.1 = (bf16[2,512,256]{1,2,0:T(8,128)(2,1)S(1)}, bf16[2,512,256]{1,2,0:T(8,128)(2,1)S(1)}, u32[]{:S(2)}, u32[]{:S(2)}) collective-permute-start(bf16[2,512,256]{1,2,0:T(8,128)(2,1)S(1)} %broadcast_select_fusion.7), channel_id=1, source_target_pairs={{0,16},{2,18},{17,1},{19,3},{4,20},{6,22},{21,5},{23,7},{8,24},{10... | collective-permute-start | bytes 1572872 | tf_op jit(solution)/shard_map/ppermute | solution.py:138
  45.3 6.6 %collective-permute-start.13 = (bf16[2,256,256]{1,2,0:T(8,128)(2,1)S(1)}, bf16[2,256,256]{1,2,0:T(8,128)(2,1)S(1)}, u32[]{:S(2)}, u32[]{:S(2)}) collective-permute-start(bf16[2,256,256]{1,2,0:T(8,128)(2,1)S(1)} %slice.91), channel_id=1, source_target_pairs={{0,3},{1,0},{2,1},{3,2},{4,7},{5,4},{6,5},{7,6},{8,11},{9,8},{10,9... | collective-permute-start | bytes 786440 | tf_op jit(solution)/shard_map/ppermute | solution.py:100
  47.8 7.8 %collective-permute-start.14 = (bf16[2,256,256]{1,2,0:T(8,128)(2,1)S(1)}, bf16[2,256,256]{1,2,0:T(8,128)(2,1)S(1)}, u32[]{:S(2)}, u32[]{:S(2)}) collective-permute-start(bf16[2,256,256]{1,2,0:T(8,128)(2,1)S(1)} %slice.92), channel_id=1, source_target_pairs={{0,1},{1,2},{2,3},{3,0},{4,5},{5,6},{6,7},{7,4},{8,9},{9,10},{10,1... | collective-permute-start | bytes 786440 | tf_op jit(solution)/shard_map/ppermute | solution.py:101
  57.8 15.5 %collective-permute-start.8 = (bf16[2,1024,256]{1,2,0:T(8,128)(2,1)S(1)}, bf16[2,1024,256]{1,2,0:T(8,128)(2,1)}, u32[]{:S(2)}, u32[]{:S(2)}) collective-permute-start(bf16[2,1024,256]{1,2,0:T(8,128)(2,1)S(1)} %broadcast_select_fusion), channel_id=1, source_target_pairs={{0,16},{2,18},{17,1},{19,3},{4,20},{6,22},{21,5},{23,7},{8,24},{10... | collective-permute-start | bytes 3145736 | tf_op jit(solution)/shard_map/ppermute | solution.py:138
  63.3 20.9 %collective-permute-start.18 = (bf16[512,256]{1,0:T(8,128)(2,1)}, bf16[512,256]{1,0:T(8,128)(2,1)}, u32[]{:S(2)}, u32[]{:S(2)}) collective-permute-start(bf16[512,256]{1,0:T(8,128)(2,1)} %bitcast.226), channel_id=1, source_target_pairs={{0,32},{32,64},{64,96},{96,0},{1,33},{33,65},{65,97},{97,1},{2,34}... | collective-permute-start | bytes 786440 | tf_op jit(solution)/shard_map/ppermute | solution.py:142
  64.8 23.5 %collective-permute-start.2 = (bf16[512,256]{1,0:T(8,128)(2,1)}, bf16[512,256]{1,0:T(8,128)(2,1)}, u32[]{:S(2)}, u32[]{:S(2)}) collective-permute-start(bf16[512,256]{1,0:T(8,128)(2,1)} %bitcast.227), channel_id=1, source_target_pairs={{0,96},{32,0},{64,32},{96,64},{1,97},{33,1},{65,33},{97,65},{2,98}... | collective-permute-start | bytes 786440 | tf_op jit(solution)/shard_map/ppermute | solution.py:140
  68.3 11.6 %collective-permute-start.16 = (bf16[512,256]{1,0:T(8,128)(2,1)}, bf16[512,256]{1,0:T(8,128)(2,1)}, u32[]{:S(2)}, u32[]{:S(2)}) collective-permute-start(bf16[512,256]{1,0:T(8,128)(2,1)} %bitcast.228), channel_id=1, source_target_pairs={{0,96},{32,0},{64,32},{96,64},{1,97},{33,1},{65,33},{97,65},{2,98}... | collective-permute-start | bytes 786440 | tf_op jit(solution)/shard_map/ppermute | solution.py:140
  79.9 11.1 %collective-permute-start.24 = (bf16[512,256]{1,0:T(8,128)(2,1)}, bf16[512,256]{1,0:T(8,128)(2,1)S(1)}, u32[]{:S(2)}, u32[]{:S(2)}) collective-permute-start(bf16[512,256]{1,0:T(8,128)(2,1)} %collective-permute-done.16), channel_id=1, source_target_pairs={{0,96},{32,0},{64,32},{96,64},{1,97},{33,1},{65,33},{97,65},{2,98}... | collective-permute-start | bytes 786440 | tf_op jit(solution)/shard_map/ppermute | solution.py:144
  82.8 12.0 %collective-permute-start.17 = (bf16[512,256]{1,0:T(8,128)(2,1)}, bf16[512,256]{1,0:T(8,128)(2,1)}, u32[]{:S(2)}, u32[]{:S(2)}) collective-permute-start(bf16[512,256]{1,0:T(8,128)(2,1)} %collective-permute-done.16), channel_id=1, source_target_pairs={{0,16},{16,0},{1,17},{17,1},{2,18},{18,2},{3,19},{19,3},{4,20},{20... | collective-permute-start | bytes 786440 | tf_op jit(solution)/shard_map/ppermute | solution.py:133
  84.1 10.7 %collective-permute-start.19 = (bf16[512,256]{1,0:T(8,128)(2,1)}, bf16[512,256]{1,0:T(8,128)(2,1)}, u32[]{:S(2)}, u32[]{:S(2)}) collective-permute-start(bf16[512,256]{1,0:T(8,128)(2,1)} %collective-permute-done.18), channel_id=1, source_target_pairs={{0,32},{32,64},{64,96},{96,0},{1,33},{33,65},{65,97},{97,1},{2,34}... | collective-permute-start | bytes 786440 | tf_op jit(solution)/shard_map/ppermute | solution.py:142
  86.3 19.3 %collective-permute-start.21 = (bf16[1024,256]{1,0:T(8,128)(2,1)}, bf16[1024,256]{1,0:T(8,128)(2,1)S(1)}, u32[]{:S(2)}, u32[]{:S(2)}) collective-permute-start(bf16[1024,256]{1,0:T(8,128)(2,1)} %bitcast.224), channel_id=1, source_target_pairs={{0,32},{32,64},{64,96},{96,0},{1,33},{33,65},{65,97},{97,1},{2,34}... | collective-permute-start | bytes 1572872 | tf_op jit(solution)/shard_map/ppermute | solution.py:142
  88.3 14.3 %collective-permute-start.9 = (bf16[1024,256]{1,0:T(8,128)(2,1)S(1)}, bf16[1024,256]{1,0:T(8,128)(2,1)S(1)}, u32[]{:S(2)}, u32[]{:S(2)}) collective-permute-start(bf16[1024,256]{1,0:T(8,128)(2,1)S(1)} %bitcast.225), channel_id=1, source_target_pairs={{0,96},{32,0},{64,32},{96,64},{1,97},{33,1},{65,33},{97,65},{2,98}... | collective-permute-start | bytes 1572872 | tf_op jit(solution)/shard_map/ppermute | solution.py:140
  91.0 6.2 %collective-permute-start.3 = (bf16[512,256]{1,0:T(8,128)(2,1)}, bf16[512,256]{1,0:T(8,128)(2,1)S(1)}, u32[]{:S(2)}, u32[]{:S(2)}) collective-permute-start(bf16[512,256]{1,0:T(8,128)(2,1)} %collective-permute-done.2), channel_id=1, source_target_pairs={{0,16},{16,0},{1,17},{17,1},{2,18},{18,2},{3,19},{19,3},{4,20},{20... | collective-permute-start | bytes 786440 | tf_op jit(solution)/shard_map/ppermute | solution.py:133
  94.8 4.4 %collective-permute-start.20 = (bf16[512,256]{1,0:T(8,128)(2,1)}, bf16[512,256]{1,0:T(8,128)(2,1)S(1)}, u32[]{:S(2)}, u32[]{:S(2)}) collective-permute-start(bf16[512,256]{1,0:T(8,128)(2,1)} %collective-permute-done.19), channel_id=1, source_target_pairs={{0,16},{16,0},{1,17},{17,1},{2,18},{18,2},{3,19},{19,3},{4,20},{20... | collective-permute-start | bytes 786440 | tf_op jit(solution)/shard_map/ppermute | solution.py:133
  105.6 14.8 %collective-permute-start.22 = (bf16[1024,256]{1,0:T(8,128)(2,1)S(1)}, bf16[1024,256]{1,0:T(8,128)(2,1)S(1)}, u32[]{:S(2)}, u32[]{:S(2)}) collective-permute-start(bf16[1024,256]{1,0:T(8,128)(2,1)S(1)} %collective-permute-done.21), channel_id=1, source_target_pairs={{0,32},{32,64},{64,96},{96,0},{1,33},{33,65},{65,97},{97,1},{2,34}... | collective-permute-start | bytes 1572872 | tf_op jit(solution)/shard_map/ppermute | solution.py:142
  124.5 15.8 %collective-permute-start.26 = (f32[2,256,256]{2,1,0:T(8,128)S(1)}, f32[2,256,256]{2,1,0:T(8,128)S(1)}, u32[]{:S(2)}, u32[]{:S(2)}) collective-permute-start(f32[2,256,256]{2,1,0:T(8,128)S(1)} %get-tuple-element.21), channel_id=1, source_target_pairs={{0,4},{1,5},{2,6},{3,7},{16,20},{17,21},{18,22},{19,23},{32,36},{3... | collective-permute-start | bytes 1572872 | tf_op jit(solution)/shard_map/ppermute | solution.py:181
  127.4 18.7 %collective-permute-start.29 = (f32[2,256,256]{2,1,0:T(8,128)}, f32[2,256,256]{2,1,0:T(8,128)}, u32[]{:S(2)}, u32[]{:S(2)}) collective-permute-start(f32[2,256,256]{2,1,0:T(8,128)} %get-tuple-element.22), channel_id=1, source_target_pairs={{12,8},{13,9},{14,10},{15,11},{28,24},{29,25},{30,26},{31,27},{44,... | collective-permute-start | bytes 1572872 | tf_op jit(solution)/shard_map/ppermute | solution.py:182
  140.4 15.0 %collective-permute-start.27 = (f32[2,256,256]{2,1,0:T(8,128)S(1)}, f32[2,256,256]{2,1,0:T(8,128)S(1)}, u32[]{:S(2)}, u32[]{:S(2)}) collective-permute-start(f32[2,256,256]{2,1,0:T(8,128)S(1)} %bitcast_add_fusion.2), channel_id=1, source_target_pairs={{0,4},{4,8},{1,5},{5,9},{2,6},{6,10},{3,7},{7,11},{16,20},{20,24},... | collective-permute-start | bytes 1572872 | tf_op jit(solution)/shard_map/ppermute | solution.py:181
  157.6 14.4 %collective-permute-start.30 = (f32[2,256,256]{2,1,0:T(8,128)}, f32[2,256,256]{2,1,0:T(8,128)}, u32[]{:S(2)}, u32[]{:S(2)}) collective-permute-start(f32[2,256,256]{2,1,0:T(8,128)} %get-tuple-element.20), channel_id=1, source_target_pairs={{12,8},{8,4},{13,9},{9,5},{14,10},{10,6},{15,11},{11,7},{28,24},{2... | collective-permute-start | bytes 1572872 | tf_op jit(solution)/shard_map/ppermute | solution.py:182
  160.9 16.6 %collective-permute-start.28 = (f32[2,256,256]{2,1,0:T(8,128)}, f32[2,256,256]{2,1,0:T(8,128)S(1)}, u32[]{:S(2)}, u32[]{:S(2)}) collective-permute-start(f32[2,256,256]{2,1,0:T(8,128)} %get-tuple-element.19), channel_id=1, source_target_pairs={{0,4},{4,8},{8,12},{1,5},{5,9},{9,13},{2,6},{6,10},{10,14},{3,7},{... | collective-permute-start | bytes 1572872 | tf_op jit(solution)/shard_map/ppermute | solution.py:181
  173.1 13.3 %collective-permute-start.31 = (f32[2,256,256]{2,1,0:T(8,128)S(1)}, f32[2,256,256]{2,1,0:T(8,128)}, u32[]{:S(2)}, u32[]{:S(2)}) collective-permute-start(f32[2,256,256]{2,1,0:T(8,128)S(1)} %bitcast_add_fusion.1), channel_id=1, source_target_pairs={{12,8},{8,4},{4,0},{13,9},{9,5},{5,1},{14,10},{10,6},{6,2},{15,11}... | collective-permute-start | bytes 1572872 | tf_op jit(solution)/shard_map/ppermute | solution.py:182
  188.2 18.6 %collective-permute-start.33 = (f32[256,256]{0,1:T(8,128)S(1)}, f32[256,256]{0,1:T(8,128)S(1)}, u32[]{:S(2)}, u32[]{:S(2)}) collective-permute-start(f32[256,256]{0,1:T(8,128)S(1)} %copy.55), channel_id=1, source_target_pairs={{0,2},{4,4},{8,0},{12,130},{1,3},{5,1},{9,5},{13,131},{2,138},{6,1... | collective-permute-start | bytes 786440 | tf_op jit(solution)/shard_map/ppermute | solution.py:196
  191.4 15.8 %collective-permute-start.34 = (f32[256,256]{1,0:T(8,128)S(1)}, f32[256,256]{1,0:T(8,128)S(1)}, u32[]{:S(2)}, u32[]{:S(2)}) collective-permute-start(f32[256,256]{1,0:T(8,128)S(1)} %copy.63), channel_id=1, source_target_pairs={{0,2},{4,4},{8,8},{12,130},{1,3},{5,1},{9,5},{13,131},{2,138},{6,1... | collective-permute-start | bytes 786440 | tf_op jit(solution)/shard_map/ppermute | solution.py:196
  199.1 49.8 %collective-permute-start.35 = (f32[256,256]{0,1:T(8,128)}, f32[256,256]{0,1:T(8,128)S(1)}, u32[]{:S(2)}, u32[]{:S(2)}) collective-permute-start(f32[256,256]{0,1:T(8,128)} %get-tuple-element.38), channel_id=1, source_target_pairs={{0,32},{4,64},{12,40},{1,48},{5,16},{9,80},{13,56},{2,168},{6,200}... | collective-permute-start | bytes 786440 | tf_op jit(solution)/shard_map/ppermute | solution.py:196
  201.1 52.4 %collective-permute-start.32 = (f32[256,256]{0,1:T(8,128)}, f32[256,256]{0,1:T(8,128)S(1)}, u32[]{:S(2)}, u32[]{:S(2)}) collective-permute-start(f32[256,256]{0,1:T(8,128)} %get-tuple-element.65), channel_id=1, source_target_pairs={{0,32},{4,64},{8,128},{12,40},{1,48},{5,16},{9,80},{13,56},{2,168}... | collective-permute-start | bytes 786440 | tf_op jit(solution)/shard_map/ppermute | solution.py:196
  (19 other events, 73.2 us)

commit v3 on v2

v3 whole, which is shorter than its diff:
```python
import itertools

import jax
import jax.numpy as jnp
import numpy as np
from jax import lax
from jax.sharding import Mesh
from jax.sharding import PartitionSpec as P

AXES = ("zh", "y", "core", "zl", "x")
SIZES = (2, 4, 2, 4, 4)
BLOCKS = 4


def rcv_of(zh, y, core):
    return (zh * 4 + y) * 2 + core


def device_of(row, col):
    return row * 16 + col


def z_of(row, col):
    return (row // 8) * 4 + col // 4


def held_pair(f, y, core, x, block):
    e_col, core_col = x // 2, x % 2
    if block < 2:
        e_row, dy = block, 1
    elif block == 2:
        e_row, dy = (e_col if y < 2 else 1 - e_col), 2
    else:
        if core_col == core:
            return None
        e_row, dy = (e_col if core == 0 else 1 - e_col), 0
    return rcv_of(f ^ e_row, y, core), rcv_of(f ^ e_col, (y + dy) % 4, core_col)


def deliveries(f, y, core, x, block):
    pair = held_pair(f, y, core, x, block)
    if pair is not None:
        row, col = pair
        plain, flipped = device_of(row, col), device_of(col, row)
        first, second = (plain, flipped) if f == 0 else (flipped, plain)
        return [(0, first), (1, first), (2, second), (3, second)]
    e_col = x // 2
    r0, r1 = rcv_of(0, y, core), rcv_of(1, y, core)
    own = rcv_of(f ^ e_col, y, core)
    d01, d10 = device_of(r0, r1), device_of(r1, r0)
    diag = device_of(own, own)
    if f == 0:
        return [(0, diag), (1, d01 if e_col == 0 else d10), (2, d10 if e_col == 0 else d01)]
    return [(1, diag), (0, d01 if e_col == 0 else d10), (3, d10 if e_col == 0 else d01)]


ROOTS = (
    (0x1d8a8f5a5b6d8927, 0xa0a990abf59a70e5),
    (0xf76030e586f052f8, 0x570e254e2c438e5b),
    (0x6758c4619e2552b9, 0x79d69d67e05aa158),
    (0x55aa8b65a45a9866, 0x65dea759bb55aa11),
)


def root_of(block, f, y, core, x):
    return ROOTS[block][f] >> (2 * (31 - ((y * 2 + core) * 4 + x))) & 3


def places():
    return itertools.product(range(2), range(4), range(2), range(4))


def sum_perms(block):
    perms = [[], [], []]
    for f, y, core, x in places():
        root = root_of(block, f, y, core, x)
        target = device_of(rcv_of(f, y, core), root * 4 + x)
        for back in (1, 2, 3):
            perms[back - 1].append((device_of(rcv_of(f, y, core), (root - back) % 4 * 4 + x), target))
    return perms


def owner_perms(block):
    perms = [[], [], [], []]
    for f, y, core, x in places():
        source = device_of(rcv_of(f, y, core), root_of(block, f, y, core, x) * 4 + x)
        for slot, target in deliveries(f, y, core, x, block):
            perms[slot].append((source, target))
    for perm in perms:
        assert len({s for s, _ in perm}) == len(perm) == len({t for _, t in perm})
    return perms


def owner_cases():
    case = np.zeros((16, 16), np.int32)
    for f, y, core, x in places():
        for block in range(BLOCKS):
            pair = held_pair(f, y, core, x, block)
            if pair is not None and f == 0:
                case[pair] = 1
    for y, core in itertools.product(range(4), range(2)):
        r0, r1 = rcv_of(0, y, core), rcv_of(1, y, core)
        case[r0, r0] = case[r1, r1] = 2
        case[r0, r1], case[r1, r0] = 3, 4
    return case


def ring(n, step):
    return [(i, (i + step) % n) for i in range(n)]


def gather_x(block):
    half = block.shape[1] // 2
    above = lax.ppermute(block, "x", ring(4, -1))
    below = lax.ppermute(block, "x", ring(4, 1))
    far_a = lax.ppermute(above[:, :half], "x", ring(4, -1))
    far_b = lax.ppermute(below[:, half:], "x", ring(4, 1))
    return block, jnp.concatenate([above, below], axis=1), jnp.concatenate([far_a, far_b], axis=1)


def with_turned(real, imag):
    return jnp.stack([jnp.concatenate([real, imag], axis=1), jnp.concatenate([imag, -real], axis=1)])


def first_of(value, *after):
    return lax.optimization_barrier((value, *after))[0] if after else value


def product(rows, cols):
    return jnp.einsum("psm,psn->mn", rows, cols, preferred_element_type=jnp.float32)


def body(wavefield):
    case_of = owner_cases()
    f, y, core, zl, x = (lax.axis_index(name) for name in AXES)
    n = wavefield.shape[3]
    shots = wavefield.shape[2] * 16
    scale = 1.0 / jnp.sqrt(jnp.float32(shots))

    own = lax.dynamic_index_in_dim(wavefield, f, 0, keepdims=False)
    other = lax.dynamic_index_in_dim(wavefield, 1 - f, 0, keepdims=False)
    other = lax.ppermute(other, "zh", ring(2, 1))
    group0, group1 = gather_x(own), gather_x(other)

    e_col, core_col = x // 2, x % 2
    same = core_col == core
    one_way = [(a * 4 + b, (1 - a) * 4 + b) for a in range(2) for b in range(4) if b % 2 == a]
    cols0, part = [], []
    for block0, block1 in zip(group0, group1):
        mine = jnp.where(e_col == 0, block0, block1)
        cols0.append(jnp.where(same, mine, lax.ppermute(mine, ("core", "x"), one_way)))
        part.append(lax.dynamic_index_in_dim(cols0[-1], core, 0, keepdims=False))

    def from_y(step, value, *after):
        return lax.ppermute(first_of(value, *after), "y", ring(4, -step))

    near, far = [None] * 3, [None] * 3
    near[0], far[0] = from_y(1, part[0]), from_y(2, part[0])
    near[1] = from_y(1, part[1], near[0], far[0])
    near[2] = from_y(1, part[2], near[1])
    far[1] = from_y(2, part[1], near[1])
    far[2] = from_y(2, part[2], near[2], far[1])

    def on_both(mine):
        other = lax.ppermute(mine, "core", ring(2, 1))
        return with_turned(jnp.where(core == 0, mine, other), jnp.where(core == 0, other, mine))

    rows = [jnp.concatenate(blocks, axis=2) for blocks in zip(group0, group1)]
    e_row2 = jnp.where(y < 2, e_col, 1 - e_col)
    rows2 = [jnp.where(e_row2 == 0, block0, block1) for block0, block1 in zip(group0, group1)]

    def parts_of(a):
        return jnp.stack([a[:, :n], a[:, n:]])

    product0 = sum(product(r, with_turned(c[0], c[1])) for r, c in zip(rows, cols0))
    e_row0 = jnp.where(same, 1 - e_col, jnp.where(core == 0, e_col, 1 - e_col))
    upper = lax.broadcasted_iota(jnp.int32, (n, n), 0) <= lax.broadcasted_iota(jnp.int32, (n, n), 1)
    diag = lax.dynamic_slice_in_dim(product0, e_col * n, n, 0)
    off = lax.dynamic_slice_in_dim(product0, e_row0 * n, n, 0)
    packed = jnp.where(upper, diag[:, :n], diag[:, n:])
    block3 = jnp.stack(
        [
            jnp.where(same, packed, off[:, :n]),
            jnp.where(same & (e_col == 0), off[:, :n], off[:, n:]),
        ]
    )

    def summed(block, number):
        return sum((lax.ppermute(block, AXES, perm) for perm in sum_perms(number)), block) * scale

    held3 = summed(block3, 3)
    product1 = sum(product(r, on_both(c)) for r, c in zip(rows, near))
    held0, held1 = summed(parts_of(product1[:n]), 0), summed(parts_of(product1[n:]), 1)
    cols2 = [on_both(c) for c in far]
    cols2[2] = first_of(cols2[2], held3)
    block2 = parts_of(sum(product(r, c) for r, c in zip(rows2, cols2)))
    held2 = summed(first_of(block2, held0, held1), 2)

    is0 = f == 0

    def turned(block):
        return jnp.stack([block[0].T, -block[1].T])

    firsts, seconds = [], []
    for number, held in ((0, held0), (1, held1), (2, held2)):
        perms = owner_perms(number)
        assert perms[0] == perms[1] and perms[2] == perms[3]
        firsts.append(lax.ppermute(jnp.where(is0, held, turned(held)), AXES, perms[0]))
        seconds.append(lax.ppermute(jnp.where(is0, turned(held), held), AXES, perms[2]))
    plain_a, plain_b = held3[0], held3[1]
    turned_a, turned_b = held3[0].T, -held3[1].T
    other_turned = jnp.where(e_col == 0, held3[1].T, turned_b)
    send = [
        jnp.where(is0, plain_a, jnp.where(same, plain_b, turned_a)),
        jnp.where(is0, jnp.where(same, other_turned, plain_b), jnp.where(same, plain_a, turned_b)),
        jnp.where(is0, jnp.where(same, plain_b, turned_a), plain_a),
        jnp.where(is0, turned_b, jnp.where(same, other_turned, plain_b)),
    ]
    last = [lax.ppermute(s, AXES, perm) for s, perm in zip(send, owner_perms(3))]
    first, second = sum(firsts), sum(seconds)
    got = [first[0] + last[0], first[1] + last[1], second[0] + last[2], second[1] + last[3]]

    case = jnp.asarray(case_of)[rcv_of(f, y, core), zl * 4 + x]

    def unpack(packed):
        strict = lax.broadcasted_iota(jnp.int32, (n, n), 0) < lax.broadcasted_iota(jnp.int32, (n, n), 1)
        top, low = jnp.where(upper, packed, 0.0), jnp.where(upper, 0.0, packed)
        return top + jnp.where(strict, packed, 0.0).T, low - low.T

    real_d0, imag_d0 = unpack(got[0])
    real_d1, imag_d1 = unpack(got[1])

    def pick(plain, flipped, diag, d01, d10):
        return jnp.where(
            case == 0, flipped, jnp.where(case == 1, plain, jnp.where(case == 2, diag, jnp.where(case == 3, d01, d10)))
        )

    a1, b1, a2, b2 = got
    return jnp.stack(
        [
            jnp.stack([pick(a1, a2, real_d0, b1, a2), pick(b1, b2, imag_d0, a2, b1)]),
            jnp.stack([pick(a2, a1, real_d1, a1, b2), pick(b2, b1, imag_d1, b2, a1)]),
        ]
    )


def solution(mesh):
    fine = Mesh(mesh.devices.reshape(SIZES), AXES)
    return jax.shard_map(
        body,
        mesh=fine,
        in_specs=(P(None, None, ("zl", "x"), ("zh", "y", "core")),),
        out_specs=P(None, None, ("zh", "y", "core"), ("zl", "x")),
        check_vma=False,
    )
```

time: 257 us -> 270 us (1.051)
  the two profiles are of different devices: /device:TPU:34 before, /device:TPU:163 now
where the time goes in v3:
time: 270 us; the launch traced here: 269 us
  starting transfers between devices  121 us (45%)
  waiting for transfers between devices  85.2 us (32%)
  other arithmetic  25.8 us (10%)
  local copies, waits for them, and re-layouts  23.7 us (9%)
  matrix products  9.29 us (3%)
  between operations  3.82 us (1%)
    ppermute x4, starting transfers between devices, body(): lax.ppermute(s, AXES, perm)  42.8 us
    ppermute x12, starting transfers between devices, summed(): lax.ppermute(block, AXES, perm)  20.7 us
    ppermute x12, waiting for transfers between devices, summed(): lax.ppermute(block, AXES, perm)  18.3 us
    ppermute x6, starting transfers between devices, on_both(): other = lax.ppermute(mine, 'core', ring(2, 1))  17.2 us
    ppermute x2, waiting for transfers between devices, gather_x(): above = lax.ppermute(block, 'x', ring(4, -1))  16 us
    ppermute x1, waiting for transfers between devices, body(): other = lax.ppermute(other, 'zh', ring(2, 1))  14.7 us
    ppermute x3, waiting for transfers between devices, body(): lax.ppermute(jnp.where(is0, turned(held), held), AXES, perms[2])  14.6 us
    ppermute x6, waiting for transfers between devices, from_y(): return lax.ppermute(first_of(value, *after), 'y', ring(4, -step))  13.7 us
  transfers between devices with their start and end apart: 46, of which 14 were waited for; matrix products, arithmetic and copies ran while one was open for 18% of the time, Pallas kernels for 0%

profile of v3, /device:TPU:163, one launch (start us, length us, event | category | flops | bytes accessed | tf_op | source)
XLA Modules:
  0.0 268.8 jit_solution(14887641459562143997)
XLA Ops:
  3.4 10.9 %collective-permute-done.4 = bf16[2,512,256]{1,2,0:T(8,128)(2,1)S(1)} collective-permute-done((bf16[2,512,256]{1,2,0:T(8,128)(2,1)S(1)}, bf16[2,512,256]{1,2,0:T(8,128)(2,1)S(1)}, u32[]{:S(2)}, u32[]{:S(2)}) %collective-permute-start.4) | collective-permute-done | bytes 524320 | tf_op jit(solution)/shard_map/ppermute | solution.py:114
  16.0 14.7 %collective-permute-done = bf16[2,512,256]{1,2,0:T(8,128)(2,1)S(1)} collective-permute-done((bf16[2,512,256]{1,2,0:T(8,128)(2,1)S(1)}, bf16[2,512,256]{1,2,0:T(8,128)(2,1)S(1)}, u32[]{:S(2)}, u32[]{:S(2)}) %collective-permute-start) | collective-permute-done | bytes 524320 | tf_op jit(solution)/shard_map/ppermute | solution.py:142
  30.7 1.5 collective-permute-start.6
  32.3 4.5 %collective-permute-start.1 = (bf16[2,512,256]{1,2,0:T(8,128)(2,1)S(1)}, bf16[2,512,256]{1,2,0:T(8,128)(2,1)S(1)}, u32[]{:S(2)}, u32[]{:S(2)}) collective-permute-start(bf16[2,512,256]{1,2,0:T(8,128)(2,1)S(1)} %broadcast_select_fusion.7), channel_id=1, source_target_pairs={{0,16},{2,18},{17,1},{19,3},{4,20},{6,22},{21,5},{23,7},{8,24},{10... | collective-permute-start | bytes 1572872 | tf_op jit(solution)/shard_map/ppermute | solution.py:151
  37.0 5.0 %collective-permute-done.6 = bf16[2,512,256]{1,2,0:T(8,128)(2,1)S(1)} collective-permute-done((bf16[2,512,256]{1,2,0:T(8,128)(2,1)S(1)}, bf16[2,512,256]{1,2,0:T(8,128)(2,1)S(1)}, u32[]{:S(2)}, u32[]{:S(2)}) %collective-permute-start.6) | collective-permute-done | bytes 524320 | tf_op jit(solution)/shard_map/ppermute | solution.py:114
  42.1 1.9 collective-permute-start.14
  44.8 3.3 %collective-permute-done.14 = bf16[2,256,256]{1,2,0:T(8,128)(2,1)S(1)} collective-permute-done((bf16[2,256,256]{1,2,0:T(8,128)(2,1)S(1)}, bf16[2,256,256]{1,2,0:T(8,128)(2,1)S(1)}, u32[]{:S(2)}, u32[]{:S(2)}) %collective-permute-start.14) | collective-permute-done | bytes 262176 | tf_op jit(solution)/shard_map/ppermute | solution.py:116
  48.1 3.2 %collective-permute-done.15 = bf16[2,256,256]{1,2,0:T(8,128)(2,1)S(1)} collective-permute-done((bf16[2,256,256]{1,2,0:T(8,128)(2,1)S(1)}, bf16[2,256,256]{1,2,0:T(8,128)(2,1)S(1)}, u32[]{:S(2)}, u32[]{:S(2)}) %collective-permute-start.15) | collective-permute-done | bytes 262176 | tf_op jit(solution)/shard_map/ppermute | solution.py:117
  51.4 6.0 %collective-permute-start.16 = (bf16[2,512,256]{1,2,0:T(8,128)(2,1)S(1)}, bf16[2,512,256]{1,2,0:T(8,128)(2,1)S(1)}, u32[]{:S(2)}, u32[]{:S(2)}) collective-permute-start(bf16[2,512,256]{1,2,0:T(8,128)(2,1)S(1)} %broadcast_select_fusion.6), channel_id=1, source_target_pairs={{0,16},{2,18},{17,1},{19,3},{4,20},{6,22},{21,5},{23,7},{8,24},{10... | collective-permute-start | bytes 1572872 | tf_op jit(solution)/shard_map/ppermute | solution.py:151
  57.5 2.3 collective-permute-start.8
  61.2 1.8 copy.72
  63.0 2.7 %collective-permute-start.2 = (bf16[512,256]{1,0:T(8,128)(2,1)}, bf16[512,256]{1,0:T(8,128)(2,1)}, u32[]{:S(2)}, u32[]{:S(2)}) collective-permute-start(bf16[512,256]{1,0:T(8,128)(2,1)} %bitcast.232), channel_id=1, source_target_pairs={{0,96},{32,0},{64,32},{96,64},{1,97},{33,1},{65,33},{97,65},{2,98}... | collective-permute-start | bytes 786440 | tf_op jit(solution)/shard_map/ppermute | solution.py:155
  66.1 1.8 copy.74
  72.2 3.6 %collective-permute-done.9 = bf16[512,256]{1,0:T(8,128)(2,1)} collective-permute-done((bf16[512,256]{1,0:T(8,128)(2,1)}, bf16[512,256]{1,0:T(8,128)(2,1)}, u32[]{:S(2)}, u32[]{:S(2)}) %collective-permute-start.9) | collective-permute-done | bytes 262176 | tf_op jit(solution)/shard_map/ppermute | solution.py:155
  83.6 3.4 %collective-permute-start.10 = (bf16[1024,256]{1,0:T(8,128)(2,1)}, bf16[1024,256]{1,0:T(8,128)(2,1)}, u32[]{:S(2)}, u32[]{:S(2)}) collective-permute-start(bf16[1024,256]{1,0:T(8,128)(2,1)} %bitcast.7), channel_id=1, source_target_pairs={{0,96},{32,0},{64,32},{96,64},{1,97},{33,1},{65,33},{97,65},{2,98}... | collective-permute-start | bytes 1572872 | tf_op jit(solution)/shard_map/ppermute | solution.py:155
  89.2 6.9 %collective-permute-done.10 = bf16[1024,256]{1,0:T(8,128)(2,1)} collective-permute-done((bf16[1024,256]{1,0:T(8,128)(2,1)}, bf16[1024,256]{1,0:T(8,128)(2,1)}, u32[]{:S(2)}, u32[]{:S(2)}) %collective-permute-start.10) | collective-permute-done | bytes 524320 | tf_op jit(solution)/shard_map/ppermute | solution.py:155
  96.1 2.5 collective-permute-start.17
  98.6 1.7 convolution_bitcast_fusion.3
  102.1 5.7 %collective-permute-start.11 = (bf16[1024,256]{1,0:T(8,128)(2,1)}, bf16[1024,256]{1,0:T(8,128)(2,1)}, u32[]{:S(2)}, u32[]{:S(2)}) collective-permute-start(bf16[1024,256]{1,0:T(8,128)(2,1)} %collective-permute-done.10), channel_id=1, source_target_pairs={{0,16},{16,0},{1,17},{17,1},{2,18},{18,2},{3,19},{19,3},{4,20},{20... | collective-permute-start | bytes 1572872 | tf_op jit(solution)/shard_map/ppermute | solution.py:165
  107.9 9.7 %collective-permute-start.18 = (bf16[512,256]{1,0:T(8,128)(2,1)S(1)}, bf16[512,256]{1,0:T(8,128)(2,1)}, u32[]{:S(2)}, u32[]{:S(2)}) collective-permute-start(bf16[512,256]{1,0:T(8,128)(2,1)S(1)} %collective-permute-done.17), channel_id=1, source_target_pairs={{0,16},{16,0},{1,17},{17,1},{2,18},{18,2},{3,19},{19,3},{4,20},{20... | collective-permute-start | bytes 786440 | tf_op jit(solution)/shard_map/ppermute | solution.py:165
  117.6 1.5 add_multiply_fusion.1
  122.1 1.8 collective-permute-start.30
  128.4 3.2 %collective-permute-done.30 = bf16[512,256]{1,0:T(8,128)(2,1)} collective-permute-done((bf16[512,256]{1,0:T(8,128)(2,1)S(1)}, bf16[512,256]{1,0:T(8,128)(2,1)}, u32[]{:S(2)}, u32[]{:S(2)}) %collective-permute-start.30) | collective-permute-done | bytes 262176 | tf_op jit(solution)/shard_map/ppermute | solution.py:155
  134.4 7.6 %collective-permute-start.19 = (f32[2,256,256]{1,2,0:T(8,128)S(1)}, f32[2,256,256]{1,2,0:T(8,128)S(1)}, u32[]{:S(2)}, u32[]{:S(2)}) collective-permute-start(f32[2,256,256]{1,2,0:T(8,128)S(1)} %pad_maximum_fusion.15), channel_id=1, source_target_pairs={{12,0},{1,5},{10,14},{3,7},{20,24},{29,17},{22,26},{23,27},{36,40}... | collective-permute-start | bytes 1572872 | tf_op jit(solution)/shard_map/ppermute | solution.py:189
  142.1 2.5 collective-permute-start.25
  151.1 13.4 %collective-permute-done.19 = f32[2,256,256]{1,2,0:T(8,128)S(1)} collective-permute-done((f32[2,256,256]{1,2,0:T(8,128)S(1)}, f32[2,256,256]{1,2,0:T(8,128)S(1)}, u32[]{:S(2)}, u32[]{:S(2)}) %collective-permute-start.19) | collective-permute-done | bytes 524320 | tf_op jit(solution)/shard_map/ppermute | solution.py:189
  177.8 4.9 %collective-permute-done.37 = f32[2,256,256]{1,2,0:T(8,128)} collective-permute-done((f32[2,256,256]{1,2,0:T(8,128)S(1)}, f32[2,256,256]{1,2,0:T(8,128)}, u32[]{:S(2)}, u32[]{:S(2)}) %collective-permute-start.37) | collective-permute-done | bytes 524320 | tf_op jit(solution)/shard_map/ppermute | solution.py:189
  185.5 2.0 collective-permute-start.42
  188.4 3.6 %collective-permute-start.45 = (f32[256,256]{0,1:T(8,128)}, f32[256,256]{0,1:T(8,128)S(1)}, u32[]{:S(2)}, u32[]{:S(2)}) collective-permute-start(f32[256,256]{0,1:T(8,128)} %get-tuple-element.54), channel_id=1, source_target_pairs={{5,16},{7,152},{24,9},{26,129},{33,50},{47,186},{52,43},{54,163},{... | collective-permute-start | bytes 786440 | tf_op jit(solution)/shard_map/ppermute | solution.py:219
  199.1 36.5 %collective-permute-start.43 = (f32[256,256]{1,0:T(8,128)}, f32[256,256]{1,0:T(8,128)}, u32[]{:S(2)}, u32[]{:S(2)}) collective-permute-start(f32[256,256]{1,0:T(8,128)} %get-tuple-element.33), channel_id=1, source_target_pairs={{4,0},{5,1},{6,136},{7,137},{24,144},{25,17},{26,24},{27,153},{40,... | collective-permute-start | bytes 786440 | tf_op jit(solution)/shard_map/ppermute | solution.py:219
  244.5 1.9 collective-permute-start.38
  248.9 14.6 %collective-permute-done.38 = f32[2,256,256]{1,2,0:T(8,128)} collective-permute-done((f32[2,256,256]{1,2,0:T(8,128)}, f32[2,256,256]{1,2,0:T(8,128)}, u32[]{:S(2)}, u32[]{:S(2)}) %collective-permute-start.38) | collective-permute-done | bytes 524320 | tf_op jit(solution)/shard_map/ppermute | solution.py:209
  (231 shorter events, 78.0 us)
Async XLA Ops:
  1.5 12.9 %collective-permute-start.4 = (bf16[2,512,256]{1,2,0:T(8,128)(2,1)S(1)}, bf16[2,512,256]{1,2,0:T(8,128)(2,1)S(1)}, u32[]{:S(2)}, u32[]{:S(2)}) collective-permute-start(bf16[2,512,256]{1,2,0:T(8,128)(2,1)S(1)} %bitcast.224), channel_id=1, source_target_pairs={{0,3},{1,0},{2,1},{3,2},{4,7},{5,4},{6,5},{7,6},{8,11},{9,8},{10,9... | collective-permute-start | bytes 1572872 | tf_op jit(solution)/shard_map/ppermute | solution.py:114
  1.8 13.8 %collective-permute-start.5 = (bf16[2,512,256]{1,2,0:T(8,128)(2,1)S(1)}, bf16[2,512,256]{1,2,0:T(8,128)(2,1)S(1)}, u32[]{:S(2)}, u32[]{:S(2)}) collective-permute-start(bf16[2,512,256]{1,2,0:T(8,128)(2,1)S(1)} %bitcast.225), channel_id=1, source_target_pairs={{0,1},{1,2},{2,3},{3,0},{4,5},{5,6},{6,7},{7,4},{8,9},{9,10},{10,1... | collective-permute-start | bytes 1572872 | tf_op jit(solution)/shard_map/ppermute | solution.py:115
  3.2 27.5 %collective-permute-start = (bf16[2,512,256]{1,2,0:T(8,128)(2,1)S(1)}, bf16[2,512,256]{1,2,0:T(8,128)(2,1)S(1)}, u32[]{:S(2)}, u32[]{:S(2)}) collective-permute-start(bf16[2,512,256]{1,2,0:T(8,128)(2,1)S(1)} %bitcast.229), channel_id=1, source_target_pairs={{0,128},{128,0},{1,129},{129,1},{2,130},{130,2},{3,131},{131,3},{4... | collective-permute-start | bytes 1572872 | tf_op jit(solution)/shard_map/ppermute | solution.py:142
  14.4 22.6 %collective-permute-start.12 = (bf16[2,256,256]{1,2,0:T(8,128)(2,1)S(1)}, bf16[2,256,256]{1,2,0:T(8,128)(2,1)S(1)}, u32[]{:S(2)}, u32[]{:S(2)}) collective-permute-start(bf16[2,256,256]{1,2,0:T(8,128)(2,1)S(1)} %slice.144), channel_id=1, source_target_pairs={{0,3},{1,0},{2,1},{3,2},{4,7},{5,4},{6,5},{7,6},{8,11},{9,8},{10,9... | collective-permute-start | bytes 786440 | tf_op jit(solution)/shard_map/ppermute | solution.py:116
  15.6 28.3 %collective-permute-start.13 = (bf16[2,256,256]{1,2,0:T(8,128)(2,1)S(1)}, bf16[2,256,256]{1,2,0:T(8,128)(2,1)S(1)}, u32[]{:S(2)}, u32[]{:S(2)}) collective-permute-start(bf16[2,256,256]{1,2,0:T(8,128)(2,1)S(1)} %slice.145), channel_id=1, source_target_pairs={{0,1},{1,2},{2,3},{3,0},{4,5},{5,6},{6,7},{7,4},{8,9},{9,10},{10,1... | collective-permute-start | bytes 786440 | tf_op jit(solution)/shard_map/ppermute | solution.py:117
  32.3 12.3 %collective-permute-start.7 = (bf16[2,512,256]{1,2,0:T(8,128)(2,1)S(1)}, bf16[2,512,256]{1,2,0:T(8,128)(2,1)S(1)}, u32[]{:S(2)}, u32[]{:S(2)}) collective-permute-start(bf16[2,512,256]{1,2,0:T(8,128)(2,1)S(1)} %collective-permute-done), channel_id=1, source_target_pairs={{0,1},{1,2},{2,3},{3,0},{4,5},{5,6},{6,7},{7,4},{8,9},{9,10},{10,1... | collective-permute-start | bytes 1572872 | tf_op jit(solution)/shard_map/ppermute | solution.py:115
  32.3 27.5 %collective-permute-start.1 = (bf16[2,512,256]{1,2,0:T(8,128)(2,1)S(1)}, bf16[2,512,256]{1,2,0:T(8,128)(2,1)S(1)}, u32[]{:S(2)}, u32[]{:S(2)}) collective-permute-start(bf16[2,512,256]{1,2,0:T(8,128)(2,1)S(1)} %broadcast_select_fusion.7), channel_id=1, source_target_pairs={{0,16},{2,18},{17,1},{19,3},{4,20},{6,22},{21,5},{23,7},{8,24},{10... | collective-permute-start | bytes 1572872 | tf_op jit(solution)/shard_map/ppermute | solution.py:151
  57.5 14.1 %collective-permute-start.8 = (bf16[2,1024,256]{1,2,0:T(8,128)(2,1)S(1)}, bf16[2,1024,256]{1,2,0:T(8,128)(2,1)}, u32[]{:S(2)}, u32[]{:S(2)}) collective-permute-start(bf16[2,1024,256]{1,2,0:T(8,128)(2,1)S(1)} %broadcast_select_fusion), channel_id=1, source_target_pairs={{0,16},{2,18},{17,1},{19,3},{4,20},{6,22},{21,5},{23,7},{8,24},{10... | collective-permute-start | bytes 3145736 | tf_op jit(solution)/shard_map/ppermute | solution.py:151
  63.0 14.6 %collective-permute-start.2 = (bf16[512,256]{1,0:T(8,128)(2,1)}, bf16[512,256]{1,0:T(8,128)(2,1)}, u32[]{:S(2)}, u32[]{:S(2)}) collective-permute-start(bf16[512,256]{1,0:T(8,128)(2,1)} %bitcast.232), channel_id=1, source_target_pairs={{0,96},{32,0},{64,32},{96,64},{1,97},{33,1},{65,33},{97,65},{2,98}... | collective-permute-start | bytes 786440 | tf_op jit(solution)/shard_map/ppermute | solution.py:155
  78.7 23.5 %collective-permute-start.34 = (f32[2,256,256]{1,2,0:T(8,128)}, f32[2,256,256]{1,2,0:T(8,128)}, u32[]{:S(2)}, u32[]{:S(2)}) collective-permute-start(f32[2,256,256]{1,2,0:T(8,128)} %pad_maximum_fusion.19), channel_id=1, source_target_pairs={{8,4},{9,5},{10,6},{11,7},{28,24},{29,25},{30,26},{31,27},{44,40},... | collective-permute-start | bytes 1572872 | tf_op jit(solution)/shard_map/ppermute | solution.py:189
  79.9 37.6 %collective-permute-start.33 = (f32[2,256,256]{1,2,0:T(8,128)}, f32[2,256,256]{1,2,0:T(8,128)}, u32[]{:S(2)}, u32[]{:S(2)}) collective-permute-start(f32[2,256,256]{1,2,0:T(8,128)} %pad_maximum_fusion.19), channel_id=1, source_target_pairs={{12,4},{13,5},{14,6},{15,7},{16,24},{17,25},{18,26},{19,27},{32,40... | collective-permute-start | bytes 1572872 | tf_op jit(solution)/shard_map/ppermute | solution.py:189
  81.2 36.4 %collective-permute-start.32 = (f32[2,256,256]{1,2,0:T(8,128)}, f32[2,256,256]{1,2,0:T(8,128)}, u32[]{:S(2)}, u32[]{:S(2)}) collective-permute-start(f32[2,256,256]{1,2,0:T(8,128)} %pad_maximum_fusion.19), channel_id=1, source_target_pairs={{0,4},{1,5},{2,6},{3,7},{20,24},{21,25},{22,26},{23,27},{36,40},{4... | collective-permute-start | bytes 1572872 | tf_op jit(solution)/shard_map/ppermute | solution.py:189
  83.6 12.5 %collective-permute-start.10 = (bf16[1024,256]{1,0:T(8,128)(2,1)}, bf16[1024,256]{1,0:T(8,128)(2,1)}, u32[]{:S(2)}, u32[]{:S(2)}) collective-permute-start(bf16[1024,256]{1,0:T(8,128)(2,1)} %bitcast.7), channel_id=1, source_target_pairs={{0,96},{32,0},{64,32},{96,64},{1,97},{33,1},{65,33},{97,65},{2,98}... | collective-permute-start | bytes 1572872 | tf_op jit(solution)/shard_map/ppermute | solution.py:155
  101.6 20.3 %collective-permute-start.28 = (bf16[1024,256]{1,0:T(8,128)(2,1)}, bf16[1024,256]{1,0:T(8,128)(2,1)S(1)}, u32[]{:S(2)}, u32[]{:S(2)}) collective-permute-start(bf16[1024,256]{1,0:T(8,128)(2,1)} %bitcast.7), channel_id=1, source_target_pairs={{0,64},{32,96},{64,0},{96,32},{1,65},{33,97},{65,1},{97,33},{2,66}... | collective-permute-start | bytes 1572872 | tf_op jit(solution)/shard_map/ppermute | solution.py:155
  102.1 21.8 %collective-permute-start.11 = (bf16[1024,256]{1,0:T(8,128)(2,1)}, bf16[1024,256]{1,0:T(8,128)(2,1)}, u32[]{:S(2)}, u32[]{:S(2)}) collective-permute-start(bf16[1024,256]{1,0:T(8,128)(2,1)} %collective-permute-done.10), channel_id=1, source_target_pairs={{0,16},{16,0},{1,17},{17,1},{2,18},{18,2},{3,19},{19,3},{4,20},{20... | collective-permute-start | bytes 1572872 | tf_op jit(solution)/shard_map/ppermute | solution.py:165
  131.6 13.0 %collective-permute-start.31 = (bf16[512,256]{1,0:T(8,128)(2,1)}, bf16[512,256]{1,0:T(8,128)(2,1)S(1)}, u32[]{:S(2)}, u32[]{:S(2)}) collective-permute-start(bf16[512,256]{1,0:T(8,128)(2,1)} %collective-permute-done.30), channel_id=1, source_target_pairs={{0,16},{16,0},{1,17},{17,1},{2,18},{18,2},{3,19},{19,3},{4,20},{20... | collective-permute-start | bytes 786440 | tf_op jit(solution)/shard_map/ppermute | solution.py:165
  132.9 17.4 %collective-permute-start.21 = (f32[2,256,256]{1,2,0:T(8,128)S(1)}, f32[2,256,256]{1,2,0:T(8,128)S(1)}, u32[]{:S(2)}, u32[]{:S(2)}) collective-permute-start(f32[2,256,256]{1,2,0:T(8,128)S(1)} %pad_maximum_fusion.15), channel_id=1, source_target_pairs={{4,0},{9,5},{2,14},{11,7},{28,24},{21,17},{30,26},{31,27},{44,40},... | collective-permute-start | bytes 1572872 | tf_op jit(solution)/shard_map/ppermute | solution.py:189
  133.7 17.4 %collective-permute-start.20 = (f32[2,256,256]{1,2,0:T(8,128)S(1)}, f32[2,256,256]{1,2,0:T(8,128)S(1)}, u32[]{:S(2)}, u32[]{:S(2)}) collective-permute-start(f32[2,256,256]{1,2,0:T(8,128)S(1)} %pad_maximum_fusion.15), channel_id=1, source_target_pairs={{8,0},{13,5},{6,14},{15,7},{16,24},{25,17},{18,26},{19,27},{32,40}... | collective-permute-start | bytes 1572872 | tf_op jit(solution)/shard_map/ppermute | solution.py:189
  134.4 30.1 %collective-permute-start.19 = (f32[2,256,256]{1,2,0:T(8,128)S(1)}, f32[2,256,256]{1,2,0:T(8,128)S(1)}, u32[]{:S(2)}, u32[]{:S(2)}) collective-permute-start(f32[2,256,256]{1,2,0:T(8,128)S(1)} %pad_maximum_fusion.15), channel_id=1, source_target_pairs={{12,0},{1,5},{10,14},{3,7},{20,24},{29,17},{22,26},{23,27},{36,40}... | collective-permute-start | bytes 1572872 | tf_op jit(solution)/shard_map/ppermute | solution.py:189
  142.1 22.6 %collective-permute-start.25 = (f32[2,256,256]{2,1,0:T(8,128)S(1)}, f32[2,256,256]{2,1,0:T(8,128)S(1)}, u32[]{:S(2)}, u32[]{:S(2)}) collective-permute-start(f32[2,256,256]{2,1,0:T(8,128)S(1)} %pad_maximum_fusion.17), channel_id=1, source_target_pairs={{0,12},{1,13},{10,6},{3,15},{24,20},{29,25},{22,18},{23,19},{36,32... | collective-permute-start | bytes 1572872 | tf_op jit(solution)/shard_map/ppermute | solution.py:189
  146.8 17.8 %collective-permute-start.24 = (f32[2,256,256]{2,1,0:T(8,128)S(1)}, f32[2,256,256]{2,1,0:T(8,128)S(1)}, u32[]{:S(2)}, u32[]{:S(2)}) collective-permute-start(f32[2,256,256]{2,1,0:T(8,128)S(1)} %pad_maximum_fusion.17), channel_id=1, source_target_pairs={{4,12},{5,13},{14,6},{7,15},{28,20},{17,25},{26,18},{27,19},{40,32... | collective-permute-start | bytes 1572872 | tf_op jit(solution)/shard_map/ppermute | solution.py:189
  150.3 14.4 %collective-permute-start.23 = (f32[2,256,256]{2,1,0:T(8,128)S(1)}, f32[2,256,256]{2,1,0:T(8,128)S(1)}, u32[]{:S(2)}, u32[]{:S(2)}) collective-permute-start(f32[2,256,256]{2,1,0:T(8,128)S(1)} %pad_maximum_fusion.17), channel_id=1, source_target_pairs={{8,12},{9,13},{2,6},{11,15},{16,20},{21,25},{30,18},{31,19},{44,32... | collective-permute-start | bytes 1572872 | tf_op jit(solution)/shard_map/ppermute | solution.py:189
  164.9 17.8 %collective-permute-start.37 = (f32[2,256,256]{1,2,0:T(8,128)S(1)}, f32[2,256,256]{1,2,0:T(8,128)}, u32[]{:S(2)}, u32[]{:S(2)}) collective-permute-start(f32[2,256,256]{1,2,0:T(8,128)S(1)} %pad_maximum_fusion.20), channel_id=1, source_target_pairs={{8,4},{13,9},{10,6},{3,15},{24,20},{25,21},{30,26},{23,19},{32,44}... | collective-permute-start | bytes 1572872 | tf_op jit(solution)/shard_map/ppermute | solution.py:189
  166.2 16.6 %collective-permute-start.36 = (f32[2,256,256]{1,2,0:T(8,128)S(1)}, f32[2,256,256]{1,2,0:T(8,128)}, u32[]{:S(2)}, u32[]{:S(2)}) collective-permute-start(f32[2,256,256]{1,2,0:T(8,128)S(1)} %pad_maximum_fusion.20), channel_id=1, source_target_pairs={{12,4},{1,9},{14,6},{7,15},{28,20},{29,21},{18,26},{27,19},{36,44}... | collective-permute-start | bytes 1572872 | tf_op jit(solution)/shard_map/ppermute | solution.py:189
  167.5 15.3 %collective-permute-start.35 = (f32[2,256,256]{1,2,0:T(8,128)S(1)}, f32[2,256,256]{1,2,0:T(8,128)}, u32[]{:S(2)}, u32[]{:S(2)}) collective-permute-start(f32[2,256,256]{1,2,0:T(8,128)S(1)} %pad_maximum_fusion.20), channel_id=1, source_target_pairs={{0,4},{5,9},{2,6},{11,15},{16,20},{17,21},{22,26},{31,19},{40,44},... | collective-permute-start | bytes 1572872 | tf_op jit(solution)/shard_map/ppermute | solution.py:189
  172.9 65.4 %collective-permute-start.40 = (f32[2,256,256]{1,2,0:T(8,128)}, f32[2,256,256]{1,2,0:T(8,128)}, u32[]{:S(2)}, u32[]{:S(2)}) collective-permute-start(f32[2,256,256]{1,2,0:T(8,128)} %get-tuple-element.35), channel_id=1, source_target_pairs={{0,2},{5,3},{14,10},{7,11},{24,18},{17,19},{26,26},{27,27},{40,36}... | collective-permute-start | bytes 1572872 | tf_op jit(solution)/shard_map/ppermute | solution.py:208
  176.3 68.2 %collective-permute-start.41 = (f32[2,256,256]{2,1,0:T(8,128)}, f32[2,256,256]{2,1,0:T(8,128)}, u32[]{:S(2)}, u32[]{:S(2)}) collective-permute-start(f32[2,256,256]{2,1,0:T(8,128)} %broadcast_select_fusion.10), channel_id=1, source_target_pairs={{12,130},{13,131},{6,138},{15,139},{20,146},{25,147},{18,154},{19,... | collective-permute-start | bytes 1572872 | tf_op jit(solution)/shard_map/ppermute | solution.py:208
  185.5 55.6 %collective-permute-start.42 = (f32[2,256,256]{1,2,0:T(8,128)S(1)}, f32[2,256,256]{1,2,0:T(8,128)S(1)}, u32[]{:S(2)}, u32[]{:S(2)}) collective-permute-start(f32[2,256,256]{1,2,0:T(8,128)S(1)} %get-tuple-element.37), channel_id=1, source_target_pairs={{4,4},{9,5},{6,140},{15,141},{20,20},{21,21},{26,156},{19,157},{44... | collective-permute-start | bytes 1572872 | tf_op jit(solution)/shard_map/ppermute | solution.py:208
  192.0 44.7 %collective-permute-start.44 = (f32[256,256]{0,1:T(8,128)}, f32[256,256]{0,1:T(8,128)S(1)}, u32[]{:S(2)}, u32[]{:S(2)}) collective-permute-start(f32[256,256]{0,1:T(8,128)} %get-tuple-element.53), channel_id=1, source_target_pairs={{4,8},{5,1},{6,128},{7,137},{24,144},{25,25},{26,24},{27,145},{40,... | collective-permute-start | bytes 786440 | tf_op jit(solution)/shard_map/ppermute | solution.py:219
  199.1 48.5 %collective-permute-start.43 = (f32[256,256]{1,0:T(8,128)}, f32[256,256]{1,0:T(8,128)}, u32[]{:S(2)}, u32[]{:S(2)}) collective-permute-start(f32[256,256]{1,0:T(8,128)} %get-tuple-element.33), channel_id=1, source_target_pairs={{4,0},{5,1},{6,136},{7,137},{24,144},{25,17},{26,24},{27,153},{40,... | collective-permute-start | bytes 786440 | tf_op jit(solution)/shard_map/ppermute | solution.py:219
  236.8 28.7 %collective-permute-start.39 = (f32[256,256]{1,0:T(8,128)}, f32[256,256]{1,0:T(8,128)}, u32[]{:S(2)}, u32[]{:S(2)}) collective-permute-start(f32[256,256]{1,0:T(8,128)} %get-tuple-element.32), channel_id=1, source_target_pairs={{4,128},{5,16},{6,8},{7,152},{24,9},{25,145},{26,129},{27,25},{40,... | collective-permute-start | bytes 786440 | tf_op jit(solution)/shard_map/ppermute | solution.py:219
  244.5 19.0 %collective-permute-start.38 = (f32[2,256,256]{1,2,0:T(8,128)}, f32[2,256,256]{1,2,0:T(8,128)}, u32[]{:S(2)}, u32[]{:S(2)}) collective-permute-start(f32[2,256,256]{1,2,0:T(8,128)} %get-tuple-element.36), channel_id=1, source_target_pairs={{4,64},{9,80},{6,200},{15,216},{20,65},{21,81},{26,201},{19,217},{... | collective-permute-start | bytes 1572872 | tf_op jit(solution)/shard_map/ppermute | solution.py:209
  (41 other events, 329.7 us)

commit v4 on v0

v4 whole, which is shorter than its diff:
```python
import itertools

import jax
import jax.numpy as jnp
import numpy as np
from jax import lax
from jax.sharding import Mesh
from jax.sharding import PartitionSpec as P

AXES = ("zh", "y", "core", "zl", "x")
SIZES = (2, 4, 2, 4, 4)
BLOCKS = 4


def rcv_of(zh, y, core):
    return (zh * 4 + y) * 2 + core


def device_of(row, col):
    return row * 16 + col


def places():
    return itertools.product(range(2), range(4), range(2), range(4))


def held_pair(f, y, core, x, block, core_col):
    e_col = x // 2
    if block < 2:
        e_row, dy = block, 1
    elif block == 2:
        e_row, dy = (e_col if y < 2 else 1 - e_col), 2
    elif core_col != core:
        e_row, dy = (e_col if core == 0 else 1 - e_col), 0
    elif e_col == f:
        return rcv_of(1, y, core), rcv_of(0, y, core)
    else:
        return None
    return rcv_of(f ^ e_row, y, core), rcv_of(f ^ e_col, (y + dy) % 4, core_col)


def deliveries(f, y, core, x, block):
    out = []
    for core_col in range(2):
        j = core_col ^ (x % 2)
        pair = held_pair(f, y, core, x, block, core_col)
        if pair is None:
            first, second = (device_of(r, r) for r in (rcv_of(f, y, core), rcv_of(1 - f, y, core)))
        else:
            first, second = device_of(*pair), device_of(*pair[::-1])
            if f == 1:
                first, second = second, first
        out += [(j, first), (2 + j, second)]
    return out


SLOTS = (
    (
        ((0x78, 0x93, 0x87, 0x4e), (0x72, 0xd8, 0x4e, 0x8d)),
        ((0xe1, 0x4e, 0x93, 0x63), (0xc9, 0x72, 0x8d, 0x4e)),
        ((0xb1, 0x87, 0x2d, 0x27), (0x93, 0xb1, 0x2d, 0x2d)),
        ((0x6c, 0x8d, 0x93, 0x2d), (0x93, 0x93, 0xe1, 0x2d)),
    ),
    (
        ((0x8d, 0x39, 0xb1, 0x4e), (0xc9, 0xe1, 0x72, 0x72)),
        ((0xb1, 0x2d, 0xd2, 0xd2), (0x8d, 0x39, 0xb1, 0x72)),
        ((0x36, 0xe1, 0x4e, 0x72), (0x39, 0xc6, 0xd2, 0x4e)),
        ((0xb1, 0xc6, 0x4e, 0x78), (0x1b, 0xb1, 0x9c, 0x4e)),
    ),
)


def slots_of(f, y, core, x):
    code = SLOTS[f][y][core][x]
    return [code >> (2 * zl) & 3 for zl in range(4)]


def tables():
    slots = np.zeros((2, 4, 2, 4, 4), np.int32)
    perms = [[], [], [], []]
    for f, y, core, x in places():
        slots[f, y, core, x] = slots_of(f, y, core, x)
        for zl in range(4):
            source = device_of(rcv_of(f, y, core), zl * 4 + x)
            for slot, target in deliveries(f, y, core, x, slots[f, y, core, x, zl]):
                perms[slot].append((source, target))
    for perm in perms:
        assert len({s for s, _ in perm}) == len(perm) == len({t for _, t in perm}) == 256
    case = np.zeros((16, 16), np.int32)
    for f, y, core, x in places():
        for block, core_col in itertools.product(range(BLOCKS), range(2)):
            pair = held_pair(f, y, core, x, block, core_col)
            if pair is not None and f == 0:
                case[pair] = 1
    for row in range(16):
        case[row, row] = 2
    return slots, perms, case


def ring(n, step):
    return [(i, (i + step) % n) for i in range(n)]


def gather_x(block):
    half = block.shape[1] // 2
    above = lax.ppermute(block, "x", ring(4, -1))
    below = lax.ppermute(block, "x", ring(4, 1))
    far_a = lax.ppermute(above[:, :half], "x", ring(4, -1))
    far_b = lax.ppermute(below[:, half:], "x", ring(4, 1))
    return jnp.concatenate([block, above, below, far_a, far_b], axis=1)


def dot(rows, cols):
    return lax.dot_general(rows, cols, (((0,), (0,)), ((), ())), preferred_element_type=jnp.float32)


def product(rows, cols):
    real = jnp.einsum("psm,psn->mn", rows, cols, preferred_element_type=jnp.float32)
    return jnp.stack([real, dot(rows[0], cols[1]) - dot(rows[1], cols[0])])


def body(wavefield):
    slots, perms, case_of = tables()
    f, y, core, zl, x = (lax.axis_index(name) for name in AXES)
    n = wavefield.shape[3]
    half = n // 2
    scale = 1.0 / jnp.sqrt(jnp.float32(wavefield.shape[2] * 16))
    e_col, h_col = x // 2, x % 2

    own = lax.dynamic_index_in_dim(wavefield, f, 0, keepdims=False)
    other = lax.dynamic_index_in_dim(wavefield, 1 - f, 0, keepdims=False)
    other = lax.ppermute(other, "zh", ring(2, 1))

    near = [lax.ppermute(block, "y", ring(4, -1)) for block in (own, other)]
    far = [lax.ppermute(block, "y", ring(4, -2)) for block in (own, other)]
    block0, block1 = gather_x(own), gather_x(other)

    def half_of(block, h):
        return jnp.where(h == 0, block[..., :half], block[..., half:])

    def quarter(pair, place):
        return half_of(jnp.where(place // 2 == 0, pair[0], pair[1]), place % 2)

    def quarters(place):
        return jnp.stack([quarter(near, place), quarter(far, place)])

    pieces = [quarters(x)]
    for step in (-1, 1, 2):
        pieces.append(lax.ppermute(quarters((x + step) % 4), "x", ring(4, step)))
    mine = jnp.concatenate(pieces, axis=2)

    def both(a, b):
        return jnp.where(core == 0, jnp.concatenate([a, b], -1), jnp.concatenate([b, a], -1))

    cols = both(mine, lax.ppermute(mine, "core", ring(2, 1)))
    mine0 = half_of(jnp.where(e_col == 0, block0, block1), h_col)
    other0 = lax.ppermute(mine0, "core", ring(2, 1))

    rows = jnp.concatenate([block0, block1], axis=2)
    upper = lax.broadcasted_iota(jnp.int32, (n, n), 0) <= lax.broadcasted_iota(jnp.int32, (n, n), 1)
    upper_half = half_of(upper, h_col)
    cross = product(jnp.where((e_col == 0) == (core == 0), block0, block1), other0)
    inner = product(rows, half_of(block0, h_col))
    inner1 = product(rows, half_of(block1, h_col))
    is0 = f == 0
    diag0, diag1 = jnp.where(is0, inner[:, :n], inner1[:, n:]), jnp.where(is0, inner1[:, n:], inner[:, :n])
    packed = jnp.stack([jnp.where(upper_half, d[0], d[1]) for d in (diag0, diag1)])
    block3 = both(jnp.where(e_col == f, jnp.where(is0, inner[:, n:], inner1[:, :n]), packed), cross)

    product1 = product(rows, cols[0])
    product2 = product(jnp.where((e_col == 0) == (y < 2), block0, block1), cols[1])
    blocks = jnp.stack([product1[:, :n], product1[:, n:], product2, block3])

    order = jnp.asarray(slots)[f, y, core, x]
    held = sum_over_zl(blocks, order, zl) * scale

    def part(j):
        return jnp.where((h_col ^ j) == 0, held[..., :half], held[..., half:])

    got = [lax.ppermute(part(slot % 2), AXES, perm) for slot, perm in enumerate(perms)]
    row, col = rcv_of(f, y, core), zl * 4 + x
    case = jnp.asarray(case_of)[row, col]
    swapped = jnp.where(case == 0, row, col) % 2 == 1

    def joined(a, b):
        return jnp.where(swapped, jnp.concatenate([b, a], -1), jnp.concatenate([a, b], -1))

    first, second = joined(got[0], got[1]), joined(got[2], got[3])

    def unpack(packed):
        strict = lax.broadcasted_iota(jnp.int32, (n, n), 0) < lax.broadcasted_iota(jnp.int32, (n, n), 1)
        top, low = jnp.where(upper, packed, 0.0), jnp.where(upper, 0.0, packed)
        return jnp.stack([top + jnp.where(strict, packed, 0.0).T, low - low.T])

    def turned(block):
        return jnp.stack([block[0].T, -block[1].T])

    diag_first, diag_second = (unpack(jnp.where(is0, a[0], a[1])) for a in (first, second))
    out0 = jnp.where(case == 1, first, jnp.where(case == 0, turned(second), jnp.where(is0, diag_first, diag_second)))
    out1 = jnp.where(case == 1, second, jnp.where(case == 0, turned(first), jnp.where(is0, diag_second, diag_first)))
    return jnp.stack([out0, out1])


def sum_over_zl(blocks, order, zl):
    def partial_of(slot):
        return lax.dynamic_index_in_dim(blocks, order[slot], 0, keepdims=False)

    total = partial_of(zl)
    for step in (1, 2, 3):
        total = total + lax.ppermute(partial_of((zl + step) % 4), "zl", ring(4, step))
    return total


def solution(mesh):
    fine = Mesh(mesh.devices.reshape(SIZES), AXES)
    return jax.shard_map(
        body,
        mesh=fine,
        in_specs=(P(None, None, ("zl", "x"), ("zh", "y", "core")),),
        out_specs=P(None, None, ("zh", "y", "core"), ("zl", "x")),
        check_vma=False,
    )
```

time: 438 us -> 222 us (0.51)
  waiting for transfers between devices: 372 us -> 108 us
  starting transfers between devices: 0.04 us -> 64 us
  matrix products: 34.9 us -> 11.7 us
  local copies, waits for them, and re-layouts: 4.3 us -> 14.4 us
  between operations: 13.4 us -> 9 us
    all_gather x1 -> x0, waiting for transfers between devices: 187 us -> none  [body(): lax.all_gather(wavefield, 'rcv', axis=3, tiled=True)]
    reduce_scatter x1 -> x0, waiting for transfers between devices: 184 us -> none  [body(): lax.psum_scatter(partial_gram, 'shot', scatter_dimension=3, tiled=True)]
    ppermute x0 -> x25, waiting for transfers between devices: none -> 108 us  [the longest x4 35.4 us: body(): lax.ppermute(part(slot % 2), AXES, perm)]
    ppermute x0 -> x25, starting transfers between devices: none -> 64 us  [the longest x4 29.7 us: body(): lax.ppermute(part(slot % 2), AXES, perm)]
    dot_general x4 -> x15, matrix products: 34.9 us -> 11.7 us  [the longest x10 6.36 us: dot(): lax.dot_general(rows, cols, (((0,), (0,)), ((), ())), preferred_element_t...]
    select_n x0 -> x17, other arithmetic: none -> 9.56 us  [the longest x2 3.44 us: both(): jnp.where(core == 0, jnp.concatenate([a, b], -1), jnp.concatenate([b, a],...]
    another operation x1 -> x16, other arithmetic: 11.6 us -> 3.59 us  [the longest x3 1.06 us: unpack(): return jnp.stack([top + jnp.where(strict, packed, 0.0).T, low - low.T])]
    squeeze x0 -> x6, local copies, waits for them, and re-layouts: none -> 4.39 us  [the longest x5 2.52 us: partial_of(): return lax.dynamic_index_in_dim(blocks, order[slot], 0, keepdims=False)]
  transfers between devices with their start and end apart: 2 -> 25, of which waited for: 2 -> 12; matrix products, arithmetic and copies ran while one was open for 0% -> 9% of each run, Pallas kernels for 0% -> 0%
where the time goes in v4:
time: 222 us; the launch traced here: 221 us
  waiting for transfers between devices  108 us (49%)
  starting transfers between devices  64 us (29%)
  local copies, waits for them, and re-layouts  14.4 us (6%)
  other arithmetic  14 us (6%)
  matrix products  11.7 us (5%)
  between operations  9 us (4%)
    ppermute x4, waiting for transfers between devices, body(): lax.ppermute(part(slot % 2), AXES, perm)  35.4 us
    ppermute x3, waiting for transfers between devices, sum_over_zl(): lax.ppermute(partial_of((zl + step) % 4), 'zl', ring(4, step))  34 us
    ppermute x4, starting transfers between devices, body(): lax.ppermute(part(slot % 2), AXES, perm)  29.7 us
    ppermute x3, waiting for transfers between devices, body(): pieces.append(lax.ppermute(quarters((x + step) % 4), 'x', ring(4, step)))  15 us
    ppermute x2, waiting for transfers between devices, body(): near = [lax.ppermute(block, 'y', ring(4, -1)) for block in (own, other)]  9.81 us
    ppermute x2, waiting for transfers between devices, gather_x(): below = lax.ppermute(block, 'x', ring(4, 1))  7.41 us
    ppermute x1, starting transfers between devices, body(): other = lax.ppermute(other, 'zh', ring(2, 1))  7.19 us
    ppermute x2, starting transfers between devices, gather_x(): far_a = lax.ppermute(above[:, :half], 'x', ring(4, -1))  6.7 us
  transfers between devices with their start and end apart: 25, of which 12 were waited for; matrix products, arithmetic and copies ran while one was open for 9% of the time, Pallas kernels for 0%

profile of v4, /device:TPU:16, one launch (start us, length us, event | category | flops | bytes accessed | tf_op | source)
XLA Modules:
  0.0 220.8 jit_solution(208656143207396161)
XLA Ops:
  0.0 1.9 constant_dynamic-update-slice_fusion.4
  1.9 1.5 collective-permute-start.1
  3.4 1.7 collective-permute-start
  5.1 1.9 dynamic-slice_bitcast_fusion.4
  7.0 7.2 %collective-permute-start.4 = (bf16[2,512,256]{2,1,0:T(8,128)(2,1)}, bf16[2,512,256]{2,1,0:T(8,128)(2,1)}, u32[]{:S(2)}, u32[]{:S(2)}) collective-permute-start(bf16[2,512,256]{2,1,0:T(8,128)(2,1)} %dynamic-slice_bitcast_fusion.4), channel_id=1, source_target_pairs={{0,128},{128,0},{1,129},{129,1},{2,130},{130,2},{3,131},{131,3},{4... | collective-permute-start | bytes 1572872 | tf_op jit(solution)/shard_map/ppermute | solution.py:132
  14.7 2.9 %collective-permute-start.11 = (bf16[2,512,256]{2,1,0:T(8,128)(2,1)}, bf16[2,512,256]{2,1,0:T(8,128)(2,1)}, u32[]{:S(2)}, u32[]{:S(2)}) collective-permute-start(bf16[2,512,256]{2,1,0:T(8,128)(2,1)} %get-tuple-element.8), channel_id=1, source_target_pairs={{0,64},{32,96},{64,0},{96,32},{1,65},{33,97},{65,1},{97,33},{2,66}... | collective-permute-start | bytes 1572872 | tf_op jit(solution)/shard_map/ppermute | solution.py:135
  17.6 1.4 fusion.52
  26.5 3.0 %collective-permute-start.2 = (bf16[2,256,256]{2,1,0:T(8,128)(2,1)S(1)}, bf16[2,256,256]{2,1,0:T(8,128)(2,1)S(1)}, u32[]{:S(2)}, u32[]{:S(2)}) collective-permute-start(bf16[2,256,256]{2,1,0:T(8,128)(2,1)S(1)} %slice.272), channel_id=1, source_target_pairs={{0,3},{1,0},{2,1},{3,2},{4,7},{5,4},{6,5},{7,6},{8,11},{9,8},{10,9... | collective-permute-start | bytes 786440 | tf_op jit(solution)/shard_map/ppermute | solution.py:108
  30.8 2.7 %collective-permute-done.2 = bf16[2,256,256]{2,1,0:T(8,128)(2,1)S(1)} collective-permute-done((bf16[2,256,256]{2,1,0:T(8,128)(2,1)S(1)}, bf16[2,256,256]{2,1,0:T(8,128)(2,1)S(1)}, u32[]{:S(2)}, u32[]{:S(2)}) %collective-permute-start.2) | collective-permute-done | bytes 262176 | tf_op jit(solution)/shard_map/ppermute | solution.py:108
  34.1 2.6 %collective-permute-done.3 = bf16[2,256,256]{2,1,0:T(8,128)(2,1)S(1)} collective-permute-done((bf16[2,256,256]{2,1,0:T(8,128)(2,1)S(1)}, bf16[2,256,256]{2,1,0:T(8,128)(2,1)S(1)}, u32[]{:S(2)}, u32[]{:S(2)}) %collective-permute-start.3) | collective-permute-done | bytes 262176 | tf_op jit(solution)/shard_map/ppermute | solution.py:109
  37.9 7.4 %collective-permute-done.6 = bf16[2,512,256]{2,1,0:T(8,128)(2,1)S(1)} collective-permute-done((bf16[2,512,256]{2,1,0:T(8,128)(2,1)}, bf16[2,512,256]{2,1,0:T(8,128)(2,1)S(1)}, u32[]{:S(2)}, u32[]{:S(2)}) %collective-permute-start.6) | collective-permute-done | bytes 524320 | tf_op jit(solution)/shard_map/ppermute | solution.py:107
  46.3 3.7 %collective-permute-start.7 = (bf16[2,256,256]{2,1,0:T(8,128)(2,1)S(1)}, bf16[2,256,256]{2,1,0:T(8,128)(2,1)S(1)}, u32[]{:S(2)}, u32[]{:S(2)}) collective-permute-start(bf16[2,256,256]{2,1,0:T(8,128)(2,1)S(1)} %slice.274), channel_id=1, source_target_pairs={{0,3},{1,0},{2,1},{3,2},{4,7},{5,4},{6,5},{7,6},{8,11},{9,8},{10,9... | collective-permute-start | bytes 786440 | tf_op jit(solution)/shard_map/ppermute | solution.py:108
  51.2 9.8 %collective-permute-done.10 = bf16[2,512,256]{2,1,0:T(8,128)(2,1)S(1)} collective-permute-done((bf16[2,512,256]{2,1,0:T(8,128)(2,1)}, bf16[2,512,256]{2,1,0:T(8,128)(2,1)S(1)}, u32[]{:S(2)}, u32[]{:S(2)}) %collective-permute-start.10) | collective-permute-done | bytes 524320 | tf_op jit(solution)/shard_map/ppermute | solution.py:134
  62.3 1.9 collective-permute-start.15
  65.3 2.7 %collective-permute-start.13 = (bf16[2,2,512,128]{3,2,1,0:T(8,128)(2,1)S(1)}, bf16[2,2,512,128]{3,2,1,0:T(8,128)(2,1)S(1)}, u32[]{:S(2)}, u32[]{:S(2)}) collective-permute-start(bf16[2,2,512,128]{3,2,1,0:T(8,128)(2,1)S(1)} %pad_maximum_fusion.12), channel_id=1, source_target_pairs={{0,3},{1,0},{2,1},{3,2},{4,7},{5,4},{6,5},{7,6},{8,11},{9,8},{10,9... | collective-permute-start | bytes 1572872 | tf_op jit(solution)/shard_map/ppermute | solution.py:149
  71.7 1.3 fusion.10
  73.0 5.8 %collective-permute-done.15 = bf16[2,2,512,128]{3,2,1,0:T(8,128)(2,1)S(1)} collective-permute-done((bf16[2,2,512,128]{3,2,1,0:T(8,128)(2,1)S(1)}, bf16[2,2,512,128]{3,2,1,0:T(8,128)(2,1)S(1)}, u32[]{:S(2)}, u32[]{:S(2)}) %collective-permute-start.15) | collective-permute-done | bytes 524320 | tf_op jit(solution)/shard_map/ppermute | solution.py:149
  78.8 9.2 %collective-permute-done.14 = bf16[2,2,512,128]{3,2,1,0:T(8,128)(2,1)S(1)} collective-permute-done((bf16[2,2,512,128]{3,2,1,0:T(8,128)(2,1)S(1)}, bf16[2,2,512,128]{3,2,1,0:T(8,128)(2,1)S(1)}, u32[]{:S(2)}, u32[]{:S(2)}) %collective-permute-start.14) | collective-permute-done | bytes 524320 | tf_op jit(solution)/shard_map/ppermute | solution.py:149
  89.0 1.3 fusion.11
  92.4 3.4 %maximum_select_fusion = bf16[2,2,2048,256]{3,2,1,0:T(8,128)(2,1)S(1)} fusion(bf16[2,2,2048,128]{3,2,1,0:T(8,128)(2,1)S(1)} %collective-permute-done.16, bf16[2,2,512,128]{3,2,1,0:T(8,128)(2,1)S(1)} %collective-permute-done.15, bf16[2,2,512,128]{3,2,1,0:T(8,128)(2,1)S(1)} %collective-permute-done.14, bf16[2,2,512,128]{3,2,1,0:T(8,128)(2,1)S(1)} %collective-permute-done.13, ...), kind=kLoop, calls=%fused_computation.5 | loop fusion | flops 52428800 | bytes 8388609 | tf_op jit(solution)/shard_map/jit(_where)/select_n | solution.py:153
  95.9 1.3 fusion.7
  103.0 3.8 %collective-permute-start.19 = (f32[2,256,256]{1,2,0:T(8,128)}, f32[2,256,256]{1,2,0:T(8,128)S(1)}, u32[]{:S(2)}, u32[]{:S(2)}) collective-permute-start(f32[2,256,256]{1,2,0:T(8,128)} %copy.48), channel_id=1, source_target_pairs={{0,8},{4,12},{8,0},{12,4},{1,9},{5,13},{9,1},{13,5},{2,10},{6,14},... | collective-permute-start | bytes 1572872 | tf_op jit(solution)/shard_map/ppermute | solution.py:210
  107.5 1.4 collective-permute-start.18
  109.0 22.3 %collective-permute-done.19 = f32[2,256,256]{1,2,0:T(8,128)S(1)} collective-permute-done((f32[2,256,256]{1,2,0:T(8,128)}, f32[2,256,256]{1,2,0:T(8,128)S(1)}, u32[]{:S(2)}, u32[]{:S(2)}) %collective-permute-start.19) | collective-permute-done | bytes 524320 | tf_op jit(solution)/shard_map/ppermute | solution.py:210
  131.4 11.7 %collective-permute-done.20 = f32[2,256,256]{1,2,0:T(8,128)S(1)} collective-permute-done((f32[2,256,256]{1,2,0:T(8,128)}, f32[2,256,256]{1,2,0:T(8,128)S(1)}, u32[]{:S(2)}, u32[]{:S(2)}) %collective-permute-start.20) | collective-permute-done | bytes 524320 | tf_op jit(solution)/shard_map/ppermute | solution.py:210
  143.2 1.3 collective-permute-start.23
  144.6 3.6 %collective-permute-start.24 = (f32[2,256,128]{1,2,0:T(8,128)S(1)}, f32[2,256,128]{1,2,0:T(8,128)S(1)}, u32[]{:S(2)}, u32[]{:S(2)}) collective-permute-start(f32[2,256,128]{1,2,0:T(8,128)S(1)} %get-tuple-element.36), channel_id=1, source_target_pairs={{0,32},{4,64},{8,8},{12,40},{1,16},{5,48},{9,56},{13,80},{2,136},{... | collective-permute-start | bytes 786440 | tf_op jit(solution)/shard_map/ppermute | solution.py:180
  148.2 1.3 dynamic_slice.36
  151.2 12.7 %collective-permute-start.21 = (f32[2,256,128]{1,2,0:T(8,128)S(1)}, f32[2,256,128]{1,2,0:T(8,128)S(1)}, u32[]{:S(2)}, u32[]{:S(2)}) collective-permute-start(f32[2,256,128]{1,2,0:T(8,128)S(1)} %get-tuple-element.35), channel_id=1, source_target_pairs={{0,3},{4,5},{8,1},{12,131},{1,128},{5,2},{9,130},{13,4},{2,137},{6... | collective-permute-start | bytes 786440 | tf_op jit(solution)/shard_map/ppermute | solution.py:180
  163.8 12.1 %collective-permute-start.22 = (f32[2,256,128]{1,2,0:T(8,128)S(1)}, f32[2,256,128]{1,2,0:T(8,128)S(1)}, u32[]{:S(2)}, u32[]{:S(2)}) collective-permute-start(f32[2,256,128]{1,2,0:T(8,128)S(1)} %get-tuple-element.36), channel_id=1, source_target_pairs={{0,2},{4,4},{8,128},{12,130},{1,1},{5,3},{9,131},{13,5},{2,0},{6,1... | collective-permute-start | bytes 786440 | tf_op jit(solution)/shard_map/ppermute | solution.py:180
  176.8 4.4 %collective-permute-done.21 = f32[2,256,128]{1,2,0:T(8,128)S(1)} collective-permute-done((f32[2,256,128]{1,2,0:T(8,128)S(1)}, f32[2,256,128]{1,2,0:T(8,128)S(1)}, u32[]{:S(2)}, u32[]{:S(2)}) %collective-permute-start.21) | collective-permute-done | bytes 262176 | tf_op jit(solution)/shard_map/ppermute | solution.py:180
  181.2 31.0 %collective-permute-done.22 = f32[2,256,128]{1,2,0:T(8,128)S(1)} collective-permute-done((f32[2,256,128]{1,2,0:T(8,128)S(1)}, f32[2,256,128]{1,2,0:T(8,128)S(1)}, u32[]{:S(2)}, u32[]{:S(2)}) %collective-permute-start.22) | collective-permute-done | bytes 262176 | tf_op jit(solution)/shard_map/ppermute | solution.py:180
  (106 shorter events, 31.7 us)
Async XLA Ops:
  1.9 24.2 %collective-permute-start.1 = (bf16[2,512,256]{2,1,0:T(8,128)(2,1)}, bf16[2,512,256]{2,1,0:T(8,128)(2,1)S(1)}, u32[]{:S(2)}, u32[]{:S(2)}) collective-permute-start(bf16[2,512,256]{2,1,0:T(8,128)(2,1)} %get-tuple-element.8), channel_id=1, source_target_pairs={{0,1},{1,2},{2,3},{3,0},{4,5},{5,6},{6,7},{7,4},{8,9},{9,10},{10,1... | collective-permute-start | bytes 1572872 | tf_op jit(solution)/shard_map/ppermute | solution.py:107
  3.4 23.1 %collective-permute-start = (bf16[2,512,256]{2,1,0:T(8,128)(2,1)}, bf16[2,512,256]{2,1,0:T(8,128)(2,1)S(1)}, u32[]{:S(2)}, u32[]{:S(2)}) collective-permute-start(bf16[2,512,256]{2,1,0:T(8,128)(2,1)} %get-tuple-element.8), channel_id=1, source_target_pairs={{0,3},{1,0},{2,1},{3,2},{4,7},{5,4},{6,5},{7,6},{8,11},{9,8},{10,9... | collective-permute-start | bytes 1572872 | tf_op jit(solution)/shard_map/ppermute | solution.py:106
  7.0 22.6 %collective-permute-start.4 = (bf16[2,512,256]{2,1,0:T(8,128)(2,1)}, bf16[2,512,256]{2,1,0:T(8,128)(2,1)}, u32[]{:S(2)}, u32[]{:S(2)}) collective-permute-start(bf16[2,512,256]{2,1,0:T(8,128)(2,1)} %dynamic-slice_bitcast_fusion.4), channel_id=1, source_target_pairs={{0,128},{128,0},{1,129},{129,1},{2,130},{130,2},{3,131},{131,3},{4... | collective-permute-start | bytes 1572872 | tf_op jit(solution)/shard_map/ppermute | solution.py:132
  14.2 37.0 %collective-permute-start.9 = (bf16[2,512,256]{2,1,0:T(8,128)(2,1)}, bf16[2,512,256]{2,1,0:T(8,128)(2,1)}, u32[]{:S(2)}, u32[]{:S(2)}) collective-permute-start(bf16[2,512,256]{2,1,0:T(8,128)(2,1)} %get-tuple-element.8), channel_id=1, source_target_pairs={{0,96},{32,0},{64,32},{96,64},{1,97},{33,1},{65,33},{97,65},{2,98}... | collective-permute-start | bytes 1572872 | tf_op jit(solution)/shard_map/ppermute | solution.py:134
  14.7 31.7 %collective-permute-start.11 = (bf16[2,512,256]{2,1,0:T(8,128)(2,1)}, bf16[2,512,256]{2,1,0:T(8,128)(2,1)}, u32[]{:S(2)}, u32[]{:S(2)}) collective-permute-start(bf16[2,512,256]{2,1,0:T(8,128)(2,1)} %get-tuple-element.8), channel_id=1, source_target_pairs={{0,64},{32,96},{64,0},{96,32},{1,65},{33,97},{65,1},{97,33},{2,66}... | collective-permute-start | bytes 1572872 | tf_op jit(solution)/shard_map/ppermute | solution.py:135
  26.1 10.5 %collective-permute-start.3 = (bf16[2,256,256]{2,1,0:T(8,128)(2,1)S(1)}, bf16[2,256,256]{2,1,0:T(8,128)(2,1)S(1)}, u32[]{:S(2)}, u32[]{:S(2)}) collective-permute-start(bf16[2,256,256]{2,1,0:T(8,128)(2,1)S(1)} %slice.273), channel_id=1, source_target_pairs={{0,1},{1,2},{2,3},{3,0},{4,5},{5,6},{6,7},{7,4},{8,9},{9,10},{10,1... | collective-permute-start | bytes 786440 | tf_op jit(solution)/shard_map/ppermute | solution.py:109
  26.5 6.9 %collective-permute-start.2 = (bf16[2,256,256]{2,1,0:T(8,128)(2,1)S(1)}, bf16[2,256,256]{2,1,0:T(8,128)(2,1)S(1)}, u32[]{:S(2)}, u32[]{:S(2)}) collective-permute-start(bf16[2,256,256]{2,1,0:T(8,128)(2,1)S(1)} %slice.272), channel_id=1, source_target_pairs={{0,3},{1,0},{2,1},{3,2},{4,7},{5,4},{6,5},{7,6},{8,11},{9,8},{10,9... | collective-permute-start | bytes 786440 | tf_op jit(solution)/shard_map/ppermute | solution.py:108
  29.6 15.7 %collective-permute-start.6 = (bf16[2,512,256]{2,1,0:T(8,128)(2,1)}, bf16[2,512,256]{2,1,0:T(8,128)(2,1)S(1)}, u32[]{:S(2)}, u32[]{:S(2)}) collective-permute-start(bf16[2,512,256]{2,1,0:T(8,128)(2,1)} %collective-permute-done.4), channel_id=1, source_target_pairs={{0,1},{1,2},{2,3},{3,0},{4,5},{5,6},{6,7},{7,4},{8,9},{9,10},{10,1... | collective-permute-start | bytes 1572872 | tf_op jit(solution)/shard_map/ppermute | solution.py:107
  33.5 16.5 %collective-permute-start.12 = (bf16[2,512,256]{2,1,0:T(8,128)(2,1)}, bf16[2,512,256]{2,1,0:T(8,128)(2,1)S(1)}, u32[]{:S(2)}, u32[]{:S(2)}) collective-permute-start(bf16[2,512,256]{2,1,0:T(8,128)(2,1)} %collective-permute-done.4), channel_id=1, source_target_pairs={{0,64},{32,96},{64,0},{96,32},{1,65},{33,97},{65,1},{97,33},{2,66}... | collective-permute-start | bytes 1572872 | tf_op jit(solution)/shard_map/ppermute | solution.py:135
  36.7 9.6 %collective-permute-start.5 = (bf16[2,512,256]{2,1,0:T(8,128)(2,1)}, bf16[2,512,256]{2,1,0:T(8,128)(2,1)S(1)}, u32[]{:S(2)}, u32[]{:S(2)}) collective-permute-start(bf16[2,512,256]{2,1,0:T(8,128)(2,1)} %collective-permute-done.4), channel_id=1, source_target_pairs={{0,3},{1,0},{2,1},{3,2},{4,7},{5,4},{6,5},{7,6},{8,11},{9,8},{10,9... | collective-permute-start | bytes 1572872 | tf_op jit(solution)/shard_map/ppermute | solution.py:106
  45.3 15.7 %collective-permute-start.10 = (bf16[2,512,256]{2,1,0:T(8,128)(2,1)}, bf16[2,512,256]{2,1,0:T(8,128)(2,1)S(1)}, u32[]{:S(2)}, u32[]{:S(2)}) collective-permute-start(bf16[2,512,256]{2,1,0:T(8,128)(2,1)} %collective-permute-done.4), channel_id=1, source_target_pairs={{0,96},{32,0},{64,32},{96,64},{1,97},{33,1},{65,33},{97,65},{2,98}... | collective-permute-start | bytes 1572872 | tf_op jit(solution)/shard_map/ppermute | solution.py:134
  46.3 22.0 %collective-permute-start.8 = (bf16[2,256,256]{2,1,0:T(8,128)(2,1)S(1)}, bf16[2,256,256]{2,1,0:T(8,128)(2,1)S(1)}, u32[]{:S(2)}, u32[]{:S(2)}) collective-permute-start(bf16[2,256,256]{2,1,0:T(8,128)(2,1)S(1)} %slice.275), channel_id=1, source_target_pairs={{0,1},{1,2},{2,3},{3,0},{4,5},{5,6},{6,7},{7,4},{8,9},{9,10},{10,1... | collective-permute-start | bytes 786440 | tf_op jit(solution)/shard_map/ppermute | solution.py:109
  46.3 21.9 %collective-permute-start.7 = (bf16[2,256,256]{2,1,0:T(8,128)(2,1)S(1)}, bf16[2,256,256]{2,1,0:T(8,128)(2,1)S(1)}, u32[]{:S(2)}, u32[]{:S(2)}) collective-permute-start(bf16[2,256,256]{2,1,0:T(8,128)(2,1)S(1)} %slice.274), channel_id=1, source_target_pairs={{0,3},{1,0},{2,1},{3,2},{4,7},{5,4},{6,5},{7,6},{8,11},{9,8},{10,9... | collective-permute-start | bytes 786440 | tf_op jit(solution)/shard_map/ppermute | solution.py:108
  62.3 16.5 %collective-permute-start.15 = (bf16[2,2,512,128]{3,2,1,0:T(8,128)(2,1)S(1)}, bf16[2,2,512,128]{3,2,1,0:T(8,128)(2,1)S(1)}, u32[]{:S(2)}, u32[]{:S(2)}) collective-permute-start(bf16[2,2,512,128]{3,2,1,0:T(8,128)(2,1)S(1)} %pad_maximum_fusion.14), channel_id=1, source_target_pairs={{0,2},{1,3},{2,0},{3,1},{4,6},{5,7},{6,4},{7,5},{8,10},{9,11},{10,... | collective-permute-start | bytes 1572872 | tf_op jit(solution)/shard_map/ppermute | solution.py:149
  64.3 23.7 %collective-permute-start.14 = (bf16[2,2,512,128]{3,2,1,0:T(8,128)(2,1)S(1)}, bf16[2,2,512,128]{3,2,1,0:T(8,128)(2,1)S(1)}, u32[]{:S(2)}, u32[]{:S(2)}) collective-permute-start(bf16[2,2,512,128]{3,2,1,0:T(8,128)(2,1)S(1)} %pad_maximum_fusion.13), channel_id=1, source_target_pairs={{0,1},{1,2},{2,3},{3,0},{4,5},{5,6},{6,7},{7,4},{8,9},{9,10},{10,1... | collective-permute-start | bytes 1572872 | tf_op jit(solution)/shard_map/ppermute | solution.py:149
  65.3 22.7 %collective-permute-start.13 = (bf16[2,2,512,128]{3,2,1,0:T(8,128)(2,1)S(1)}, bf16[2,2,512,128]{3,2,1,0:T(8,128)(2,1)S(1)}, u32[]{:S(2)}, u32[]{:S(2)}) collective-permute-start(bf16[2,2,512,128]{3,2,1,0:T(8,128)(2,1)S(1)} %pad_maximum_fusion.12), channel_id=1, source_target_pairs={{0,3},{1,0},{2,1},{3,2},{4,7},{5,4},{6,5},{7,6},{8,11},{9,8},{10,9... | collective-permute-start | bytes 1572872 | tf_op jit(solution)/shard_map/ppermute | solution.py:149
  70.9 19.6 %collective-permute-start.17 = (bf16[2,2048,128]{2,1,0:T(8,128)(2,1)S(1)}, bf16[2,2048,128]{2,1,0:T(8,128)(2,1)S(1)}, u32[]{:S(2)}, u32[]{:S(2)}) collective-permute-start(bf16[2,2048,128]{2,1,0:T(8,128)(2,1)S(1)} %slice_select_fusion), channel_id=1, source_target_pairs={{0,16},{16,0},{1,17},{17,1},{2,18},{18,2},{3,19},{19,3},{4,20},{20... | collective-permute-start | bytes 3145736 | tf_op jit(solution)/shard_map/ppermute | solution.py:157
  88.2 4.2 %collective-permute-start.16 = (bf16[2,2,2048,128]{3,2,1,0:T(8,128)(2,1)S(1)}, bf16[2,2,2048,128]{3,2,1,0:T(8,128)(2,1)S(1)}, u32[]{:S(2)}, u32[]{:S(2)}) collective-permute-start(bf16[2,2,2048,128]{3,2,1,0:T(8,128)(2,1)S(1)} %pad_maximum_fusion.1), channel_id=1, source_target_pairs={{0,16},{16,0},{1,17},{17,1},{2,18},{18,2},{3,19},{19,3},{4,20},{20... | collective-permute-start | bytes 6291464 | tf_op jit(solution)/shard_map/ppermute | solution.py:155
  103.0 28.4 %collective-permute-start.19 = (f32[2,256,256]{1,2,0:T(8,128)}, f32[2,256,256]{1,2,0:T(8,128)S(1)}, u32[]{:S(2)}, u32[]{:S(2)}) collective-permute-start(f32[2,256,256]{1,2,0:T(8,128)} %copy.48), channel_id=1, source_target_pairs={{0,8},{4,12},{8,0},{12,4},{1,9},{5,13},{9,1},{13,5},{2,10},{6,14},... | collective-permute-start | bytes 1572872 | tf_op jit(solution)/shard_map/ppermute | solution.py:210
  106.8 36.2 %collective-permute-start.20 = (f32[2,256,256]{1,2,0:T(8,128)}, f32[2,256,256]{1,2,0:T(8,128)S(1)}, u32[]{:S(2)}, u32[]{:S(2)}) collective-permute-start(f32[2,256,256]{1,2,0:T(8,128)} %copy.49), channel_id=1, source_target_pairs={{0,12},{4,0},{8,4},{12,8},{1,13},{5,1},{9,5},{13,9},{2,14},{6,2},{... | collective-permute-start | bytes 1572872 | tf_op jit(solution)/shard_map/ppermute | solution.py:210
  107.5 35.6 %collective-permute-start.18 = (f32[2,256,256]{1,2,0:T(8,128)S(1)}, f32[2,256,256]{1,2,0:T(8,128)S(1)}, u32[]{:S(2)}, u32[]{:S(2)}) collective-permute-start(f32[2,256,256]{1,2,0:T(8,128)S(1)} %copy.46), channel_id=1, source_target_pairs={{0,4},{4,8},{8,12},{12,0},{1,5},{5,9},{9,13},{13,1},{2,6},{6,10},{... | collective-permute-start | bytes 1572872 | tf_op jit(solution)/shard_map/ppermute | solution.py:210
  143.2 32.7 %collective-permute-start.23 = (f32[2,256,128]{1,2,0:T(8,128)S(1)}, f32[2,256,128]{1,2,0:T(8,128)S(1)}, u32[]{:S(2)}, u32[]{:S(2)}) collective-permute-start(f32[2,256,128]{1,2,0:T(8,128)S(1)} %get-tuple-element.35), channel_id=1, source_target_pairs={{0,48},{4,80},{8,16},{12,56},{1,8},{5,32},{9,40},{13,64},{2,152},{... | collective-permute-start | bytes 786440 | tf_op jit(solution)/shard_map/ppermute | solution.py:180
  144.6 31.4 %collective-permute-start.24 = (f32[2,256,128]{1,2,0:T(8,128)S(1)}, f32[2,256,128]{1,2,0:T(8,128)S(1)}, u32[]{:S(2)}, u32[]{:S(2)}) collective-permute-start(f32[2,256,128]{1,2,0:T(8,128)S(1)} %get-tuple-element.36), channel_id=1, source_target_pairs={{0,32},{4,64},{8,8},{12,40},{1,16},{5,48},{9,56},{13,80},{2,136},{... | collective-permute-start | bytes 786440 | tf_op jit(solution)/shard_map/ppermute | solution.py:180
  151.2 30.0 %collective-permute-start.21 = (f32[2,256,128]{1,2,0:T(8,128)S(1)}, f32[2,256,128]{1,2,0:T(8,128)S(1)}, u32[]{:S(2)}, u32[]{:S(2)}) collective-permute-start(f32[2,256,128]{1,2,0:T(8,128)S(1)} %get-tuple-element.35), channel_id=1, source_target_pairs={{0,3},{4,5},{8,1},{12,131},{1,128},{5,2},{9,130},{13,4},{2,137},{6... | collective-permute-start | bytes 786440 | tf_op jit(solution)/shard_map/ppermute | solution.py:180
  163.8 48.4 %collective-permute-start.22 = (f32[2,256,128]{1,2,0:T(8,128)S(1)}, f32[2,256,128]{1,2,0:T(8,128)S(1)}, u32[]{:S(2)}, u32[]{:S(2)}) collective-permute-start(f32[2,256,128]{1,2,0:T(8,128)S(1)} %get-tuple-element.36), channel_id=1, source_target_pairs={{0,2},{4,4},{8,128},{12,130},{1,1},{5,3},{9,131},{13,5},{2,0},{6,1... | collective-permute-start | bytes 786440 | tf_op jit(solution)/shard_map/ppermute | solution.py:180

commit v5 on v4

--- a/solution.py
+++ b/solution.py
@@ -24,14 +24,21 @@
     return itertools.product(range(2), range(4), range(2), range(4))
 
 
+QUARTERS = (
+    ((0, 1, 2, 3), (0, 1, 2, 3), (0, 2, 1, 3), (2, 0, 3, 1)),
+    ((0, 1, 2, 3), (0, 1, 2, 3), (0, 2, 1, 3), (3, 1, 2, 0)),
+)
+
+
 def held_pair(f, y, core, x, block, core_col):
-    e_col = x // 2
+    e_quarter = QUARTERS[f][y][x] // 2
+    e_col = e_quarter ^ core_col
     if block < 2:
         e_row, dy = block, 1
     elif block == 2:
-        e_row, dy = (e_col if y < 2 else 1 - e_col), 2
+        e_row, dy = e_quarter ^ core ^ (y // 2), 2
     elif core_col != core:
-        e_row, dy = (e_col if core == 0 else 1 - e_col), 0
+        e_row, dy = 1 - e_quarter, 0
     elif e_col == f:
         return rcv_of(1, y, core), rcv_of(0, y, core)
     else:
@@ -42,7 +49,7 @@
 def deliveries(f, y, core, x, block):
     out = []
     for core_col in range(2):
-        j = core_col ^ (x % 2)
+        j = core_col ^ (QUARTERS[f][y][x] % 2)
         pair = held_pair(f, y, core, x, block, core_col)
         if pair is None:
             first, second = (device_of(r, r) for r in (rcv_of(f, y, core), rcv_of(1 - f, y, core)))
@@ -56,16 +63,16 @@
 
 SLOTS = (
     (
-        ((0x78, 0x93, 0x87, 0x4e), (0x72, 0xd8, 0x4e, 0x8d)),
-        ((0xe1, 0x4e, 0x93, 0x63), (0xc9, 0x72, 0x8d, 0x4e)),
-        ((0xb1, 0x87, 0x2d, 0x27), (0x93, 0xb1, 0x2d, 0x2d)),
-        ((0x6c, 0x8d, 0x93, 0x2d), (0x93, 0x93, 0xe1, 0x2d)),
+        ((0xe4, 0xb4, 0x4b, 0x4b), (0xc6, 0x4e, 0xe4, 0xe4)),
+        ((0xe1, 0xe1, 0x87, 0x27), (0xc9, 0xc9, 0xe1, 0xd8)),
+        ((0xb1, 0x2d, 0xb1, 0x2d), (0xe1, 0xc9, 0xe1, 0xc9)),
+        ((0x9c, 0x93, 0x9c, 0x93), (0xc9, 0xe4, 0xe4, 0xe4)),
     ),
     (
-        ((0x8d, 0x39, 0xb1, 0x4e), (0xc9, 0xe1, 0x72, 0x72)),
-        ((0xb1, 0x2d, 0xd2, 0xd2), (0x8d, 0x39, 0xb1, 0x72)),
-        ((0x36, 0xe1, 0x4e, 0x72), (0x39, 0xc6, 0xd2, 0x4e)),
-        ((0xb1, 0xc6, 0x4e, 0x78), (0x1b, 0xb1, 0x9c, 0x4e)),
+        ((0xe1, 0xe1, 0x72, 0x72), (0x63, 0x63, 0x78, 0x78)),
+        ((0xe1, 0xe1, 0x27, 0x39), (0x27, 0x27, 0xe1, 0xd8)),
+        ((0xe1, 0xd2, 0xb1, 0xc6), (0x4e, 0xb1, 0x27, 0x93)),
+        ((0x72, 0xc9, 0xe1, 0xe1), (0x8d, 0x6c, 0x93, 0x27)),
     ),
 )
 
@@ -125,7 +132,9 @@
     n = wavefield.shape[3]
     half = n // 2
     scale = 1.0 / jnp.sqrt(jnp.float32(wavefield.shape[2] * 16))
-    e_col, h_col = x // 2, x % 2
+    quarter_at = jnp.asarray(QUARTERS, jnp.int32)[f, y]
+    e_quarter, h_col = quarter_at[x] // 2, quarter_at[x] % 2
+    e_col = e_quarter ^ core
 
     own = lax.dynamic_index_in_dim(wavefield, f, 0, keepdims=False)
     other = lax.dynamic_index_in_dim(wavefield, 1 - f, 0, keepdims=False)
@@ -138,11 +147,11 @@
     def half_of(block, h):
         return jnp.where(h == 0, block[..., :half], block[..., half:])
 
-    def quarter(pair, place):
-        return half_of(jnp.where(place // 2 == 0, pair[0], pair[1]), place % 2)
+    def quarter(pair, number):
+        return half_of(jnp.where(number // 2 == core, pair[0], pair[1]), number % 2)
 
     def quarters(place):
-        return jnp.stack([quarter(near, place), quarter(far, place)])
+        return jnp.stack([quarter(near, quarter_at[place]), quarter(far, quarter_at[place])])
 
     pieces = [quarters(x)]
     for step in (-1, 1, 2):
@@ -159,7 +168,7 @@
     rows = jnp.concatenate([block0, block1], axis=2)
     upper = lax.broadcasted_iota(jnp.int32, (n, n), 0) <= lax.broadcasted_iota(jnp.int32, (n, n), 1)
     upper_half = half_of(upper, h_col)
-    cross = product(jnp.where((e_col == 0) == (core == 0), block0, block1), other0)
+    cross = product(jnp.where(e_quarter == 1, block0, block1), other0)
     inner = product(rows, half_of(block0, h_col))
     inner1 = product(rows, half_of(block1, h_col))
     is0 = f == 0
@@ -168,11 +177,13 @@
     block3 = both(jnp.where(e_col == f, jnp.where(is0, inner[:, n:], inner1[:, :n]), packed), cross)
 
     product1 = product(rows, cols[0])
-    product2 = product(jnp.where((e_col == 0) == (y < 2), block0, block1), cols[1])
+    product2 = product(jnp.where(e_col == y // 2, block0, block1), cols[1])
     blocks = jnp.stack([product1[:, :n], product1[:, n:], product2, block3])
 
     order = jnp.asarray(slots)[f, y, core, x]
-    held = sum_over_zl(blocks, order, zl) * scale
+    ordered = jnp.stack([lax.dynamic_index_in_dim(blocks, order[slot], 0, keepdims=False) for slot in range(BLOCKS)])
+    held = lax.psum_scatter(ordered, "zl")
+    held = held * scale
 
     def part(j):
         return jnp.where((h_col ^ j) == 0, held[..., :half], held[..., half:])
@@ -199,16 +210,6 @@
     out0 = jnp.where(case == 1, first, jnp.where(case == 0, turned(second), jnp.where(is0, diag_first, diag_second)))
     out1 = jnp.where(case == 1, second, jnp.where(case == 0, turned(first), jnp.where(is0, diag_second, diag_first)))
     return jnp.stack([out0, out1])
-
-
-def sum_over_zl(blocks, order, zl):
-    def partial_of(slot):
-        return lax.dynamic_index_in_dim(blocks, order[slot], 0, keepdims=False)
-
-    total = partial_of(zl)
-    for step in (1, 2, 3):
-        total = total + lax.ppermute(partial_of((zl + step) % 4), "zl", ring(4, step))
-    return total
 
 
 def solution(mesh):

time: 222 us -> 234 us (1.054)
  between operations: 9 us -> 33 us
  starting transfers between devices: 64 us -> 51.7 us
  waiting for transfers between devices: 108 us -> 102 us
  other arithmetic: 14 us -> 19.5 us
  matrix products: 11.7 us -> 9.36 us
    reduce_scatter x0 -> x1, waiting for transfers between devices: none -> 46.7 us  [body(): held = lax.psum_scatter(ordered, 'zl')]
    ppermute x3 -> x0, waiting for transfers between devices: 34 us -> none  [sum_over_zl(): lax.ppermute(partial_of((zl + step) % 4), 'zl', ring(4, step))]
    ppermute x4, waiting for transfers between devices: 35.4 us -> 22.1 us  [body(): lax.ppermute(part(slot % 2), AXES, perm)]
    ppermute x4, starting transfers between devices: 29.7 us -> 23.2 us  [body(): lax.ppermute(part(slot % 2), AXES, perm)]
    ppermute x3 -> x0, starting transfers between devices: 5.85 us -> none  [sum_over_zl(): lax.ppermute(partial_of((zl + step) % 4), 'zl', ring(4, step))]
    unnamed x8 -> x34, local copies, waits for them, and re-layouts: 3.19 us -> 7.73 us
    ppermute x2, waiting for transfers between devices: 9.81 us -> 5.69 us  [body(): near = [lax.ppermute(block, 'y', ring(4, -1)) for block in (own, other)]]
    select_n x2, other arithmetic: 3.44 us -> 5.98 us  [both(): jnp.where(core == 0, jnp.concatenate([a, b], -1), jnp.concatenate([b, a],...]
  transfers between devices with their start and end apart: 25 -> 23, of which waited for: 12 -> 13; matrix products, arithmetic and copies ran while one was open for 9% -> 9% of each run, Pallas kernels for 0% -> 0%
where the time goes in v5:
time: 234 us; the launch traced here: 231 us
  waiting for transfers between devices  102 us (44%)
  starting transfers between devices  51.7 us (22%)
  between operations  33 us (14%)
  other arithmetic  19.5 us (8%)
  local copies, waits for them, and re-layouts  15.9 us (7%)
  matrix products  9.36 us (4%)
    reduce_scatter x1, waiting for transfers between devices, body(): held = lax.psum_scatter(ordered, 'zl')  46.7 us
    ppermute x4, starting transfers between devices, body(): lax.ppermute(part(slot % 2), AXES, perm)  23.2 us
    ppermute x4, waiting for transfers between devices, body(): lax.ppermute(part(slot % 2), AXES, perm)  22.1 us
    ppermute x3, waiting for transfers between devices, body(): pieces.append(lax.ppermute(quarters((x + step) % 4), 'x', ring(4, step)))  13.2 us
    unnamed x34, local copies, waits for them, and re-layouts  7.73 us
    ppermute x2, waiting for transfers between devices, gather_x(): below = lax.ppermute(block, 'x', ring(4, 1))  7.41 us
    ppermute x1, starting transfers between devices, body(): other = lax.ppermute(other, 'zh', ring(2, 1))  7.19 us
    ppermute x2, starting transfers between devices, gather_x(): far_a = lax.ppermute(above[:, :half], 'x', ring(4, -1))  6.7 us
  transfers between devices with their start and end apart: 23, of which 13 were waited for; matrix products, arithmetic and copies ran while one was open for 9% of the time, Pallas kernels for 0%

profile of v5, /device:TPU:16, one launch (start us, length us, event | category | flops | bytes accessed | tf_op | source)
XLA Modules:
  0.0 231.1 jit_solution(7882229324632002360)
XLA Ops:
  6.5 1.9 constant_dynamic-update-slice_fusion.4
  8.5 1.5 collective-permute-start.1
  9.9 1.7 collective-permute-start
  11.7 1.9 dynamic-slice_bitcast_fusion
  13.6 7.2 %collective-permute-start.4 = (bf16[2,512,256]{2,1,0:T(8,128)(2,1)}, bf16[2,512,256]{2,1,0:T(8,128)(2,1)}, u32[]{:S(2)}, u32[]{:S(2)}) collective-permute-start(bf16[2,512,256]{2,1,0:T(8,128)(2,1)} %dynamic-slice_bitcast_fusion), channel_id=1, source_target_pairs={{0,128},{128,0},{1,129},{129,1},{2,130},{130,2},{3,131},{131,3},{4... | collective-permute-start | bytes 1572872 | tf_op jit(solution)/shard_map/ppermute | solution.py:141
  21.2 2.9 %collective-permute-start.11 = (bf16[2,512,256]{2,1,0:T(8,128)(2,1)}, bf16[2,512,256]{2,1,0:T(8,128)(2,1)}, u32[]{:S(2)}, u32[]{:S(2)}) collective-permute-start(bf16[2,512,256]{2,1,0:T(8,128)(2,1)} %get-tuple-element.10), channel_id=1, source_target_pairs={{0,64},{32,96},{64,0},{96,32},{1,65},{33,97},{65,1},{97,33},{2,66}... | collective-permute-start | bytes 1572872 | tf_op jit(solution)/shard_map/ppermute | solution.py:144
  44.3 3.0 %collective-permute-start.2 = (bf16[2,256,256]{2,1,0:T(8,128)(2,1)S(1)}, bf16[2,256,256]{2,1,0:T(8,128)(2,1)S(1)}, u32[]{:S(2)}, u32[]{:S(2)}) collective-permute-start(bf16[2,256,256]{2,1,0:T(8,128)(2,1)S(1)} %slice.292), channel_id=1, source_target_pairs={{0,3},{1,0},{2,1},{3,2},{4,7},{5,4},{6,5},{7,6},{8,11},{9,8},{10,9... | collective-permute-start | bytes 786440 | tf_op jit(solution)/shard_map/ppermute | solution.py:115
  48.5 2.7 %collective-permute-done.2 = bf16[2,256,256]{2,1,0:T(8,128)(2,1)S(1)} collective-permute-done((bf16[2,256,256]{2,1,0:T(8,128)(2,1)S(1)}, bf16[2,256,256]{2,1,0:T(8,128)(2,1)S(1)}, u32[]{:S(2)}, u32[]{:S(2)}) %collective-permute-start.2) | collective-permute-done | bytes 262176 | tf_op jit(solution)/shard_map/ppermute | solution.py:115
  51.8 2.6 %collective-permute-done.3 = bf16[2,256,256]{2,1,0:T(8,128)(2,1)S(1)} collective-permute-done((bf16[2,256,256]{2,1,0:T(8,128)(2,1)S(1)}, bf16[2,256,256]{2,1,0:T(8,128)(2,1)S(1)}, u32[]{:S(2)}, u32[]{:S(2)}) %collective-permute-start.3) | collective-permute-done | bytes 262176 | tf_op jit(solution)/shard_map/ppermute | solution.py:116
  55.6 7.4 %collective-permute-done.6 = bf16[2,512,256]{2,1,0:T(8,128)(2,1)S(1)} collective-permute-done((bf16[2,512,256]{2,1,0:T(8,128)(2,1)}, bf16[2,512,256]{2,1,0:T(8,128)(2,1)S(1)}, u32[]{:S(2)}, u32[]{:S(2)}) %collective-permute-start.6) | collective-permute-done | bytes 524320 | tf_op jit(solution)/shard_map/ppermute | solution.py:114
  64.0 3.7 %collective-permute-start.7 = (bf16[2,256,256]{2,1,0:T(8,128)(2,1)S(1)}, bf16[2,256,256]{2,1,0:T(8,128)(2,1)S(1)}, u32[]{:S(2)}, u32[]{:S(2)}) collective-permute-start(bf16[2,256,256]{2,1,0:T(8,128)(2,1)S(1)} %slice.294), channel_id=1, source_target_pairs={{0,3},{1,0},{2,1},{3,2},{4,7},{5,4},{6,5},{7,6},{8,11},{9,8},{10,9... | collective-permute-start | bytes 786440 | tf_op jit(solution)/shard_map/ppermute | solution.py:115
  68.9 5.7 %collective-permute-done.10 = bf16[2,512,256]{2,1,0:T(8,128)(2,1)S(1)} collective-permute-done((bf16[2,512,256]{2,1,0:T(8,128)(2,1)}, bf16[2,512,256]{2,1,0:T(8,128)(2,1)S(1)}, u32[]{:S(2)}, u32[]{:S(2)}) %collective-permute-start.10) | collective-permute-done | bytes 524320 | tf_op jit(solution)/shard_map/ppermute | solution.py:143
  75.9 1.7 collective-permute-start.15
  77.7 2.3 collective-permute-start.14
  80.1 1.3 collective-permute-start.13
  84.2 1.8 broadcast_select_fusion.2
  87.6 4.8 %collective-permute-done.15 = bf16[2,2,512,128]{3,2,1,0:T(8,128)(2,1)S(1)} collective-permute-done((bf16[2,2,512,128]{3,2,1,0:T(8,128)(2,1)S(1)}, bf16[2,2,512,128]{3,2,1,0:T(8,128)(2,1)S(1)}, u32[]{:S(2)}, u32[]{:S(2)}) %collective-permute-start.15) | collective-permute-done | bytes 524320 | tf_op jit(solution)/shard_map/ppermute | solution.py:158
  92.4 6.8 %collective-permute-done.14 = bf16[2,2,512,128]{3,2,1,0:T(8,128)(2,1)S(1)} collective-permute-done((bf16[2,2,512,128]{3,2,1,0:T(8,128)(2,1)S(1)}, bf16[2,2,512,128]{3,2,1,0:T(8,128)(2,1)S(1)}, u32[]{:S(2)}, u32[]{:S(2)}) %collective-permute-start.14) | collective-permute-done | bytes 524320 | tf_op jit(solution)/shard_map/ppermute | solution.py:158
  99.2 1.6 collective-permute-done.13
  100.8 1.6 pad_maximum_fusion.1
  107.2 5.9 %maximum_select_fusion = bf16[2,2,2048,256]{3,2,1,0:T(8,128)(2,1)S(1)} fusion(bf16[2,2,2048,128]{3,2,1,0:T(8,128)(2,1)} %collective-permute-done.16, bf16[2,2,512,128]{3,2,1,0:T(8,128)(2,1)} %copy-done.7, bf16[2,2,512,128]{3,2,1,0:T(8,128)(2,1)} %copy-done.8, bf16[2,2,512,128]{3,2,1,0:T(8,128)(2,1)} %copy-done.9, ...), kind=kLoop, calls=%fused_computation.5 | loop fusion | flops 52428800 | bytes 8388609 | tf_op jit(solution)/shard_map/jit(_where)/select_n | solution.py:162
  113.1 1.3 fusion.7
  121.0 1.5 pad_maximum_fusion.3
  122.5 46.7 %reduce-scatter.2.cloned.1.call-done = f32[1,2,256,256]{3,2,1,0:T(8,128)} async-done(((f32[4,2,256,256]{3,2,1,0:T(8,128)}), f32[1,2,256,256]{3,2,1,0:T(8,128)}) %reduce-scatter.2.cloned.1.call-update) | async-done | bytes 524304 | tf_op jit(solution)/shard_map/reduce_scatter | solution.py:185
  171.1 6.0 %collective-permute-start.20 = (f32[2,256,128]{2,1,0:T(8,128)}, f32[2,256,128]{2,1,0:T(8,128)S(1)}, u32[]{:S(2)}, u32[]{:S(2)}) collective-permute-start(f32[2,256,128]{2,1,0:T(8,128)} %get-tuple-element.36), channel_id=1, source_target_pairs={{0,176},{4,184},{8,208},{12,152},{1,32},{5,40},{9,8},{13,64},{2,16... | collective-permute-start | bytes 786440 | tf_op jit(solution)/shard_map/ppermute | solution.py:191
  177.1 2.5 %collective-permute-start.21 = (f32[2,256,128]{2,1,0:T(8,128)}, f32[2,256,128]{2,1,0:T(8,128)S(1)}, u32[]{:S(2)}, u32[]{:S(2)}) collective-permute-start(f32[2,256,128]{2,1,0:T(8,128)} %get-tuple-element.37), channel_id=1, source_target_pairs={{0,32},{4,40},{8,64},{12,8},{1,176},{5,184},{9,152},{13,208},{2,13... | collective-permute-start | bytes 786440 | tf_op jit(solution)/shard_map/ppermute | solution.py:191
  179.7 1.3 dynamic_slice.45
  182.4 4.4 %collective-permute-start.18 = (f32[2,256,128]{2,1,0:T(8,128)}, f32[2,256,128]{2,1,0:T(8,128)S(1)}, u32[]{:S(2)}, u32[]{:S(2)}) collective-permute-start(f32[2,256,128]{2,1,0:T(8,128)} %get-tuple-element.36), channel_id=1, source_target_pairs={{0,11},{4,139},{8,13},{12,137},{1,2},{5,130},{9,128},{13,4},{2,1},... | collective-permute-start | bytes 786440 | tf_op jit(solution)/shard_map/ppermute | solution.py:191
  186.8 10.3 %collective-permute-start.19 = (f32[2,256,128]{2,1,0:T(8,128)}, f32[2,256,128]{2,1,0:T(8,128)S(1)}, u32[]{:S(2)}, u32[]{:S(2)}) collective-permute-start(f32[2,256,128]{2,1,0:T(8,128)} %get-tuple-element.37), channel_id=1, source_target_pairs={{0,2},{4,130},{8,4},{12,128},{1,11},{5,139},{9,137},{13,13},{2,0},... | collective-permute-start | bytes 786440 | tf_op jit(solution)/shard_map/ppermute | solution.py:191
  197.1 11.5 %collective-permute-done.20 = f32[2,256,128]{2,1,0:T(8,128)S(1)} collective-permute-done((f32[2,256,128]{2,1,0:T(8,128)}, f32[2,256,128]{2,1,0:T(8,128)S(1)}, u32[]{:S(2)}, u32[]{:S(2)}) %collective-permute-start.20) | collective-permute-done | bytes 262176 | tf_op jit(solution)/shard_map/ppermute | solution.py:191
  209.5 4.9 %collective-permute-done.18 = f32[2,256,128]{2,1,0:T(8,128)S(1)} collective-permute-done((f32[2,256,128]{2,1,0:T(8,128)}, f32[2,256,128]{2,1,0:T(8,128)S(1)}, u32[]{:S(2)}, u32[]{:S(2)}) %collective-permute-start.18) | collective-permute-done | bytes 262176 | tf_op jit(solution)/shard_map/ppermute | solution.py:191
  214.5 5.6 %collective-permute-done.19 = f32[2,256,128]{2,1,0:T(8,128)S(1)} collective-permute-done((f32[2,256,128]{2,1,0:T(8,128)}, f32[2,256,128]{2,1,0:T(8,128)S(1)}, u32[]{:S(2)}, u32[]{:S(2)}) %collective-permute-start.19) | collective-permute-done | bytes 262176 | tf_op jit(solution)/shard_map/ppermute | solution.py:191
  (130 shorter events, 32.0 us)
Async XLA Ops:
  6.5 17.6 %copy-start.12 = (s32[2,4,4]{2,1,0:T(4,128)S(1)}, s32[2,4,4]{2,1,0:T(4,128)}, u32[]{:S(2)}) copy-start(s32[2,4,4]{2,1,0:T(4,128)} %constant.227.clone) | copy-start | bytes 388
  6.5 162.7 %reduce-scatter.2.cloned.1.call-start = ((), (), s32[]{:S(2)}) async-start(), calls=%async_computation.1 | async-start | bytes 2621440 | tf_op jit(solution)/shard_map/reduce_scatter | solution.py:185
  8.5 35.4 %collective-permute-start.1 = (bf16[2,512,256]{2,1,0:T(8,128)(2,1)}, bf16[2,512,256]{2,1,0:T(8,128)(2,1)S(1)}, u32[]{:S(2)}, u32[]{:S(2)}) collective-permute-start(bf16[2,512,256]{2,1,0:T(8,128)(2,1)} %get-tuple-element.10), channel_id=1, source_target_pairs={{0,1},{1,2},{2,3},{3,0},{4,5},{5,6},{6,7},{7,4},{8,9},{9,10},{10,1... | collective-permute-start | bytes 1572872 | tf_op jit(solution)/shard_map/ppermute | solution.py:114
  9.9 34.3 %collective-permute-start = (bf16[2,512,256]{2,1,0:T(8,128)(2,1)}, bf16[2,512,256]{2,1,0:T(8,128)(2,1)S(1)}, u32[]{:S(2)}, u32[]{:S(2)}) collective-permute-start(bf16[2,512,256]{2,1,0:T(8,128)(2,1)} %get-tuple-element.10), channel_id=1, source_target_pairs={{0,3},{1,0},{2,1},{3,2},{4,7},{5,4},{6,5},{7,6},{8,11},{9,8},{10,9... | collective-permute-start | bytes 1572872 | tf_op jit(solution)/shard_map/ppermute | solution.py:113
  13.6 33.7 %collective-permute-start.4 = (bf16[2,512,256]{2,1,0:T(8,128)(2,1)}, bf16[2,512,256]{2,1,0:T(8,128)(2,1)}, u32[]{:S(2)}, u32[]{:S(2)}) collective-permute-start(bf16[2,512,256]{2,1,0:T(8,128)(2,1)} %dynamic-slice_bitcast_fusion), channel_id=1, source_target_pairs={{0,128},{128,0},{1,129},{129,1},{2,130},{130,2},{3,131},{131,3},{4... | collective-permute-start | bytes 1572872 | tf_op jit(solution)/shard_map/ppermute | solution.py:141
  20.8 48.1 %collective-permute-start.9 = (bf16[2,512,256]{2,1,0:T(8,128)(2,1)}, bf16[2,512,256]{2,1,0:T(8,128)(2,1)}, u32[]{:S(2)}, u32[]{:S(2)}) collective-permute-start(bf16[2,512,256]{2,1,0:T(8,128)(2,1)} %get-tuple-element.10), channel_id=1, source_target_pairs={{0,96},{32,0},{64,32},{96,64},{1,97},{33,1},{65,33},{97,65},{2,98}... | collective-permute-start | bytes 1572872 | tf_op jit(solution)/shard_map/ppermute | solution.py:143
  21.2 42.8 %collective-permute-start.11 = (bf16[2,512,256]{2,1,0:T(8,128)(2,1)}, bf16[2,512,256]{2,1,0:T(8,128)(2,1)}, u32[]{:S(2)}, u32[]{:S(2)}) collective-permute-start(bf16[2,512,256]{2,1,0:T(8,128)(2,1)} %get-tuple-element.10), channel_id=1, source_target_pairs={{0,64},{32,96},{64,0},{96,32},{1,65},{33,97},{65,1},{97,33},{2,66}... | collective-permute-start | bytes 1572872 | tf_op jit(solution)/shard_map/ppermute | solution.py:144
  43.9 10.5 %collective-permute-start.3 = (bf16[2,256,256]{2,1,0:T(8,128)(2,1)S(1)}, bf16[2,256,256]{2,1,0:T(8,128)(2,1)S(1)}, u32[]{:S(2)}, u32[]{:S(2)}) collective-permute-start(bf16[2,256,256]{2,1,0:T(8,128)(2,1)S(1)} %slice.293), channel_id=1, source_target_pairs={{0,1},{1,2},{2,3},{3,0},{4,5},{5,6},{6,7},{7,4},{8,9},{9,10},{10,1... | collective-permute-start | bytes 786440 | tf_op jit(solution)/shard_map/ppermute | solution.py:116
  44.3 6.9 %collective-permute-start.2 = (bf16[2,256,256]{2,1,0:T(8,128)(2,1)S(1)}, bf16[2,256,256]{2,1,0:T(8,128)(2,1)S(1)}, u32[]{:S(2)}, u32[]{:S(2)}) collective-permute-start(bf16[2,256,256]{2,1,0:T(8,128)(2,1)S(1)} %slice.292), channel_id=1, source_target_pairs={{0,3},{1,0},{2,1},{3,2},{4,7},{5,4},{6,5},{7,6},{8,11},{9,8},{10,9... | collective-permute-start | bytes 786440 | tf_op jit(solution)/shard_map/ppermute | solution.py:115
  47.3 15.7 %collective-permute-start.6 = (bf16[2,512,256]{2,1,0:T(8,128)(2,1)}, bf16[2,512,256]{2,1,0:T(8,128)(2,1)S(1)}, u32[]{:S(2)}, u32[]{:S(2)}) collective-permute-start(bf16[2,512,256]{2,1,0:T(8,128)(2,1)} %collective-permute-done.4), channel_id=1, source_target_pairs={{0,1},{1,2},{2,3},{3,0},{4,5},{5,6},{6,7},{7,4},{8,9},{9,10},{10,1... | collective-permute-start | bytes 1572872 | tf_op jit(solution)/shard_map/ppermute | solution.py:114
  51.2 16.5 %collective-permute-start.12 = (bf16[2,512,256]{2,1,0:T(8,128)(2,1)}, bf16[2,512,256]{2,1,0:T(8,128)(2,1)S(1)}, u32[]{:S(2)}, u32[]{:S(2)}) collective-permute-start(bf16[2,512,256]{2,1,0:T(8,128)(2,1)} %collective-permute-done.4), channel_id=1, source_target_pairs={{0,64},{32,96},{64,0},{96,32},{1,65},{33,97},{65,1},{97,33},{2,66}... | collective-permute-start | bytes 1572872 | tf_op jit(solution)/shard_map/ppermute | solution.py:144
  54.4 9.6 %collective-permute-start.5 = (bf16[2,512,256]{2,1,0:T(8,128)(2,1)}, bf16[2,512,256]{2,1,0:T(8,128)(2,1)S(1)}, u32[]{:S(2)}, u32[]{:S(2)}) collective-permute-start(bf16[2,512,256]{2,1,0:T(8,128)(2,1)} %collective-permute-done.4), channel_id=1, source_target_pairs={{0,3},{1,0},{2,1},{3,2},{4,7},{5,4},{6,5},{7,6},{8,11},{9,8},{10,9... | collective-permute-start | bytes 1572872 | tf_op jit(solution)/shard_map/ppermute | solution.py:113
  63.1 11.5 %collective-permute-start.10 = (bf16[2,512,256]{2,1,0:T(8,128)(2,1)}, bf16[2,512,256]{2,1,0:T(8,128)(2,1)S(1)}, u32[]{:S(2)}, u32[]{:S(2)}) collective-permute-start(bf16[2,512,256]{2,1,0:T(8,128)(2,1)} %collective-permute-done.4), channel_id=1, source_target_pairs={{0,96},{32,0},{64,32},{96,64},{1,97},{33,1},{65,33},{97,65},{2,98}... | collective-permute-start | bytes 1572872 | tf_op jit(solution)/shard_map/ppermute | solution.py:143
  64.0 17.6 %collective-permute-start.8 = (bf16[2,256,256]{2,1,0:T(8,128)(2,1)S(1)}, bf16[2,256,256]{2,1,0:T(8,128)(2,1)S(1)}, u32[]{:S(2)}, u32[]{:S(2)}) collective-permute-start(bf16[2,256,256]{2,1,0:T(8,128)(2,1)S(1)} %slice.295), channel_id=1, source_target_pairs={{0,1},{1,2},{2,3},{3,0},{4,5},{5,6},{6,7},{7,4},{8,9},{9,10},{10,1... | collective-permute-start | bytes 786440 | tf_op jit(solution)/shard_map/ppermute | solution.py:116
  64.0 17.6 %collective-permute-start.7 = (bf16[2,256,256]{2,1,0:T(8,128)(2,1)S(1)}, bf16[2,256,256]{2,1,0:T(8,128)(2,1)S(1)}, u32[]{:S(2)}, u32[]{:S(2)}) collective-permute-start(bf16[2,256,256]{2,1,0:T(8,128)(2,1)S(1)} %slice.294), channel_id=1, source_target_pairs={{0,3},{1,0},{2,1},{3,2},{4,7},{5,4},{6,5},{7,6},{8,11},{9,8},{10,9... | collective-permute-start | bytes 786440 | tf_op jit(solution)/shard_map/ppermute | solution.py:115
  75.9 16.5 %collective-permute-start.15 = (bf16[2,2,512,128]{3,2,1,0:T(8,128)(2,1)S(1)}, bf16[2,2,512,128]{3,2,1,0:T(8,128)(2,1)S(1)}, u32[]{:S(2)}, u32[]{:S(2)}) collective-permute-start(bf16[2,2,512,128]{3,2,1,0:T(8,128)(2,1)S(1)} %pad_maximum_fusion.15), channel_id=1, source_target_pairs={{0,2},{1,3},{2,0},{3,1},{4,6},{5,7},{6,4},{7,5},{8,10},{9,11},{10,... | collective-permute-start | bytes 1572872 | tf_op jit(solution)/shard_map/ppermute | solution.py:158
  77.7 21.4 %collective-permute-start.14 = (bf16[2,2,512,128]{3,2,1,0:T(8,128)(2,1)S(1)}, bf16[2,2,512,128]{3,2,1,0:T(8,128)(2,1)S(1)}, u32[]{:S(2)}, u32[]{:S(2)}) collective-permute-start(bf16[2,2,512,128]{3,2,1,0:T(8,128)(2,1)S(1)} %pad_maximum_fusion.14), channel_id=1, source_target_pairs={{0,1},{1,2},{2,3},{3,0},{4,5},{5,6},{6,7},{7,4},{8,9},{9,10},{10,1... | collective-permute-start | bytes 1572872 | tf_op jit(solution)/shard_map/ppermute | solution.py:158
  80.1 20.7 %collective-permute-start.13 = (bf16[2,2,512,128]{3,2,1,0:T(8,128)(2,1)S(1)}, bf16[2,2,512,128]{3,2,1,0:T(8,128)(2,1)S(1)}, u32[]{:S(2)}, u32[]{:S(2)}) collective-permute-start(bf16[2,2,512,128]{3,2,1,0:T(8,128)(2,1)S(1)} %pad_maximum_fusion.13), channel_id=1, source_target_pairs={{0,3},{1,0},{2,1},{3,2},{4,7},{5,4},{6,5},{7,6},{8,11},{9,8},{10,9... | collective-permute-start | bytes 1572872 | tf_op jit(solution)/shard_map/ppermute | solution.py:158
  81.7 21.5 %copy-start = (bf16[2,2048,256]{2,1,0:T(8,128)(2,1)}, bf16[2,2048,256]{2,1,0:T(8,128)(2,1)S(1)}, u32[]{:S(2)}) copy-start(bf16[2,2048,256]{2,1,0:T(8,128)(2,1)S(1)} %constant_dynamic-update-slice_fusion.5) | copy-start | bytes 6291460
  82.2 20.4 %copy-start.2 = (bf16[2048,512]{1,0:T(8,128)(2,1)}, bf16[2048,512]{1,0:T(8,128)(2,1)S(1)}, u32[]{:S(2)}) copy-start(bf16[2048,512]{1,0:T(8,128)(2,1)S(1)} %get-tuple-element.14) | copy-start | bytes 6291460
  86.2 18.1 %collective-permute-start.17 = (bf16[2,2048,128]{2,1,0:T(8,128)(2,1)S(1)}, bf16[2,2048,128]{2,1,0:T(8,128)(2,1)S(1)}, u32[]{:S(2)}, u32[]{:S(2)}) collective-permute-start(bf16[2,2048,128]{2,1,0:T(8,128)(2,1)S(1)} %slice_select_fusion), channel_id=1, source_target_pairs={{0,16},{16,0},{1,17},{17,1},{2,18},{18,2},{3,19},{19,3},{4,20},{20... | collective-permute-start | bytes 3145736 | tf_op jit(solution)/shard_map/ppermute | solution.py:166
  92.4 9.9 %copy-start.7 = (bf16[2,2,512,128]{3,2,1,0:T(8,128)(2,1)}, bf16[2,2,512,128]{3,2,1,0:T(8,128)(2,1)S(1)}, u32[]{:S(2)}) copy-start(bf16[2,2,512,128]{3,2,1,0:T(8,128)(2,1)S(1)} %collective-permute-done.15) | copy-start | bytes 1572868
  99.2 3.2 %copy-start.8 = (bf16[2,2,512,128]{3,2,1,0:T(8,128)(2,1)}, bf16[2,2,512,128]{3,2,1,0:T(8,128)(2,1)S(1)}, u32[]{:S(2)}) copy-start(bf16[2,2,512,128]{3,2,1,0:T(8,128)(2,1)S(1)} %collective-permute-done.14) | copy-start | bytes 1572868
  100.8 1.6 copy-start.9
  102.4 4.8 %collective-permute-start.16 = (bf16[2,2,2048,128]{3,2,1,0:T(8,128)(2,1)}, bf16[2,2,2048,128]{3,2,1,0:T(8,128)(2,1)}, u32[]{:S(2)}, u32[]{:S(2)}) collective-permute-start(bf16[2,2,2048,128]{3,2,1,0:T(8,128)(2,1)} %pad_maximum_fusion.1), channel_id=1, source_target_pairs={{0,16},{16,0},{1,17},{17,1},{2,18},{18,2},{3,19},{19,3},{4,20},{20... | collective-permute-start | bytes 6291464 | tf_op jit(solution)/shard_map/ppermute | solution.py:164
  106.6 6.6 %copy-start.1 = (bf16[2,2048,256]{2,1,0:T(8,128)(2,1)S(1)}, bf16[2,2048,256]{2,1,0:T(8,128)(2,1)}, u32[]{:S(2)}) copy-start(bf16[2,2048,256]{2,1,0:T(8,128)(2,1)} %copy-done) | copy-start | bytes 6291460
  113.1 1.6 copy-start.6
  116.8 1.6 copy-start.3
  171.1 37.5 %collective-permute-start.20 = (f32[2,256,128]{2,1,0:T(8,128)}, f32[2,256,128]{2,1,0:T(8,128)S(1)}, u32[]{:S(2)}, u32[]{:S(2)}) collective-permute-start(f32[2,256,128]{2,1,0:T(8,128)} %get-tuple-element.36), channel_id=1, source_target_pairs={{0,176},{4,184},{8,208},{12,152},{1,32},{5,40},{9,8},{13,64},{2,16... | collective-permute-start | bytes 786440 | tf_op jit(solution)/shard_map/ppermute | solution.py:191
  177.1 31.5 %collective-permute-start.21 = (f32[2,256,128]{2,1,0:T(8,128)}, f32[2,256,128]{2,1,0:T(8,128)S(1)}, u32[]{:S(2)}, u32[]{:S(2)}) collective-permute-start(f32[2,256,128]{2,1,0:T(8,128)} %get-tuple-element.37), channel_id=1, source_target_pairs={{0,32},{4,40},{8,64},{12,8},{1,176},{5,184},{9,152},{13,208},{2,13... | collective-permute-start | bytes 786440 | tf_op jit(solution)/shard_map/ppermute | solution.py:191
  182.4 32.1 %collective-permute-start.18 = (f32[2,256,128]{2,1,0:T(8,128)}, f32[2,256,128]{2,1,0:T(8,128)S(1)}, u32[]{:S(2)}, u32[]{:S(2)}) collective-permute-start(f32[2,256,128]{2,1,0:T(8,128)} %get-tuple-element.36), channel_id=1, source_target_pairs={{0,11},{4,139},{8,13},{12,137},{1,2},{5,130},{9,128},{13,4},{2,1},... | collective-permute-start | bytes 786440 | tf_op jit(solution)/shard_map/ppermute | solution.py:191
  186.8 33.3 %collective-permute-start.19 = (f32[2,256,128]{2,1,0:T(8,128)}, f32[2,256,128]{2,1,0:T(8,128)S(1)}, u32[]{:S(2)}, u32[]{:S(2)}) collective-permute-start(f32[2,256,128]{2,1,0:T(8,128)} %get-tuple-element.37), channel_id=1, source_target_pairs={{0,2},{4,130},{8,4},{12,128},{1,11},{5,139},{9,137},{13,13},{2,0},... | collective-permute-start | bytes 786440 | tf_op jit(solution)/shard_map/ppermute | solution.py:191
  (4 other events, 4.8 us)
Sparse Core Ops, SparseCore 0:
  122.6 46.5 reduce-scatter.1

commit v6 on v5

--- a/solution.py
+++ b/solution.py
@@ -117,13 +117,15 @@
     return jnp.concatenate([block, above, below, far_a, far_b], axis=1)
 
 
-def dot(rows, cols):
-    return lax.dot_general(rows, cols, (((0,), (0,)), ((), ())), preferred_element_type=jnp.float32)
+def first_of(value, *after):
+    return lax.optimization_barrier((value, *after))[0]
 
 
 def product(rows, cols):
-    real = jnp.einsum("psm,psn->mn", rows, cols, preferred_element_type=jnp.float32)
-    return jnp.stack([real, dot(rows[0], cols[1]) - dot(rows[1], cols[0])])
+    n = cols.shape[2]
+    turned = jnp.stack([jnp.concatenate([cols[0], cols[1]], -1), jnp.concatenate([cols[1], -cols[0]], -1)])
+    both = jnp.einsum("psm,psn->mn", rows, turned, preferred_element_type=jnp.float32)
+    return jnp.stack([both[:, :n], both[:, n:]])
 
 
 def body(wavefield):
@@ -136,8 +138,8 @@
     e_quarter, h_col = quarter_at[x] // 2, quarter_at[x] % 2
     e_col = e_quarter ^ core
 
-    own = lax.dynamic_index_in_dim(wavefield, f, 0, keepdims=False)
     other = lax.dynamic_index_in_dim(wavefield, 1 - f, 0, keepdims=False)
+    own = lax.dynamic_index_in_dim(first_of(wavefield, other), f, 0, keepdims=False)
     other = lax.ppermute(other, "zh", ring(2, 1))
 
     near = [lax.ppermute(block, "y", ring(4, -1)) for block in (own, other)]
@@ -158,37 +160,42 @@
         pieces.append(lax.ppermute(quarters((x + step) % 4), "x", ring(4, step)))
     mine = jnp.concatenate(pieces, axis=2)
 
-    def both(a, b):
-        return jnp.where(core == 0, jnp.concatenate([a, b], -1), jnp.concatenate([b, a], -1))
-
-    cols = both(mine, lax.ppermute(mine, "core", ring(2, 1)))
+    theirs = lax.ppermute(mine, "core", ring(2, 1))
     mine0 = half_of(jnp.where(e_col == 0, block0, block1), h_col)
-    other0 = lax.ppermute(mine0, "core", ring(2, 1))
+    theirs0 = lax.ppermute(mine0, "core", ring(2, 1))
 
     rows = jnp.concatenate([block0, block1], axis=2)
     upper = lax.broadcasted_iota(jnp.int32, (n, n), 0) <= lax.broadcasted_iota(jnp.int32, (n, n), 1)
     upper_half = half_of(upper, h_col)
-    cross = product(jnp.where(e_quarter == 1, block0, block1), other0)
-    inner = product(rows, half_of(block0, h_col))
+    cross = product(jnp.where(e_quarter == 1, block0, block1), theirs0)
+    inner0 = product(rows, half_of(block0, h_col))
     inner1 = product(rows, half_of(block1, h_col))
     is0 = f == 0
-    diag0, diag1 = jnp.where(is0, inner[:, :n], inner1[:, n:]), jnp.where(is0, inner1[:, n:], inner[:, :n])
+    diag0, diag1 = jnp.where(is0, inner0[:, :n], inner1[:, n:]), jnp.where(is0, inner1[:, n:], inner0[:, :n])
     packed = jnp.stack([jnp.where(upper_half, d[0], d[1]) for d in (diag0, diag1)])
-    block3 = both(jnp.where(e_col == f, jnp.where(is0, inner[:, n:], inner1[:, :n]), packed), cross)
-
-    product1 = product(rows, cols[0])
-    product2 = product(jnp.where(e_col == y // 2, block0, block1), cols[1])
-    blocks = jnp.stack([product1[:, :n], product1[:, n:], product2, block3])
-
+    inner = jnp.where(e_col == f, jnp.where(is0, inner0[:, n:], inner1[:, :n]), packed)
+
+    rows2 = jnp.where(e_col == y // 2, block0, block1)
     order = jnp.asarray(slots)[f, y, core, x]
-    ordered = jnp.stack([lax.dynamic_index_in_dim(blocks, order[slot], 0, keepdims=False) for slot in range(BLOCKS)])
-    held = lax.psum_scatter(ordered, "zl")
-    held = held * scale
-
-    def part(j):
-        return jnp.where((h_col ^ j) == 0, held[..., :half], held[..., half:])
-
-    got = [lax.ppermute(part(slot % 2), AXES, perm) for slot, perm in enumerate(perms)]
+    arrived = []
+    got = []
+    for j in range(2):
+        ours = (j ^ h_col) == core
+        cols = jnp.where(ours, mine, theirs)
+        product1 = product(rows, cols[0])
+        blocks = jnp.stack(
+            [product1[:, :n], product1[:, n:], product(rows2, cols[1]), jnp.where(ours, inner, cross)]
+        )
+        if j == 1:
+            blocks = first_of(blocks, *arrived)
+
+        def partial_of(slot, blocks=blocks):
+            return lax.dynamic_index_in_dim(blocks, order[slot], 0, keepdims=False)
+
+        arrived = [lax.ppermute(partial_of((zl + step) % 4), "zl", ring(4, step)) for step in (1, 2, 3)]
+        held = (partial_of(zl) + arrived[0] + arrived[1] + arrived[2]) * scale
+        got.append([lax.ppermute(held, AXES, perms[2 * kind + j]) for kind in range(2)])
+
     row, col = rcv_of(f, y, core), zl * 4 + x
     case = jnp.asarray(case_of)[row, col]
     swapped = jnp.where(case == 0, row, col) % 2 == 1
@@ -196,7 +203,7 @@
     def joined(a, b):
         return jnp.where(swapped, jnp.concatenate([b, a], -1), jnp.concatenate([a, b], -1))
 
-    first, second = joined(got[0], got[1]), joined(got[2], got[3])
+    first, second = (joined(got[0][kind], got[1][kind]) for kind in range(2))
 
     def unpack(packed):
         strict = lax.broadcasted_iota(jnp.int32, (n, n), 0) < lax.broadcasted_iota(jnp.int32, (n, n), 1)

time: 234 us -> 214 us (0.915)
  the two profiles are of different devices: /device:TPU:16 before, /device:TPU:96 now
where the time goes in v6:
time: 214 us; the launch traced here: 213 us
  waiting for transfers between devices  102 us (48%)
  starting transfers between devices  52.9 us (25%)
  between operations  19.7 us (9%)
  local copies, waits for them, and re-layouts  16.8 us (8%)
  other arithmetic  13.5 us (6%)
  matrix products  8.46 us (4%)
    ppermute x6, waiting for transfers between devices, body(): lax.ppermute(partial_of((zl + step) % 4), 'zl', ring(4, step))  44.5 us
    ppermute x4, waiting for transfers between devices, body(): lax.ppermute(held, AXES, perms[2 * kind + j])  24 us
    ppermute x2, waiting for transfers between devices, gather_x(): far_a = lax.ppermute(above[:, :half], 'x', ring(4, -1))  22 us
    ppermute x4, starting transfers between devices, body(): lax.ppermute(held, AXES, perms[2 * kind + j])  13.6 us
    dot_general x7, matrix products, product(): jnp.einsum('psm,psn->mn', rows, turned, preferred_element_type=jnp.float32)  8.46 us
    ppermute x6, starting transfers between devices, body(): lax.ppermute(partial_of((zl + step) % 4), 'zl', ring(4, step))  8.31 us
    ppermute x2, starting transfers between devices, gather_x(): above = lax.ppermute(block, 'x', ring(4, -1))  5.94 us
    ppermute x3, starting transfers between devices, body(): pieces.append(lax.ppermute(quarters((x + step) % 4), 'x', ring(4, step)))  5.59 us
  transfers between devices with their start and end apart: 28, of which 11 were waited for; matrix products, arithmetic and copies ran while one was open for 9% of the time, Pallas kernels for 0%

profile of v6, /device:TPU:96, one launch (start us, length us, event | category | flops | bytes accessed | tf_op | source)
XLA Modules:
  0.0 213.1 jit_solution(5326938152976221455)
XLA Ops:
  0.0 1.9 dynamic-slice_bitcast_fusion.1
  1.9 1.9 constant_dynamic-update-slice_fusion.4
  3.8 2.8 %collective-permute-start = (bf16[2,512,256]{2,1,0:T(8,128)(2,1)}, bf16[2,512,256]{2,1,0:T(8,128)(2,1)S(1)}, u32[]{:S(2)}, u32[]{:S(2)}) collective-permute-start(bf16[2,512,256]{2,1,0:T(8,128)(2,1)} %get-tuple-element.14), channel_id=1, source_target_pairs={{0,3},{1,0},{2,1},{3,2},{4,7},{5,4},{6,5},{7,6},{8,11},{9,8},{10,9... | collective-permute-start | bytes 1572872 | tf_op jit(solution)/shard_map/ppermute | solution.py:113
  6.5 4.5 %collective-permute-start.4 = (bf16[2,512,256]{2,1,0:T(8,128)(2,1)}, bf16[2,512,256]{2,1,0:T(8,128)(2,1)}, u32[]{:S(2)}, u32[]{:S(2)}) collective-permute-start(bf16[2,512,256]{2,1,0:T(8,128)(2,1)} %dynamic-slice_bitcast_fusion.1), channel_id=1, source_target_pairs={{0,128},{128,0},{1,129},{129,1},{2,130},{130,2},{3,131},{131,3},{4... | collective-permute-start | bytes 1572872 | tf_op jit(solution)/shard_map/ppermute | solution.py:143
  11.0 3.0 %collective-permute-start.9 = (bf16[2,512,256]{2,1,0:T(8,128)(2,1)}, bf16[2,512,256]{2,1,0:T(8,128)(2,1)}, u32[]{:S(2)}, u32[]{:S(2)}) collective-permute-start(bf16[2,512,256]{2,1,0:T(8,128)(2,1)} %get-tuple-element.14), channel_id=1, source_target_pairs={{0,96},{32,0},{64,32},{96,64},{1,97},{33,1},{65,33},{97,65},{2,98}... | collective-permute-start | bytes 1572872 | tf_op jit(solution)/shard_map/ppermute | solution.py:145
  25.3 1.5 fusion.97
  34.4 3.3 %collective-permute-start.2 = (bf16[2,256,256]{2,1,0:T(8,128)(2,1)S(1)}, bf16[2,256,256]{2,1,0:T(8,128)(2,1)S(1)}, u32[]{:S(2)}, u32[]{:S(2)}) collective-permute-start(bf16[2,256,256]{2,1,0:T(8,128)(2,1)S(1)} %slice.328), channel_id=1, source_target_pairs={{0,3},{1,0},{2,1},{3,2},{4,7},{5,4},{6,5},{7,6},{8,11},{9,8},{10,9... | collective-permute-start | bytes 786440 | tf_op jit(solution)/shard_map/ppermute | solution.py:115
  40.2 1.7 collective-permute-done.2
  41.9 2.9 %collective-permute-start.12 = (bf16[2,512,256]{2,1,0:T(8,128)(2,1)}, bf16[2,512,256]{2,1,0:T(8,128)(2,1)S(1)}, u32[]{:S(2)}, u32[]{:S(2)}) collective-permute-start(bf16[2,512,256]{2,1,0:T(8,128)(2,1)} %collective-permute-done.4), channel_id=1, source_target_pairs={{0,64},{32,96},{64,0},{96,32},{1,65},{33,97},{65,1},{97,33},{2,66}... | collective-permute-start | bytes 1572872 | tf_op jit(solution)/shard_map/ppermute | solution.py:146
  45.4 3.2 %collective-permute-start.5 = (bf16[2,512,256]{2,1,0:T(8,128)(2,1)}, bf16[2,512,256]{2,1,0:T(8,128)(2,1)S(1)}, u32[]{:S(2)}, u32[]{:S(2)}) collective-permute-start(bf16[2,512,256]{2,1,0:T(8,128)(2,1)} %collective-permute-done.4), channel_id=1, source_target_pairs={{0,3},{1,0},{2,1},{3,2},{4,7},{5,4},{6,5},{7,6},{8,11},{9,8},{10,9... | collective-permute-start | bytes 1572872 | tf_op jit(solution)/shard_map/ppermute | solution.py:113
  49.2 3.8 %collective-permute-done.10 = bf16[2,512,256]{2,1,0:T(8,128)(2,1)S(1)} collective-permute-done((bf16[2,512,256]{2,1,0:T(8,128)(2,1)}, bf16[2,512,256]{2,1,0:T(8,128)(2,1)S(1)}, u32[]{:S(2)}, u32[]{:S(2)}) %collective-permute-start.10) | collective-permute-done | bytes 524320 | tf_op jit(solution)/shard_map/ppermute | solution.py:145
  56.0 4.0 %collective-permute-start.13 = (bf16[2,2,512,128]{3,2,1,0:T(8,128)(2,1)S(1)}, bf16[2,2,512,128]{3,2,1,0:T(8,128)(2,1)S(1)}, u32[]{:S(2)}, u32[]{:S(2)}) collective-permute-start(bf16[2,2,512,128]{3,2,1,0:T(8,128)(2,1)S(1)} %pad_maximum_fusion.5), channel_id=1, source_target_pairs={{0,3},{1,0},{2,1},{3,2},{4,7},{5,4},{6,5},{7,6},{8,11},{9,8},{10,9... | collective-permute-start | bytes 1572872 | tf_op jit(solution)/shard_map/ppermute | solution.py:160
  60.4 1.5 collective-permute-start.15
  61.9 2.0 collective-permute-start.7
  65.1 20.3 %collective-permute-done.7 = bf16[2,256,256]{2,1,0:T(8,128)(2,1)S(1)} collective-permute-done((bf16[2,256,256]{2,1,0:T(8,128)(2,1)S(1)}, bf16[2,256,256]{2,1,0:T(8,128)(2,1)S(1)}, u32[]{:S(2)}, u32[]{:S(2)}) %collective-permute-start.7) | collective-permute-done | bytes 262176 | tf_op jit(solution)/shard_map/ppermute | solution.py:115
  85.5 4.0 %collective-permute-done.8 = bf16[2,256,256]{2,1,0:T(8,128)(2,1)S(1)} collective-permute-done((bf16[2,256,256]{2,1,0:T(8,128)(2,1)S(1)}, bf16[2,256,256]{2,1,0:T(8,128)(2,1)S(1)}, u32[]{:S(2)}, u32[]{:S(2)}) %collective-permute-start.8) | collective-permute-done | bytes 262176 | tf_op jit(solution)/shard_map/ppermute | solution.py:116
  90.2 1.3 fusion.36
  95.9 2.1 %collective-permute-done.16 = bf16[2,2,2048,128]{3,2,1,0:T(8,128)(2,1)S(1)} collective-permute-done((bf16[2,2,2048,128]{3,2,1,0:T(8,128)(2,1)S(1)}, bf16[2,2,2048,128]{3,2,1,0:T(8,128)(2,1)S(1)}, u32[]{:S(2)}, u32[]{:S(2)}) %collective-permute-start.16) | collective-permute-done | bytes 2097184 | tf_op jit(solution)/shard_map/ppermute | solution.py:163
  99.7 1.3 fusion.39
  106.3 1.9 collective-permute-start.18
  111.6 3.6 %collective-permute-done.18 = f32[2,256,128]{1,2,0:T(8,128)S(1)} collective-permute-done((f32[2,256,128]{1,2,0:T(8,128)}, f32[2,256,128]{1,2,0:T(8,128)S(1)}, u32[]{:S(2)}, u32[]{:S(2)}) %collective-permute-start.18) | collective-permute-done | bytes 262176 | tf_op jit(solution)/shard_map/ppermute | solution.py:195
  115.2 17.2 %collective-permute-done.19 = f32[2,256,128]{1,2,0:T(8,128)} collective-permute-done((f32[2,256,128]{1,2,0:T(8,128)}, f32[2,256,128]{1,2,0:T(8,128)}, u32[]{:S(2)}, u32[]{:S(2)}) %collective-permute-start.19) | collective-permute-done | bytes 262176 | tf_op jit(solution)/shard_map/ppermute | solution.py:195
  133.5 2.6 %collective-permute-start.22 = (f32[2,256,128]{1,2,0:T(8,128)S(1)}, f32[2,256,128]{1,2,0:T(8,128)S(1)}, u32[]{:S(2)}, u32[]{:S(2)}) collective-permute-start(f32[2,256,128]{1,2,0:T(8,128)S(1)} %copy.38), channel_id=1, source_target_pairs={{0,8},{4,12},{8,0},{12,4},{1,9},{5,13},{9,1},{13,5},{2,10},{6,14},... | collective-permute-start | bytes 786440 | tf_op jit(solution)/shard_map/ppermute | solution.py:195
  136.3 2.1 collective-permute-start.23
  139.7 1.9 collective-permute-start.27
  141.6 23.6 %collective-permute-done.22 = f32[2,256,128]{1,2,0:T(8,128)S(1)} collective-permute-done((f32[2,256,128]{1,2,0:T(8,128)S(1)}, f32[2,256,128]{1,2,0:T(8,128)S(1)}, u32[]{:S(2)}, u32[]{:S(2)}) %collective-permute-start.22) | collective-permute-done | bytes 262176 | tf_op jit(solution)/shard_map/ppermute | solution.py:195
  165.3 1.9 collective-permute-start.26
  167.3 1.3 dynamic_slice.71
  170.3 1.9 collective-permute-start.25
  172.2 7.8 %collective-permute-start.24 = (f32[2,256,128]{1,2,0:T(8,128)S(1)}, f32[2,256,128]{1,2,0:T(8,128)S(1)}, u32[]{:S(2)}, u32[]{:S(2)}) collective-permute-start(f32[2,256,128]{1,2,0:T(8,128)S(1)} %add_multiply_fusion.1), channel_id=1, source_target_pairs={{0,11},{4,139},{8,13},{12,137},{1,2},{5,130},{9,128},{13,4},{2,1},... | collective-permute-start | bytes 786440 | tf_op jit(solution)/shard_map/ppermute | solution.py:197
  180.0 24.0 %collective-permute-done.26 = f32[2,256,128]{1,2,0:T(8,128)S(1)} collective-permute-done((f32[2,256,128]{1,2,0:T(8,128)S(1)}, f32[2,256,128]{1,2,0:T(8,128)S(1)}, u32[]{:S(2)}, u32[]{:S(2)}) %collective-permute-start.26) | collective-permute-done | bytes 262176 | tf_op jit(solution)/shard_map/ppermute | solution.py:197
  208.3 1.3 maximum_select_fusion
  (144 shorter events, 35.1 us)
Async XLA Ops:
  0.0 14.7 %copy-start.4 = (s32[2,4,4]{2,1,0:T(4,128)S(1)}, s32[2,4,4]{2,1,0:T(4,128)}, u32[]{:S(2)}) copy-start(s32[2,4,4]{2,1,0:T(4,128)} %constant.358.clone) | copy-start | bytes 388
  3.8 30.6 %collective-permute-start = (bf16[2,512,256]{2,1,0:T(8,128)(2,1)}, bf16[2,512,256]{2,1,0:T(8,128)(2,1)S(1)}, u32[]{:S(2)}, u32[]{:S(2)}) collective-permute-start(bf16[2,512,256]{2,1,0:T(8,128)(2,1)} %get-tuple-element.14), channel_id=1, source_target_pairs={{0,3},{1,0},{2,1},{3,2},{4,7},{5,4},{6,5},{7,6},{8,11},{9,8},{10,9... | collective-permute-start | bytes 1572872 | tf_op jit(solution)/shard_map/ppermute | solution.py:113
  6.5 31.2 %collective-permute-start.1 = (bf16[2,512,256]{2,1,0:T(8,128)(2,1)}, bf16[2,512,256]{2,1,0:T(8,128)(2,1)S(1)}, u32[]{:S(2)}, u32[]{:S(2)}) collective-permute-start(bf16[2,512,256]{2,1,0:T(8,128)(2,1)} %get-tuple-element.14), channel_id=1, source_target_pairs={{0,1},{1,2},{2,3},{3,0},{4,5},{5,6},{6,7},{7,4},{8,9},{9,10},{10,1... | collective-permute-start | bytes 1572872 | tf_op jit(solution)/shard_map/ppermute | solution.py:114
  6.5 31.3 %collective-permute-start.4 = (bf16[2,512,256]{2,1,0:T(8,128)(2,1)}, bf16[2,512,256]{2,1,0:T(8,128)(2,1)}, u32[]{:S(2)}, u32[]{:S(2)}) collective-permute-start(bf16[2,512,256]{2,1,0:T(8,128)(2,1)} %dynamic-slice_bitcast_fusion.1), channel_id=1, source_target_pairs={{0,128},{128,0},{1,129},{129,1},{2,130},{130,2},{3,131},{131,3},{4... | collective-permute-start | bytes 1572872 | tf_op jit(solution)/shard_map/ppermute | solution.py:143
  11.0 38.0 %collective-permute-start.9 = (bf16[2,512,256]{2,1,0:T(8,128)(2,1)}, bf16[2,512,256]{2,1,0:T(8,128)(2,1)}, u32[]{:S(2)}, u32[]{:S(2)}) collective-permute-start(bf16[2,512,256]{2,1,0:T(8,128)(2,1)} %get-tuple-element.14), channel_id=1, source_target_pairs={{0,96},{32,0},{64,32},{96,64},{1,97},{33,1},{65,33},{97,65},{2,98}... | collective-permute-start | bytes 1572872 | tf_op jit(solution)/shard_map/ppermute | solution.py:145
  14.1 40.1 %collective-permute-start.11 = (bf16[2,512,256]{2,1,0:T(8,128)(2,1)}, bf16[2,512,256]{2,1,0:T(8,128)(2,1)}, u32[]{:S(2)}, u32[]{:S(2)}) collective-permute-start(bf16[2,512,256]{2,1,0:T(8,128)(2,1)} %get-tuple-element.14), channel_id=1, source_target_pairs={{0,64},{32,96},{64,0},{96,32},{1,65},{33,97},{65,1},{97,33},{2,66}... | collective-permute-start | bytes 1572872 | tf_op jit(solution)/shard_map/ppermute | solution.py:146
  34.4 7.5 %collective-permute-start.2 = (bf16[2,256,256]{2,1,0:T(8,128)(2,1)S(1)}, bf16[2,256,256]{2,1,0:T(8,128)(2,1)S(1)}, u32[]{:S(2)}, u32[]{:S(2)}) collective-permute-start(bf16[2,256,256]{2,1,0:T(8,128)(2,1)S(1)} %slice.328), channel_id=1, source_target_pairs={{0,3},{1,0},{2,1},{3,2},{4,7},{5,4},{6,5},{7,6},{8,11},{9,8},{10,9... | collective-permute-start | bytes 786440 | tf_op jit(solution)/shard_map/ppermute | solution.py:115
  37.7 7.7 %collective-permute-start.3 = (bf16[2,256,256]{2,1,0:T(8,128)(2,1)S(1)}, bf16[2,256,256]{2,1,0:T(8,128)(2,1)S(1)}, u32[]{:S(2)}, u32[]{:S(2)}) collective-permute-start(bf16[2,256,256]{2,1,0:T(8,128)(2,1)S(1)} %slice.329), channel_id=1, source_target_pairs={{0,1},{1,2},{2,3},{3,0},{4,5},{5,6},{6,7},{7,4},{8,9},{9,10},{10,1... | collective-permute-start | bytes 786440 | tf_op jit(solution)/shard_map/ppermute | solution.py:116
  37.8 15.2 %collective-permute-start.10 = (bf16[2,512,256]{2,1,0:T(8,128)(2,1)}, bf16[2,512,256]{2,1,0:T(8,128)(2,1)S(1)}, u32[]{:S(2)}, u32[]{:S(2)}) collective-permute-start(bf16[2,512,256]{2,1,0:T(8,128)(2,1)} %collective-permute-done.4), channel_id=1, source_target_pairs={{0,96},{32,0},{64,32},{96,64},{1,97},{33,1},{65,33},{97,65},{2,98}... | collective-permute-start | bytes 1572872 | tf_op jit(solution)/shard_map/ppermute | solution.py:145
  41.9 12.9 %collective-permute-start.12 = (bf16[2,512,256]{2,1,0:T(8,128)(2,1)}, bf16[2,512,256]{2,1,0:T(8,128)(2,1)S(1)}, u32[]{:S(2)}, u32[]{:S(2)}) collective-permute-start(bf16[2,512,256]{2,1,0:T(8,128)(2,1)} %collective-permute-done.4), channel_id=1, source_target_pairs={{0,64},{32,96},{64,0},{96,32},{1,65},{33,97},{65,1},{97,33},{2,66}... | collective-permute-start | bytes 1572872 | tf_op jit(solution)/shard_map/ppermute | solution.py:146
  45.4 16.5 %collective-permute-start.5 = (bf16[2,512,256]{2,1,0:T(8,128)(2,1)}, bf16[2,512,256]{2,1,0:T(8,128)(2,1)S(1)}, u32[]{:S(2)}, u32[]{:S(2)}) collective-permute-start(bf16[2,512,256]{2,1,0:T(8,128)(2,1)} %collective-permute-done.4), channel_id=1, source_target_pairs={{0,3},{1,0},{2,1},{3,2},{4,7},{5,4},{6,5},{7,6},{8,11},{9,8},{10,9... | collective-permute-start | bytes 1572872 | tf_op jit(solution)/shard_map/ppermute | solution.py:113
  49.1 14.9 %collective-permute-start.6 = (bf16[2,512,256]{2,1,0:T(8,128)(2,1)}, bf16[2,512,256]{2,1,0:T(8,128)(2,1)S(1)}, u32[]{:S(2)}, u32[]{:S(2)}) collective-permute-start(bf16[2,512,256]{2,1,0:T(8,128)(2,1)} %collective-permute-done.4), channel_id=1, source_target_pairs={{0,1},{1,2},{2,3},{3,0},{4,5},{5,6},{6,7},{7,4},{8,9},{9,10},{10,1... | collective-permute-start | bytes 1572872 | tf_op jit(solution)/shard_map/ppermute | solution.py:114
  56.0 37.2 %collective-permute-start.13 = (bf16[2,2,512,128]{3,2,1,0:T(8,128)(2,1)S(1)}, bf16[2,2,512,128]{3,2,1,0:T(8,128)(2,1)S(1)}, u32[]{:S(2)}, u32[]{:S(2)}) collective-permute-start(bf16[2,2,512,128]{3,2,1,0:T(8,128)(2,1)S(1)} %pad_maximum_fusion.5), channel_id=1, source_target_pairs={{0,3},{1,0},{2,1},{3,2},{4,7},{5,4},{6,5},{7,6},{8,11},{9,8},{10,9... | collective-permute-start | bytes 1572872 | tf_op jit(solution)/shard_map/ppermute | solution.py:160
  60.1 33.1 %collective-permute-start.14 = (bf16[2,2,512,128]{3,2,1,0:T(8,128)(2,1)S(1)}, bf16[2,2,512,128]{3,2,1,0:T(8,128)(2,1)S(1)}, u32[]{:S(2)}, u32[]{:S(2)}) collective-permute-start(bf16[2,2,512,128]{3,2,1,0:T(8,128)(2,1)S(1)} %pad_maximum_fusion.6), channel_id=1, source_target_pairs={{0,1},{1,2},{2,3},{3,0},{4,5},{5,6},{6,7},{7,4},{8,9},{9,10},{10,1... | collective-permute-start | bytes 1572872 | tf_op jit(solution)/shard_map/ppermute | solution.py:160
  60.4 32.9 %collective-permute-start.15 = (bf16[2,2,512,128]{3,2,1,0:T(8,128)(2,1)S(1)}, bf16[2,2,512,128]{3,2,1,0:T(8,128)(2,1)S(1)}, u32[]{:S(2)}, u32[]{:S(2)}) collective-permute-start(bf16[2,2,512,128]{3,2,1,0:T(8,128)(2,1)S(1)} %pad_maximum_fusion.7), channel_id=1, source_target_pairs={{0,2},{1,3},{2,0},{3,1},{4,6},{5,7},{6,4},{7,5},{8,10},{9,11},{10,... | collective-permute-start | bytes 1572872 | tf_op jit(solution)/shard_map/ppermute | solution.py:160
  61.9 23.5 %collective-permute-start.7 = (bf16[2,256,256]{2,1,0:T(8,128)(2,1)S(1)}, bf16[2,256,256]{2,1,0:T(8,128)(2,1)S(1)}, u32[]{:S(2)}, u32[]{:S(2)}) collective-permute-start(bf16[2,256,256]{2,1,0:T(8,128)(2,1)S(1)} %slice.330), channel_id=1, source_target_pairs={{0,3},{1,0},{2,1},{3,2},{4,7},{5,4},{6,5},{7,6},{8,11},{9,8},{10,9... | collective-permute-start | bytes 786440 | tf_op jit(solution)/shard_map/ppermute | solution.py:115
  64.0 25.4 %collective-permute-start.8 = (bf16[2,256,256]{2,1,0:T(8,128)(2,1)S(1)}, bf16[2,256,256]{2,1,0:T(8,128)(2,1)S(1)}, u32[]{:S(2)}, u32[]{:S(2)}) collective-permute-start(bf16[2,256,256]{2,1,0:T(8,128)(2,1)S(1)} %slice.331), channel_id=1, source_target_pairs={{0,1},{1,2},{2,3},{3,0},{4,5},{5,6},{6,7},{7,4},{8,9},{9,10},{10,1... | collective-permute-start | bytes 786440 | tf_op jit(solution)/shard_map/ppermute | solution.py:116
  90.1 4.1 %collective-permute-start.17 = (bf16[2,2048,128]{2,1,0:T(8,128)(2,1)S(1)}, bf16[2,2048,128]{2,1,0:T(8,128)(2,1)S(1)}, u32[]{:S(2)}, u32[]{:S(2)}) collective-permute-start(bf16[2,2048,128]{2,1,0:T(8,128)(2,1)S(1)} %slice_select_fusion), channel_id=1, source_target_pairs={{0,16},{16,0},{1,17},{17,1},{2,18},{18,2},{3,19},{19,3},{4,20},{20... | collective-permute-start | bytes 3145736 | tf_op jit(solution)/shard_map/ppermute | solution.py:165
  93.5 4.6 %collective-permute-start.16 = (bf16[2,2,2048,128]{3,2,1,0:T(8,128)(2,1)S(1)}, bf16[2,2,2048,128]{3,2,1,0:T(8,128)(2,1)S(1)}, u32[]{:S(2)}, u32[]{:S(2)}) collective-permute-start(bf16[2,2,2048,128]{3,2,1,0:T(8,128)(2,1)S(1)} %pad_maximum_fusion.1), channel_id=1, source_target_pairs={{0,16},{16,0},{1,17},{17,1},{2,18},{18,2},{3,19},{19,3},{4,20},{20... | collective-permute-start | bytes 6291464 | tf_op jit(solution)/shard_map/ppermute | solution.py:163
  106.3 9.0 %collective-permute-start.18 = (f32[2,256,128]{1,2,0:T(8,128)}, f32[2,256,128]{1,2,0:T(8,128)S(1)}, u32[]{:S(2)}, u32[]{:S(2)}) collective-permute-start(f32[2,256,128]{1,2,0:T(8,128)} %copy.33), channel_id=1, source_target_pairs={{0,4},{4,8},{8,12},{12,0},{1,5},{5,9},{9,13},{13,1},{2,6},{6,10},{... | collective-permute-start | bytes 786440 | tf_op jit(solution)/shard_map/ppermute | solution.py:195
  109.0 23.4 %collective-permute-start.19 = (f32[2,256,128]{1,2,0:T(8,128)}, f32[2,256,128]{1,2,0:T(8,128)}, u32[]{:S(2)}, u32[]{:S(2)}) collective-permute-start(f32[2,256,128]{1,2,0:T(8,128)} %copy.34), channel_id=1, source_target_pairs={{0,8},{4,12},{8,0},{12,4},{1,9},{5,13},{9,1},{13,5},{2,10},{6,14},... | collective-permute-start | bytes 786440 | tf_op jit(solution)/shard_map/ppermute | solution.py:195
  110.4 22.0 %collective-permute-start.20 = (f32[2,256,128]{1,2,0:T(8,128)}, f32[2,256,128]{1,2,0:T(8,128)S(1)}, u32[]{:S(2)}, u32[]{:S(2)}) collective-permute-start(f32[2,256,128]{1,2,0:T(8,128)} %copy.35), channel_id=1, source_target_pairs={{0,12},{4,0},{8,4},{12,8},{1,13},{5,1},{9,5},{13,9},{2,14},{6,2},{... | collective-permute-start | bytes 786440 | tf_op jit(solution)/shard_map/ppermute | solution.py:195
  133.2 5.5 %copy-start.3 = (f32[2,256,128]{1,2,0:T(8,128)S(1)}, f32[2,256,128]{1,2,0:T(8,128)}, u32[]{:S(2)}) copy-start(f32[2,256,128]{1,2,0:T(8,128)} %copy-done.2) | copy-start | bytes 786436
  133.3 8.3 %collective-permute-start.21 = (f32[2,256,128]{1,2,0:T(8,128)S(1)}, f32[2,256,128]{1,2,0:T(8,128)S(1)}, u32[]{:S(2)}, u32[]{:S(2)}) collective-permute-start(f32[2,256,128]{1,2,0:T(8,128)S(1)} %copy.36), channel_id=1, source_target_pairs={{0,4},{4,8},{8,12},{12,0},{1,5},{5,9},{9,13},{13,1},{2,6},{6,10},{... | collective-permute-start | bytes 786440 | tf_op jit(solution)/shard_map/ppermute | solution.py:195
  133.5 31.7 %collective-permute-start.22 = (f32[2,256,128]{1,2,0:T(8,128)S(1)}, f32[2,256,128]{1,2,0:T(8,128)S(1)}, u32[]{:S(2)}, u32[]{:S(2)}) collective-permute-start(f32[2,256,128]{1,2,0:T(8,128)S(1)} %copy.38), channel_id=1, source_target_pairs={{0,8},{4,12},{8,0},{12,4},{1,9},{5,13},{9,1},{13,5},{2,10},{6,14},... | collective-permute-start | bytes 786440 | tf_op jit(solution)/shard_map/ppermute | solution.py:195
  136.3 28.9 %collective-permute-start.23 = (f32[2,256,128]{1,2,0:T(8,128)S(1)}, f32[2,256,128]{1,2,0:T(8,128)S(1)}, u32[]{:S(2)}, u32[]{:S(2)}) collective-permute-start(f32[2,256,128]{1,2,0:T(8,128)S(1)} %copy.39), channel_id=1, source_target_pairs={{0,12},{4,0},{8,4},{12,8},{1,13},{5,1},{9,5},{13,9},{2,14},{6,2},{... | collective-permute-start | bytes 786440 | tf_op jit(solution)/shard_map/ppermute | solution.py:195
  139.7 40.3 %collective-permute-start.27 = (f32[2,256,128]{1,2,0:T(8,128)S(1)}, f32[2,256,128]{1,2,0:T(8,128)S(1)}, u32[]{:S(2)}, u32[]{:S(2)}) collective-permute-start(f32[2,256,128]{1,2,0:T(8,128)S(1)} %add_multiply_fusion), channel_id=1, source_target_pairs={{0,32},{4,40},{8,64},{12,8},{1,176},{5,184},{9,152},{13,208},{2,13... | collective-permute-start | bytes 786440 | tf_op jit(solution)/shard_map/ppermute | solution.py:197
  165.3 38.7 %collective-permute-start.26 = (f32[2,256,128]{1,2,0:T(8,128)S(1)}, f32[2,256,128]{1,2,0:T(8,128)S(1)}, u32[]{:S(2)}, u32[]{:S(2)}) collective-permute-start(f32[2,256,128]{1,2,0:T(8,128)S(1)} %add_multiply_fusion.1), channel_id=1, source_target_pairs={{0,176},{4,184},{8,208},{12,152},{1,32},{5,40},{9,8},{13,64},{2,16... | collective-permute-start | bytes 786440 | tf_op jit(solution)/shard_map/ppermute | solution.py:197
  170.3 35.0 %collective-permute-start.25 = (f32[2,256,128]{1,2,0:T(8,128)S(1)}, f32[2,256,128]{1,2,0:T(8,128)S(1)}, u32[]{:S(2)}, u32[]{:S(2)}) collective-permute-start(f32[2,256,128]{1,2,0:T(8,128)S(1)} %add_multiply_fusion), channel_id=1, source_target_pairs={{0,2},{4,130},{8,4},{12,128},{1,11},{5,139},{9,137},{13,13},{2,0},... | collective-permute-start | bytes 786440 | tf_op jit(solution)/shard_map/ppermute | solution.py:197
  172.2 33.1 %collective-permute-start.24 = (f32[2,256,128]{1,2,0:T(8,128)S(1)}, f32[2,256,128]{1,2,0:T(8,128)S(1)}, u32[]{:S(2)}, u32[]{:S(2)}) collective-permute-start(f32[2,256,128]{1,2,0:T(8,128)S(1)} %add_multiply_fusion.1), channel_id=1, source_target_pairs={{0,11},{4,139},{8,13},{12,137},{1,2},{5,130},{9,128},{13,4},{2,1},... | collective-permute-start | bytes 786440 | tf_op jit(solution)/shard_map/ppermute | solution.py:197
  205.3 0.9 copy-start
  205.3 0.7 copy-start.1
  (1 other events, 0.7 us)
